TPU v7x, 32 devices: a whole 2x2x4 slice. The times are simulated.
32 devices in a mesh: groups: 2 (over x), depth: 16 (over z, y, core).
Axes of the slice: x: 2, y: 2, z: 4, core: 2. Of those that a mesh axis runs over, the one named last changes fastest.
Arguments:
- fronts: bfloat16 [4, 64, 8, 2048], P(None, ('groups', 'depth')), parts along dimension 1, may hold values from -6 to 6
- extrap: bfloat16 [32, 16, 5, 2, 128, 128], P('depth'), may hold values from -0.15625 to 0.15625
- offsets: int32 [2, 5], replicated, may hold values from -2 to 2
- assign: int32 [2, 8], replicated, may hold values from 0 to 7, each once within a row
Outputs:
- images: float32 [8, 32, 2048], P(None, ('groups', 'depth')), parts along dimension 1
- last_fronts: bfloat16 [4, 64, 8, 2048], P(None, ('groups', 'depth')), parts along dimension 1
There are 2 independent parts, one for each index of `groups`. A program takes and returns all parts, laid end to end along the dimension named above; an argument that names none is the same for every part. Nothing has to cross between parts.
Inputs may be any that keep to these rules, and one draw needn't show every extreme that they name: `assign`: each row names every shot number once.
All inputs are finite; a program needn't handle non-finite values.
Results may differ from a plain program's by a relative error of at most 0.015.
Values may be sent and summed in bfloat16 or wider, within the bound.
No kernel may reach another device: no remote copies, remote signals or barrier semaphores. Data moves between devices by JAX's collectives and lax.ppermute only.
A program may use at most 64 MiB of HBM per device.

v0:
```python
import math

import jax
import jax.numpy as jnp
from jax import lax
from jax.sharding import PartitionSpec as P

BLOCK = 128
NBLK = 16
BAND = 5
FOWNERS = 8
HANDOVERS = 8
NFREQ = 16


def from_partner(value, axis, stride):
    mask = 2**stride
    pairs = [(source, source ^ mask) for source in range(lax.axis_size(axis))]
    return lax.ppermute(value, axis, pairs)


def passed_along(shard, axis, by):
    size = lax.axis_size(axis)
    return lax.ppermute(shard, axis, [(i, (i + by) % size) for i in range(size)])


def advance(wave_state, band_offsets, operator):
    reach = BAND // 2
    nfield, freqs, slots, points = wave_state.shape
    blocks = wave_state.reshape(nfield, freqs, slots, NBLK, BLOCK)
    padded = jnp.pad(blocks, ((0, 0), (0, 0), (0, 0), (reach, reach), (0, 0)))
    shifted = jnp.stack(
        [
            lax.dynamic_slice_in_dim(padded, band_offsets[band_pos] + reach, NBLK, 3)
            for band_pos in range(BAND)
        ],
        axis=3,
    )
    products = jnp.einsum(
        "cfskbj,fbkpjl->pcfsbl", shifted, operator, preferred_element_type=jnp.float32
    )
    real_prod = products[0]
    imag_prod = products[1]
    src_real = real_prod[0] - imag_prod[1]
    src_imag = imag_prod[0] + real_prod[1]
    rec_real = real_prod[2] + imag_prod[3]
    rec_imag = real_prod[3] - imag_prod[2]
    joined = jnp.stack([src_real, src_imag, rec_real, rec_imag])
    return joined.reshape(nfield, freqs, slots, points).astype(jnp.bfloat16)


def fold_owners(partial_value, my_owner):
    for bit_pos in range(FOWNERS.bit_length() - 2, -1, -1):
        half_rows = partial_value.shape[-2] // 2
        lower_half = partial_value[..., :half_rows, :]
        upper_half = partial_value[..., half_rows:, :]
        upper_mine = my_owner // 2**bit_pos % 2 == 1
        outgoing = jnp.where(upper_mine, lower_half, upper_half)
        kept_half = jnp.where(upper_mine, upper_half, lower_half)
        partial_value = kept_half + from_partner(outgoing, "depth", bit_pos)
    return partial_value


def on_device(fronts, extrap, offsets, assign):
    dev_index = lax.axis_index("depth")
    my_section = dev_index // FOWNERS
    my_owner = dev_index % FOWNERS
    band_offsets = lax.dynamic_index_in_dim(offsets, my_section, 0, keepdims=False)
    my_assign = lax.dynamic_index_in_dim(assign, my_section, 0, keepdims=False)
    slot_count = fronts.shape[2]
    placing = (my_assign[:, None] == jnp.arange(slot_count, dtype=jnp.int32)[None, :]).astype(
        jnp.float32
    )
    image_scale = 1.0 / math.sqrt(2.0 * NFREQ)
    wave_state = fronts
    partials = []
    advanced = fronts
    for handover in range(HANDOVERS):
        more_rounds = handover + 1 < HANDOVERS
        advanced = advance(wave_state, band_offsets, extrap)
        if more_rounds:
            wave_state = passed_along(advanced, "depth", FOWNERS)
        fields = advanced.astype(jnp.float32)
        partial_value = image_scale * jnp.sum(fields[0] * fields[2] + fields[1] * fields[3], axis=0)
        placed = jnp.einsum("ji,jx->ix", placing, partial_value, precision=lax.Precision.HIGHEST)
        partials.append(fold_owners(placed, my_owner))
    images = jnp.stack(partials)
    return (images, advanced)


def solution(mesh):
    placed = (
        P(None, ("groups", "depth"), None, None),
        P("depth", None, None, None, None, None),
        P(),
        P(),
    )
    return jax.shard_map(
        on_device,
        mesh=mesh,
        in_specs=placed,
        out_specs=(P(None, ("groups", "depth"), None), P(None, ("groups", "depth"), None, None)),
        check_vma=False,
    )
```

profile of v0, /device:TPU:0, one launch (start us, length us, event | category | flops | bytes accessed | tf_op | source)
XLA Modules:
  0.0 180.5 jit_solution(8746024615223880882)
XLA Ops:
  9.6 5.0 %fusion.16 = f32[2,4,2,8,16,128]{5,3,0,1,4,2:T(8,128)S(1)} fusion(bf16[4,2,8,5,16,128]{5,2,3,0,4,1:T(8,128)(2,1)S(1)} %fusion.57, bf16[2,16,5,2,128,128]{5,4,3,2,1,0:T(8,128)(2,1)} %param.5), kind=kOutput, calls=%fused_computation.16 | convolution fusion | flops 335544320 | bytes 12845056 | tf_op jit(solution)/shard_map/cfskbj,fbkpjl->pcfsbl/dot_general | solution.py:39
  15.1 3.1 %collective-permute-start = (f32[4,2048]{1,0:T(4,128)S(1)}, f32[4,2048]{1,0:T(4,128)S(1)}, u32[]{:S(2)}, u32[]{:S(2)}) collective-permute-start(f32[4,2048]{1,0:T(4,128)S(1)} %slice_select_fusion.7), channel_id=1, source_target_pairs={{0,4},{1,5},{2,6},{3,7},{4,0},{5,1},{6,2},{7,3},{8,12},{9,13},{10,... | collective-permute-start | bytes 98312 | tf_op jit(solution)/shard_map/ppermute | solution.py:19
  18.2 1.9 %collective-permute-done = f32[4,2048]{1,0:T(4,128)S(1)} collective-permute-done((f32[4,2048]{1,0:T(4,128)S(1)}, f32[4,2048]{1,0:T(4,128)S(1)}, u32[]{:S(2)}, u32[]{:S(2)}) %collective-permute-start) | collective-permute-done | bytes 32800 | tf_op jit(solution)/shard_map/ppermute | solution.py:19
  20.1 2.0 %collective-permute-start.1 = (f32[2,2048]{1,0:T(2,128)S(1)}, f32[2,2048]{1,0:T(2,128)S(1)}, u32[]{:S(2)}, u32[]{:S(2)}) collective-permute-start(f32[2,2048]{1,0:T(2,128)S(1)} %broadcast_select_fusion.7), channel_id=1, source_target_pairs={{0,2},{1,3},{2,0},{3,1},{4,6},{5,7},{6,4},{7,5},{8,10},{9,11},{10,... | collective-permute-start | bytes 49160 | tf_op jit(solution)/shard_map/ppermute | solution.py:19
  22.1 2.6 %collective-permute-start.3 = (bf16[4,2,8,2048]{3,2,1,0:T(8,128)(2,1)S(1)}, bf16[4,2,8,2048]{3,2,1,0:T(8,128)(2,1)S(1)}, u32[]{:S(2)}, u32[]{:S(2)}) collective-permute-start(bf16[4,2,8,2048]{3,2,1,0:T(8,128)(2,1)S(1)} %get-tuple-element.83), channel_id=1, source_target_pairs={{0,8},{1,9},{2,10},{3,11},{4,12},{5,13},{6,14},{7,15},{8,0},{9,1},... | collective-permute-start | bytes 786440 | tf_op jit(solution)/shard_map/ppermute | solution.py:24
  24.8 10.5 %collective-permute-done.3 = bf16[4,2,8,2048]{3,2,1,0:T(8,128)(2,1)S(1)} collective-permute-done((bf16[4,2,8,2048]{3,2,1,0:T(8,128)(2,1)S(1)}, bf16[4,2,8,2048]{3,2,1,0:T(8,128)(2,1)S(1)}, u32[]{:S(2)}, u32[]{:S(2)}) %collective-permute-start.3) | collective-permute-done | bytes 262176 | tf_op jit(solution)/shard_map/ppermute | solution.py:24
  36.5 5.7 %fusion.19 = f32[2,4,2,8,16,128]{5,3,0,1,4,2:T(8,128)S(1)} fusion(bf16[4,2,8,5,16,128]{5,2,3,0,4,1:T(8,128)(2,1)S(1)} %bitcast_dynamic-update-slice_fusion.30, bf16[2,16,5,2,128,128]{5,4,3,2,1,0:T(8,128)(2,1)} %param.5), kind=kOutput, calls=%fused_computation.17 | convolution fusion | flops 335544320 | bytes 12845056 | tf_op jit(solution)/shard_map/cfskbj,fbkpjl->pcfsbl/dot_general | solution.py:39
  43.5 3.1 %collective-permute-done.4 = f32[4,2048]{1,0:T(4,128)S(1)} collective-permute-done((f32[4,2048]{1,0:T(4,128)S(1)}, f32[4,2048]{1,0:T(4,128)S(1)}, u32[]{:S(2)}, u32[]{:S(2)}) %collective-permute-start.4) | collective-permute-done | bytes 32800 | tf_op jit(solution)/shard_map/ppermute | solution.py:19
  47.3 2.2 %collective-permute-start.7 = (bf16[4,2,8,2048]{3,2,1,0:T(8,128)(2,1)S(1)}, bf16[4,2,8,2048]{3,2,1,0:T(8,128)(2,1)S(1)}, u32[]{:S(2)}, u32[]{:S(2)}) collective-permute-start(bf16[4,2,8,2048]{3,2,1,0:T(8,128)(2,1)S(1)} %get-tuple-element.76), channel_id=1, source_target_pairs={{0,8},{1,9},{2,10},{3,11},{4,12},{5,13},{6,14},{7,15},{8,0},{9,1},... | collective-permute-start | bytes 786440 | tf_op jit(solution)/shard_map/ppermute | solution.py:24
  50.5 9.9 %collective-permute-done.7 = bf16[4,2,8,2048]{3,2,1,0:T(8,128)(2,1)S(1)} collective-permute-done((bf16[4,2,8,2048]{3,2,1,0:T(8,128)(2,1)S(1)}, bf16[4,2,8,2048]{3,2,1,0:T(8,128)(2,1)S(1)}, u32[]{:S(2)}, u32[]{:S(2)}) %collective-permute-start.7) | collective-permute-done | bytes 262176 | tf_op jit(solution)/shard_map/ppermute | solution.py:24
  61.6 1.7 fusion.22
  64.7 3.1 %collective-permute-done.8 = f32[4,2048]{1,0:T(4,128)S(1)} collective-permute-done((f32[4,2048]{1,0:T(4,128)S(1)}, f32[4,2048]{1,0:T(4,128)S(1)}, u32[]{:S(2)}, u32[]{:S(2)}) %collective-permute-start.8) | collective-permute-done | bytes 32800 | tf_op jit(solution)/shard_map/ppermute | solution.py:19
  69.4 2.2 %collective-permute-start.11 = (bf16[4,2,8,2048]{3,2,1,0:T(8,128)(2,1)S(1)}, bf16[4,2,8,2048]{3,2,1,0:T(8,128)(2,1)S(1)}, u32[]{:S(2)}, u32[]{:S(2)}) collective-permute-start(bf16[4,2,8,2048]{3,2,1,0:T(8,128)(2,1)S(1)} %get-tuple-element.69), channel_id=1, source_target_pairs={{0,8},{1,9},{2,10},{3,11},{4,12},{5,13},{6,14},{7,15},{8,0},{9,1},... | collective-permute-start | bytes 786440 | tf_op jit(solution)/shard_map/ppermute | solution.py:24
  71.7 10.8 %collective-permute-done.11 = bf16[4,2,8,2048]{3,2,1,0:T(8,128)(2,1)S(1)} collective-permute-done((bf16[4,2,8,2048]{3,2,1,0:T(8,128)(2,1)S(1)}, bf16[4,2,8,2048]{3,2,1,0:T(8,128)(2,1)S(1)}, u32[]{:S(2)}, u32[]{:S(2)}) %collective-permute-start.11) | collective-permute-done | bytes 262176 | tf_op jit(solution)/shard_map/ppermute | solution.py:24
  83.7 1.7 fusion.25
  86.8 3.1 %collective-permute-done.12 = f32[4,2048]{1,0:T(4,128)S(1)} collective-permute-done((f32[4,2048]{1,0:T(4,128)S(1)}, f32[4,2048]{1,0:T(4,128)S(1)}, u32[]{:S(2)}, u32[]{:S(2)}) %collective-permute-start.12) | collective-permute-done | bytes 32800 | tf_op jit(solution)/shard_map/ppermute | solution.py:19
  90.6 2.2 %collective-permute-start.15 = (bf16[4,2,8,2048]{3,2,1,0:T(8,128)(2,1)S(1)}, bf16[4,2,8,2048]{3,2,1,0:T(8,128)(2,1)S(1)}, u32[]{:S(2)}, u32[]{:S(2)}) collective-permute-start(bf16[4,2,8,2048]{3,2,1,0:T(8,128)(2,1)S(1)} %get-tuple-element.62), channel_id=1, source_target_pairs={{0,8},{1,9},{2,10},{3,11},{4,12},{5,13},{6,14},{7,15},{8,0},{9,1},... | collective-permute-start | bytes 786440 | tf_op jit(solution)/shard_map/ppermute | solution.py:24
  93.8 9.9 %collective-permute-done.15 = bf16[4,2,8,2048]{3,2,1,0:T(8,128)(2,1)S(1)} collective-permute-done((bf16[4,2,8,2048]{3,2,1,0:T(8,128)(2,1)S(1)}, bf16[4,2,8,2048]{3,2,1,0:T(8,128)(2,1)S(1)}, u32[]{:S(2)}, u32[]{:S(2)}) %collective-permute-start.15) | collective-permute-done | bytes 262176 | tf_op jit(solution)/shard_map/ppermute | solution.py:24
  104.9 1.7 fusion.28
  108.0 3.1 %collective-permute-done.16 = f32[4,2048]{1,0:T(4,128)S(1)} collective-permute-done((f32[4,2048]{1,0:T(4,128)S(1)}, f32[4,2048]{1,0:T(4,128)S(1)}, u32[]{:S(2)}, u32[]{:S(2)}) %collective-permute-start.16) | collective-permute-done | bytes 32800 | tf_op jit(solution)/shard_map/ppermute | solution.py:19
  112.7 2.2 %collective-permute-start.19 = (bf16[4,2,8,2048]{3,2,1,0:T(8,128)(2,1)S(1)}, bf16[4,2,8,2048]{3,2,1,0:T(8,128)(2,1)S(1)}, u32[]{:S(2)}, u32[]{:S(2)}) collective-permute-start(bf16[4,2,8,2048]{3,2,1,0:T(8,128)(2,1)S(1)} %get-tuple-element.55), channel_id=1, source_target_pairs={{0,8},{1,9},{2,10},{3,11},{4,12},{5,13},{6,14},{7,15},{8,0},{9,1},... | collective-permute-start | bytes 786440 | tf_op jit(solution)/shard_map/ppermute | solution.py:24
  115.0 10.8 %collective-permute-done.19 = bf16[4,2,8,2048]{3,2,1,0:T(8,128)(2,1)S(1)} collective-permute-done((bf16[4,2,8,2048]{3,2,1,0:T(8,128)(2,1)S(1)}, bf16[4,2,8,2048]{3,2,1,0:T(8,128)(2,1)S(1)}, u32[]{:S(2)}, u32[]{:S(2)}) %collective-permute-start.19) | collective-permute-done | bytes 262176 | tf_op jit(solution)/shard_map/ppermute | solution.py:24
  127.0 1.9 %fusion.31 = f32[2,4,2,8,16,128]{5,3,0,1,4,2:T(8,128)S(1)} fusion(bf16[4,2,8,5,16,128]{5,2,3,0,4,1:T(8,128)(2,1)S(1)} %bitcast_dynamic-update-slice_fusion.10, bf16[2,16,5,2,128,128]{5,4,3,2,1,0:T(8,128)(2,1)S(1)} %bitcast.362), kind=kOutput, calls=%fused_computation.21 | convolution fusion | flops 335544320 | bytes 12845056 | tf_op jit(solution)/shard_map/cfskbj,fbkpjl->pcfsbl/dot_general | solution.py:39
  130.3 3.1 %collective-permute-done.20 = f32[4,2048]{1,0:T(4,128)S(1)} collective-permute-done((f32[4,2048]{1,0:T(4,128)S(1)}, f32[4,2048]{1,0:T(4,128)S(1)}, u32[]{:S(2)}, u32[]{:S(2)}) %collective-permute-start.20) | collective-permute-done | bytes 32800 | tf_op jit(solution)/shard_map/ppermute | solution.py:19
  134.1 2.2 %collective-permute-start.23 = (bf16[4,2,8,2048]{3,2,1,0:T(8,128)(2,1)S(1)}, bf16[4,2,8,2048]{3,2,1,0:T(8,128)(2,1)S(1)}, u32[]{:S(2)}, u32[]{:S(2)}) collective-permute-start(bf16[4,2,8,2048]{3,2,1,0:T(8,128)(2,1)S(1)} %get-tuple-element.48), channel_id=1, source_target_pairs={{0,8},{1,9},{2,10},{3,11},{4,12},{5,13},{6,14},{7,15},{8,0},{9,1},... | collective-permute-start | bytes 786440 | tf_op jit(solution)/shard_map/ppermute | solution.py:24
  137.4 9.8 %collective-permute-done.23 = bf16[4,2,8,2048]{3,2,1,0:T(8,128)(2,1)S(1)} collective-permute-done((bf16[4,2,8,2048]{3,2,1,0:T(8,128)(2,1)S(1)}, bf16[4,2,8,2048]{3,2,1,0:T(8,128)(2,1)S(1)}, u32[]{:S(2)}, u32[]{:S(2)}) %collective-permute-start.23) | collective-permute-done | bytes 262176 | tf_op jit(solution)/shard_map/ppermute | solution.py:24
  148.4 1.7 fusion.34
  151.4 3.5 %collective-permute-start.27 = (bf16[4,2,8,2048]{3,2,1,0:T(8,128)(2,1)S(1)}, bf16[4,2,8,2048]{3,2,1,0:T(8,128)(2,1)S(1)}, u32[]{:S(2)}, u32[]{:S(2)}) collective-permute-start(bf16[4,2,8,2048]{3,2,1,0:T(8,128)(2,1)S(1)} %get-tuple-element.41), channel_id=1, source_target_pairs={{0,8},{1,9},{2,10},{3,11},{4,12},{5,13},{6,14},{7,15},{8,0},{9,1},... | collective-permute-start | bytes 786440 | tf_op jit(solution)/shard_map/ppermute | solution.py:24
  156.5 10.2 %collective-permute-done.27 = bf16[4,2,8,2048]{3,2,1,0:T(8,128)(2,1)S(1)} collective-permute-done((bf16[4,2,8,2048]{3,2,1,0:T(8,128)(2,1)S(1)}, bf16[4,2,8,2048]{3,2,1,0:T(8,128)(2,1)S(1)}, u32[]{:S(2)}, u32[]{:S(2)}) %collective-permute-start.27) | collective-permute-done | bytes 262176 | tf_op jit(solution)/shard_map/ppermute | solution.py:24
  167.9 1.7 fusion.37
  170.9 3.9 %collective-permute-done.28 = f32[4,2048]{1,0:T(4,128)S(1)} collective-permute-done((f32[4,2048]{1,0:T(4,128)S(1)}, f32[4,2048]{1,0:T(4,128)S(1)}, u32[]{:S(2)}, u32[]{:S(2)}) %collective-permute-start.28) | collective-permute-done | bytes 32800 | tf_op jit(solution)/shard_map/ppermute | solution.py:19
  176.4 2.2 %collective-permute-done.29 = f32[2,2048]{1,0:T(2,128)S(1)} collective-permute-done((f32[2,2048]{1,0:T(2,128)S(1)}, f32[2,2048]{1,0:T(2,128)S(1)}, u32[]{:S(2)}, u32[]{:S(2)}) %collective-permute-start.29) | collective-permute-done | bytes 16416 | tf_op jit(solution)/shard_map/ppermute | solution.py:19
  (186 shorter events, 33.7 us)
Async XLA Ops:
  15.1 5.0 %collective-permute-start = (f32[4,2048]{1,0:T(4,128)S(1)}, f32[4,2048]{1,0:T(4,128)S(1)}, u32[]{:S(2)}, u32[]{:S(2)}) collective-permute-start(f32[4,2048]{1,0:T(4,128)S(1)} %slice_select_fusion.7), channel_id=1, source_target_pairs={{0,4},{1,5},{2,6},{3,7},{4,0},{5,1},{6,2},{7,3},{8,12},{9,13},{10,... | collective-permute-start | bytes 98312 | tf_op jit(solution)/shard_map/ppermute | solution.py:19
  20.1 4.6 %collective-permute-start.1 = (f32[2,2048]{1,0:T(2,128)S(1)}, f32[2,2048]{1,0:T(2,128)S(1)}, u32[]{:S(2)}, u32[]{:S(2)}) collective-permute-start(f32[2,2048]{1,0:T(2,128)S(1)} %broadcast_select_fusion.7), channel_id=1, source_target_pairs={{0,2},{1,3},{2,0},{3,1},{4,6},{5,7},{6,4},{7,5},{8,10},{9,11},{10,... | collective-permute-start | bytes 49160 | tf_op jit(solution)/shard_map/ppermute | solution.py:19
  22.1 13.1 %collective-permute-start.3 = (bf16[4,2,8,2048]{3,2,1,0:T(8,128)(2,1)S(1)}, bf16[4,2,8,2048]{3,2,1,0:T(8,128)(2,1)S(1)}, u32[]{:S(2)}, u32[]{:S(2)}) collective-permute-start(bf16[4,2,8,2048]{3,2,1,0:T(8,128)(2,1)S(1)} %get-tuple-element.83), channel_id=1, source_target_pairs={{0,8},{1,9},{2,10},{3,11},{4,12},{5,13},{6,14},{7,15},{8,0},{9,1},... | collective-permute-start | bytes 786440 | tf_op jit(solution)/shard_map/ppermute | solution.py:24
  36.5 25.1 %slice-start = ((s8[10485760]{0:T(1024)(128)(4,1)}), s8[4194304]{0:T(1024)(128)(4,1)S(1)}, s32[]{:S(2)}) async-start(s8[10485760]{0:T(1024)(128)(4,1)} %bitcast.361), calls=%async_computation | async-start | bytes 8388608
  42.7 4.0 %collective-permute-start.4 = (f32[4,2048]{1,0:T(4,128)S(1)}, f32[4,2048]{1,0:T(4,128)S(1)}, u32[]{:S(2)}, u32[]{:S(2)}) collective-permute-start(f32[4,2048]{1,0:T(4,128)S(1)} %slice_select_fusion.6), channel_id=1, source_target_pairs={{0,4},{1,5},{2,6},{3,7},{4,0},{5,1},{6,2},{7,3},{8,12},{9,13},{10,... | collective-permute-start | bytes 98312 | tf_op jit(solution)/shard_map/ppermute | solution.py:19
  43.5 3.8 %collective-permute-start.2 = (f32[1,2048]{1,0:T(1,128)S(1)}, f32[1,2048]{1,0:T(1,128)S(1)}, u32[]{:S(2)}, u32[]{:S(2)}) collective-permute-start(f32[1,2048]{1,0:T(1,128)S(1)} %broadcast_select_fusion.22), channel_id=1, source_target_pairs={{0,1},{1,0},{2,3},{3,2},{4,5},{5,4},{6,7},{7,6},{8,9},{9,8},{10,11... | collective-permute-start | bytes 24584 | tf_op jit(solution)/shard_map/ppermute | solution.py:19
  46.7 3.8 %collective-permute-start.5 = (f32[2,2048]{1,0:T(2,128)S(1)}, f32[2,2048]{1,0:T(2,128)S(1)}, u32[]{:S(2)}, u32[]{:S(2)}) collective-permute-start(f32[2,2048]{1,0:T(2,128)S(1)} %broadcast_select_fusion.6), channel_id=1, source_target_pairs={{0,2},{1,3},{2,0},{3,1},{4,6},{5,7},{6,4},{7,5},{8,10},{9,11},{10,... | collective-permute-start | bytes 49160 | tf_op jit(solution)/shard_map/ppermute | solution.py:19
  47.3 13.2 %collective-permute-start.7 = (bf16[4,2,8,2048]{3,2,1,0:T(8,128)(2,1)S(1)}, bf16[4,2,8,2048]{3,2,1,0:T(8,128)(2,1)S(1)}, u32[]{:S(2)}, u32[]{:S(2)}) collective-permute-start(bf16[4,2,8,2048]{3,2,1,0:T(8,128)(2,1)S(1)} %get-tuple-element.76), channel_id=1, source_target_pairs={{0,8},{1,9},{2,10},{3,11},{4,12},{5,13},{6,14},{7,15},{8,0},{9,1},... | collective-permute-start | bytes 786440 | tf_op jit(solution)/shard_map/ppermute | solution.py:24
  63.9 4.0 %collective-permute-start.8 = (f32[4,2048]{1,0:T(4,128)S(1)}, f32[4,2048]{1,0:T(4,128)S(1)}, u32[]{:S(2)}, u32[]{:S(2)}) collective-permute-start(f32[4,2048]{1,0:T(4,128)S(1)} %slice_select_fusion.5), channel_id=1, source_target_pairs={{0,4},{1,5},{2,6},{3,7},{4,0},{5,1},{6,2},{7,3},{8,12},{9,13},{10,... | collective-permute-start | bytes 98312 | tf_op jit(solution)/shard_map/ppermute | solution.py:19
  64.7 4.8 %collective-permute-start.6 = (f32[1,2048]{1,0:T(1,128)S(1)}, f32[1,2048]{1,0:T(1,128)S(1)}, u32[]{:S(2)}, u32[]{:S(2)}) collective-permute-start(f32[1,2048]{1,0:T(1,128)S(1)} %broadcast_select_fusion.20), channel_id=1, source_target_pairs={{0,1},{1,0},{2,3},{3,2},{4,5},{5,4},{6,7},{7,6},{8,9},{9,8},{10,11... | collective-permute-start | bytes 24584 | tf_op jit(solution)/shard_map/ppermute | solution.py:19
  67.9 3.8 %collective-permute-start.9 = (f32[2,2048]{1,0:T(2,128)S(1)}, f32[2,2048]{1,0:T(2,128)S(1)}, u32[]{:S(2)}, u32[]{:S(2)}) collective-permute-start(f32[2,2048]{1,0:T(2,128)S(1)} %broadcast_select_fusion.5), channel_id=1, source_target_pairs={{0,2},{1,3},{2,0},{3,1},{4,6},{5,7},{6,4},{7,5},{8,10},{9,11},{10,... | collective-permute-start | bytes 49160 | tf_op jit(solution)/shard_map/ppermute | solution.py:19
  69.4 13.1 %collective-permute-start.11 = (bf16[4,2,8,2048]{3,2,1,0:T(8,128)(2,1)S(1)}, bf16[4,2,8,2048]{3,2,1,0:T(8,128)(2,1)S(1)}, u32[]{:S(2)}, u32[]{:S(2)}) collective-permute-start(bf16[4,2,8,2048]{3,2,1,0:T(8,128)(2,1)S(1)} %get-tuple-element.69), channel_id=1, source_target_pairs={{0,8},{1,9},{2,10},{3,11},{4,12},{5,13},{6,14},{7,15},{8,0},{9,1},... | collective-permute-start | bytes 786440 | tf_op jit(solution)/shard_map/ppermute | solution.py:24
  86.0 4.0 %collective-permute-start.12 = (f32[4,2048]{1,0:T(4,128)S(1)}, f32[4,2048]{1,0:T(4,128)S(1)}, u32[]{:S(2)}, u32[]{:S(2)}) collective-permute-start(f32[4,2048]{1,0:T(4,128)S(1)} %slice_select_fusion.4), channel_id=1, source_target_pairs={{0,4},{1,5},{2,6},{3,7},{4,0},{5,1},{6,2},{7,3},{8,12},{9,13},{10,... | collective-permute-start | bytes 98312 | tf_op jit(solution)/shard_map/ppermute | solution.py:19
  86.8 3.8 %collective-permute-start.10 = (f32[1,2048]{1,0:T(1,128)S(1)}, f32[1,2048]{1,0:T(1,128)S(1)}, u32[]{:S(2)}, u32[]{:S(2)}) collective-permute-start(f32[1,2048]{1,0:T(1,128)S(1)} %broadcast_select_fusion.18), channel_id=1, source_target_pairs={{0,1},{1,0},{2,3},{3,2},{4,5},{5,4},{6,7},{7,6},{8,9},{9,8},{10,11... | collective-permute-start | bytes 24584 | tf_op jit(solution)/shard_map/ppermute | solution.py:19
  90.0 3.8 %collective-permute-start.13 = (f32[2,2048]{1,0:T(2,128)S(1)}, f32[2,2048]{1,0:T(2,128)S(1)}, u32[]{:S(2)}, u32[]{:S(2)}) collective-permute-start(f32[2,2048]{1,0:T(2,128)S(1)} %broadcast_select_fusion.4), channel_id=1, source_target_pairs={{0,2},{1,3},{2,0},{3,1},{4,6},{5,7},{6,4},{7,5},{8,10},{9,11},{10,... | collective-permute-start | bytes 49160 | tf_op jit(solution)/shard_map/ppermute | solution.py:19
  90.6 13.1 %collective-permute-start.15 = (bf16[4,2,8,2048]{3,2,1,0:T(8,128)(2,1)S(1)}, bf16[4,2,8,2048]{3,2,1,0:T(8,128)(2,1)S(1)}, u32[]{:S(2)}, u32[]{:S(2)}) collective-permute-start(bf16[4,2,8,2048]{3,2,1,0:T(8,128)(2,1)S(1)} %get-tuple-element.62), channel_id=1, source_target_pairs={{0,8},{1,9},{2,10},{3,11},{4,12},{5,13},{6,14},{7,15},{8,0},{9,1},... | collective-permute-start | bytes 786440 | tf_op jit(solution)/shard_map/ppermute | solution.py:24
  107.1 4.0 %collective-permute-start.16 = (f32[4,2048]{1,0:T(4,128)S(1)}, f32[4,2048]{1,0:T(4,128)S(1)}, u32[]{:S(2)}, u32[]{:S(2)}) collective-permute-start(f32[4,2048]{1,0:T(4,128)S(1)} %slice_select_fusion.3), channel_id=1, source_target_pairs={{0,4},{1,5},{2,6},{3,7},{4,0},{5,1},{6,2},{7,3},{8,12},{9,13},{10,... | collective-permute-start | bytes 98312 | tf_op jit(solution)/shard_map/ppermute | solution.py:19
  107.9 4.8 %collective-permute-start.14 = (f32[1,2048]{1,0:T(1,128)S(1)}, f32[1,2048]{1,0:T(1,128)S(1)}, u32[]{:S(2)}, u32[]{:S(2)}) collective-permute-start(f32[1,2048]{1,0:T(1,128)S(1)} %broadcast_select_fusion.16), channel_id=1, source_target_pairs={{0,1},{1,0},{2,3},{3,2},{4,5},{5,4},{6,7},{7,6},{8,9},{9,8},{10,11... | collective-permute-start | bytes 24584 | tf_op jit(solution)/shard_map/ppermute | solution.py:19
  111.2 3.8 %collective-permute-start.17 = (f32[2,2048]{1,0:T(2,128)S(1)}, f32[2,2048]{1,0:T(2,128)S(1)}, u32[]{:S(2)}, u32[]{:S(2)}) collective-permute-start(f32[2,2048]{1,0:T(2,128)S(1)} %broadcast_select_fusion.3), channel_id=1, source_target_pairs={{0,2},{1,3},{2,0},{3,1},{4,6},{5,7},{6,4},{7,5},{8,10},{9,11},{10,... | collective-permute-start | bytes 49160 | tf_op jit(solution)/shard_map/ppermute | solution.py:19
  112.7 13.1 %collective-permute-start.19 = (bf16[4,2,8,2048]{3,2,1,0:T(8,128)(2,1)S(1)}, bf16[4,2,8,2048]{3,2,1,0:T(8,128)(2,1)S(1)}, u32[]{:S(2)}, u32[]{:S(2)}) collective-permute-start(bf16[4,2,8,2048]{3,2,1,0:T(8,128)(2,1)S(1)} %get-tuple-element.55), channel_id=1, source_target_pairs={{0,8},{1,9},{2,10},{3,11},{4,12},{5,13},{6,14},{7,15},{8,0},{9,1},... | collective-permute-start | bytes 786440 | tf_op jit(solution)/shard_map/ppermute | solution.py:24
  129.4 4.0 %collective-permute-start.20 = (f32[4,2048]{1,0:T(4,128)S(1)}, f32[4,2048]{1,0:T(4,128)S(1)}, u32[]{:S(2)}, u32[]{:S(2)}) collective-permute-start(f32[4,2048]{1,0:T(4,128)S(1)} %slice_select_fusion.2), channel_id=1, source_target_pairs={{0,4},{1,5},{2,6},{3,7},{4,0},{5,1},{6,2},{7,3},{8,12},{9,13},{10,... | collective-permute-start | bytes 98312 | tf_op jit(solution)/shard_map/ppermute | solution.py:19
  130.2 3.8 %collective-permute-start.18 = (f32[1,2048]{1,0:T(1,128)S(1)}, f32[1,2048]{1,0:T(1,128)S(1)}, u32[]{:S(2)}, u32[]{:S(2)}) collective-permute-start(f32[1,2048]{1,0:T(1,128)S(1)} %broadcast_select_fusion.14), channel_id=1, source_target_pairs={{0,1},{1,0},{2,3},{3,2},{4,5},{5,4},{6,7},{7,6},{8,9},{9,8},{10,11... | collective-permute-start | bytes 24584 | tf_op jit(solution)/shard_map/ppermute | solution.py:19
  133.5 3.8 %collective-permute-start.21 = (f32[2,2048]{1,0:T(2,128)S(1)}, f32[2,2048]{1,0:T(2,128)S(1)}, u32[]{:S(2)}, u32[]{:S(2)}) collective-permute-start(f32[2,2048]{1,0:T(2,128)S(1)} %broadcast_select_fusion.2), channel_id=1, source_target_pairs={{0,2},{1,3},{2,0},{3,1},{4,6},{5,7},{6,4},{7,5},{8,10},{9,11},{10,... | collective-permute-start | bytes 49160 | tf_op jit(solution)/shard_map/ppermute | solution.py:19
  134.1 13.1 %collective-permute-start.23 = (bf16[4,2,8,2048]{3,2,1,0:T(8,128)(2,1)S(1)}, bf16[4,2,8,2048]{3,2,1,0:T(8,128)(2,1)S(1)}, u32[]{:S(2)}, u32[]{:S(2)}) collective-permute-start(bf16[4,2,8,2048]{3,2,1,0:T(8,128)(2,1)S(1)} %get-tuple-element.48), channel_id=1, source_target_pairs={{0,8},{1,9},{2,10},{3,11},{4,12},{5,13},{6,14},{7,15},{8,0},{9,1},... | collective-permute-start | bytes 786440 | tf_op jit(solution)/shard_map/ppermute | solution.py:24
  137.3 14.1 %collective-permute-start.22 = (f32[1,2048]{1,0:T(1,128)S(1)}, f32[1,2048]{1,0:T(1,128)S(1)}, u32[]{:S(2)}, u32[]{:S(2)}) collective-permute-start(f32[1,2048]{1,0:T(1,128)S(1)} %broadcast_select_fusion.12), channel_id=1, source_target_pairs={{0,1},{1,0},{2,3},{3,2},{4,5},{5,4},{6,7},{7,6},{8,9},{9,8},{10,11... | collective-permute-start | bytes 24584 | tf_op jit(solution)/shard_map/ppermute | solution.py:19
  150.6 4.3 %collective-permute-start.24 = (f32[4,2048]{1,0:T(4,128)S(1)}, f32[4,2048]{1,0:T(4,128)S(1)}, u32[]{:S(2)}, u32[]{:S(2)}) collective-permute-start(f32[4,2048]{1,0:T(4,128)S(1)} %slice_select_fusion.1), channel_id=1, source_target_pairs={{0,4},{1,5},{2,6},{3,7},{4,0},{5,1},{6,2},{7,3},{8,12},{9,13},{10,... | collective-permute-start | bytes 98312 | tf_op jit(solution)/shard_map/ppermute | solution.py:19
  151.4 15.3 %collective-permute-start.27 = (bf16[4,2,8,2048]{3,2,1,0:T(8,128)(2,1)S(1)}, bf16[4,2,8,2048]{3,2,1,0:T(8,128)(2,1)S(1)}, u32[]{:S(2)}, u32[]{:S(2)}) collective-permute-start(bf16[4,2,8,2048]{3,2,1,0:T(8,128)(2,1)S(1)} %get-tuple-element.41), channel_id=1, source_target_pairs={{0,8},{1,9},{2,10},{3,11},{4,12},{5,13},{6,14},{7,15},{8,0},{9,1},... | collective-permute-start | bytes 786440 | tf_op jit(solution)/shard_map/ppermute | solution.py:24
  154.9 15.9 %collective-permute-start.25 = (f32[2,2048]{1,0:T(2,128)S(1)}, f32[2,2048]{1,0:T(2,128)S(1)}, u32[]{:S(2)}, u32[]{:S(2)}) collective-permute-start(f32[2,2048]{1,0:T(2,128)S(1)} %broadcast_select_fusion.1), channel_id=1, source_target_pairs={{0,2},{1,3},{2,0},{3,1},{4,6},{5,7},{6,4},{7,5},{8,10},{9,11},{10,... | collective-permute-start | bytes 49160 | tf_op jit(solution)/shard_map/ppermute | solution.py:19
  170.8 4.0 %collective-permute-start.28 = (f32[4,2048]{1,0:T(4,128)S(1)}, f32[4,2048]{1,0:T(4,128)S(1)}, u32[]{:S(2)}, u32[]{:S(2)}) collective-permute-start(f32[4,2048]{1,0:T(4,128)S(1)} %slice_select_fusion), channel_id=1, source_target_pairs={{0,4},{1,5},{2,6},{3,7},{4,0},{5,1},{6,2},{7,3},{8,12},{9,13},{10,... | collective-permute-start | bytes 98312 | tf_op jit(solution)/shard_map/ppermute | solution.py:19
  174.8 3.8 %collective-permute-start.29 = (f32[2,2048]{1,0:T(2,128)S(1)}, f32[2,2048]{1,0:T(2,128)S(1)}, u32[]{:S(2)}, u32[]{:S(2)}) collective-permute-start(f32[2,2048]{1,0:T(2,128)S(1)} %broadcast_select_fusion), channel_id=1, source_target_pairs={{0,2},{1,3},{2,0},{3,1},{4,6},{5,7},{6,4},{7,5},{8,10},{9,11},{10,... | collective-permute-start | bytes 49160 | tf_op jit(solution)/shard_map/ppermute | solution.py:19
  176.3 2.4 %collective-permute-start.26 = (f32[1,2048]{1,0:T(1,128)S(1)}, f32[1,2048]{1,0:T(1,128)S(1)}, u32[]{:S(2)}, u32[]{:S(2)}) collective-permute-start(f32[1,2048]{1,0:T(1,128)S(1)} %broadcast_select_fusion.10), channel_id=1, source_target_pairs={{0,1},{1,0},{2,3},{3,2},{4,5},{5,4},{6,7},{7,6},{8,9},{9,8},{10,11... | collective-permute-start | bytes 24584 | tf_op jit(solution)/shard_map/ppermute | solution.py:19
  178.6 1.2 collective-permute-start.30
  (4 other events, 53.6 us)
where the time goes:
time: 181 us
  waiting for transfers between devices  100 us (55%)
  starting transfers between devices  35.1 us (19%)
  matrix products  23.5 us (13%)
  local copies, waits for them, and re-layouts  11.2 us (6%)
  between operations  8.08 us (4%)
  other arithmetic  2.56 us (1%)
    ppermute x7, waiting for transfers between devices, passed_along(): lax.ppermute(shard, axis, [(i, (i + by) % size) for i in range(size)])  72.1 us
    ppermute x24, waiting for transfers between devices, from_partner(): return lax.ppermute(value, axis, pairs)  27.9 us
    dot_general x8, matrix products, advance(): jnp.einsum('cfskbj,fbkpjl->pcfsbl', shifted, operator, preferred_element_...  21.2 us
    ppermute x24, starting transfers between devices, from_partner(): return lax.ppermute(value, axis, pairs)  18.3 us
    ppermute x7, starting transfers between devices, passed_along(): lax.ppermute(shard, axis, [(i, (i + by) % size) for i in range(size)])  16.8 us
    unnamed x49, local copies, waits for them, and re-layouts  4.16 us
    dynamic_slice x7, local copies, waits for them, and re-layouts, advance(): lax.dynamic_slice_in_dim(padded, band_offsets[band_pos] + reach, NBLK, 3)  4.14 us
  transfers between devices with their start and end apart: 31, of which 21 were waited for; matrix products, arithmetic and copies ran while one was open for 4% of the time, Pallas kernels for 0%

commit v1 on v0

v1 whole, which is shorter than its diff:
```python
import functools
import math

import jax
import jax.numpy as jnp
from jax import lax
from jax.experimental import pallas as pl
from jax.experimental.pallas import tpu as pltpu
from jax.sharding import PartitionSpec as P

BLOCK = 128
HANDOVERS = 8


def advance_blocks(offs, rows, e_ref, pad_ref, adv_ref, img_ref, scale, blocks, band, slots):
    for b in blocks:
        lhs = jnp.concatenate([pad_ref[b + offs[k]] for k in range(band)], axis=1)
        er = e_ref[b, :, 0].reshape(band * BLOCK, BLOCK)
        ei = e_ref[b, :, 1].reshape(band * BLOCK, BLOCK)
        p = jnp.dot(lhs, er, preferred_element_type=jnp.float32)
        q = jnp.dot(lhs, ei, preferred_element_type=jnp.float32)
        p = [p[c * slots : (c + 1) * slots] for c in range(4)]
        q = [q[c * slots : (c + 1) * slots] for c in range(4)]
        new = jnp.concatenate([p[0] - q[1], q[0] + p[1], p[2] + q[3], p[3] - q[2]], axis=0)
        new = new.astype(jnp.bfloat16)
        adv_ref[b] = new
        f = new.astype(jnp.float32)
        f = [f[c * slots : (c + 1) * slots] for c in range(4)]
        part = scale * (f[0] * f[2] + f[1] * f[3])
        for j in range(slots):
            at = (pl.ds(rows[j], 1), b)
            img_ref[at] = part[j : j + 1]


def zero_edges(pad_ref, reach):
    nblk = pad_ref.shape[0] - 2 * reach
    edge = jnp.zeros((reach,) + pad_ref.shape[1:], pad_ref.dtype)
    pad_ref[:reach] = edge
    pad_ref[reach + nblk :] = edge


def first_kernel(scale, sec_ref, offs_hbm, asgs_hbm, e_hbm, w_hbm, *rest):
    adv_ref, img_ref, code_ref = rest[:3]
    freqs = w_hbm.shape[1]
    later = rest[3 : 3 + freqs - 1]
    e_ref, pad_ref, off_ref, asg_ref, w_ref, e_sems, w_sems = rest[3 + freqs - 1 :]
    nblk, band = e_ref.shape[:2]
    slots = w_ref.shape[2]
    reach = band // 2
    loads = [
        pltpu.make_async_copy(w_hbm, w_ref, w_sems.at[0]),
        pltpu.make_async_copy(offs_hbm, off_ref, w_sems.at[1]),
        pltpu.make_async_copy(asgs_hbm, asg_ref, w_sems.at[2]),
    ]
    for c in loads:
        c.start()
    copies = stream(e_hbm, e_ref, e_sems, 0)
    zero_edges(pad_ref, reach)
    for c in loads:
        c.wait()
    for f in range(freqs):
        for b in range(nblk):
            cols = slice(b * BLOCK, (b + 1) * BLOCK)
            block = [w_ref[c, f, :, cols].astype(jnp.float32) for c in range(4)]
            block = jnp.concatenate(block, axis=0).astype(jnp.bfloat16)
            if f == 0:
                pad_ref[reach + b] = block
            else:
                later[f - 1][b] = block
    sec = sec_ref[0]
    offs = [off_ref[sec, k] + reach for k in range(band)]
    rows = [asg_ref[sec, j] for j in range(slots)]
    for k, value in enumerate(offs + rows):
        code_ref[k] = jnp.full(code_ref.shape[1:], value, jnp.int32)
    for c, blocks in copies:
        c.wait()
        advance_blocks(
            offs, rows, e_ref, pad_ref, adv_ref, img_ref, scale, blocks, band, slots
        )


def stream(e_hbm, e_ref, sems, f):
    parts = sems.shape[0]
    per = e_ref.shape[0] // parts
    copies = []
    for i in range(parts):
        at = pl.ds(i * per, per)
        copies.append(pltpu.make_async_copy(e_hbm.at[f, at], e_ref.at[at], sems.at[i]))
        copies[-1].start()
    return [(c, range(i * per, (i + 1) * per)) for i, c in enumerate(copies)]


def next_kernel(scale, f, code_ref, e_hbm, w_ref, tok, adv_ref, img_ref, e_ref, pad_ref, e_sems):
    copies = stream(e_hbm, e_ref, e_sems, f)
    nblk, band = e_ref.shape[:2]
    reach = band // 2
    slots = img_ref.shape[0]
    code = [code_ref[k][0, 0] for k in range(band + slots)]
    zero_edges(pad_ref, reach)
    pad_ref[reach : reach + nblk] = w_ref[...]
    for c, blocks in copies:
        c.wait()
        advance_blocks(
            code[:band], code[band:], e_ref, pad_ref, adv_ref, img_ref, scale, blocks, band, slots
        )


def step_kernel(scale, f, code_ref, e_ref, w_ref, adv_ref, img_ref, pad_ref):
    nblk, band = e_ref.shape[1:3]
    reach = band // 2
    slots = img_ref.shape[0]
    code = [code_ref[k][0, 0] for k in range(band + slots)]
    zero_edges(pad_ref, reach)
    pad_ref[reach : reach + nblk] = w_ref[...]
    advance_blocks(
        code[:band], code[band:], e_ref.at[f], pad_ref, adv_ref, img_ref, scale, range(nblk),
        band, slots,
    )


SMEM = pl.BlockSpec(memory_space=pltpu.SMEM)
VMEM = pl.BlockSpec(memory_space=pltpu.VMEM)
HBM = pl.BlockSpec(memory_space=pltpu.HBM)
ANY = pl.BlockSpec(memory_space=pl.ANY)


def held(x, space):
    return pltpu.with_memory_space_constraint(x, space)


def cost(e_shape, rows):
    macs = math.prod(e_shape) * rows
    return pl.CostEstimate(flops=2 * macs, bytes_accessed=BLOCK, transcendentals=0)


def run_first(sec, offsets, assign, extrap, fronts, scale):
    nblk, band = extrap.shape[1:3]
    nfield, freqs, slots, points = fronts.shape
    rows = nfield * slots
    parts = math.gcd(4, nblk)
    wave = pltpu.VMEM((nblk, rows, BLOCK), jnp.bfloat16)
    return pl.pallas_call(
        functools.partial(first_kernel, scale),
        out_shape=(
            wave,
            pltpu.VMEM((slots, nblk, BLOCK), jnp.float32),
            pltpu.VMEM((band + slots, 8, BLOCK), jnp.int32),
        )
        + (wave,) * (freqs - 1),
        in_specs=[SMEM, HBM, HBM, HBM, HBM],
        out_specs=(VMEM,) * (2 + freqs),
        scratch_shapes=[
            pltpu.VMEM(extrap.shape[1:], extrap.dtype),
            pltpu.VMEM((nblk + 2 * (band // 2), rows, BLOCK), jnp.bfloat16),
            pltpu.SMEM(offsets.shape, jnp.int32),
            pltpu.SMEM(assign.shape, jnp.int32),
            pltpu.VMEM(fronts.shape, fronts.dtype),
            pltpu.SemaphoreType.DMA((parts,)),
            pltpu.SemaphoreType.DMA((3,)),
        ],
        compiler_params=pltpu.CompilerParams(vmem_limit_bytes=8 * 2**20),
        cost_estimate=cost(extrap.shape[1:], rows),
        name="first",
    )(held(sec, pltpu.SMEM), *[held(x, pltpu.HBM) for x in (offsets, assign, extrap, fronts)])


def run_step(f, code, e, w, scale, token=None):
    streamed = token is not None
    nblk, band = e.shape[1:3]
    rows = w.shape[1]
    pad = pltpu.VMEM((nblk + 2 * (band // 2), rows, BLOCK), jnp.bfloat16)
    scratch = [pad]
    if streamed:
        parts = math.gcd(4, nblk)
        scratch = [pltpu.VMEM(e.shape[1:], e.dtype), pad, pltpu.SemaphoreType.DMA((parts,))]
    return pl.pallas_call(
        functools.partial(next_kernel if streamed else step_kernel, scale, f),
        out_shape=(
            pltpu.VMEM((nblk, rows, BLOCK), jnp.bfloat16),
            pltpu.VMEM((rows // 4, nblk, BLOCK), jnp.float32),
        ),
        in_specs=[VMEM, HBM if streamed else VMEM, VMEM] + ([ANY] if streamed else []),
        out_specs=(VMEM, VMEM),
        scratch_shapes=scratch,
        compiler_params=pltpu.CompilerParams(vmem_limit_bytes=(8 if streamed else 4) * 2**20),
        cost_estimate=cost(e.shape[1:], rows),
        name="next" if streamed else "step",
    )(
        held(code, pltpu.VMEM),
        held(e, pltpu.HBM if streamed else pltpu.VMEM),
        held(w, pltpu.VMEM),
        *([token] if streamed else []),
    )


def fold_owners(partial, me, owners):
    bit = owners // 2
    size = lax.axis_size("depth")
    while bit:
        half = partial.shape[0] // 2
        lower, upper = partial[:half], partial[half:]
        mine_up = me // bit % 2 == 1
        outgoing = jnp.where(mine_up, lower, upper)
        kept = jnp.where(mine_up, upper, lower)
        partial = kept + lax.ppermute(outgoing, "depth", [(i, i ^ bit) for i in range(size)])
        bit //= 2
    return partial


def on_device(fronts, extrap, offsets, assign):
    sections = offsets.shape[0]
    size = lax.axis_size("depth")
    owners = size // sections
    index = lax.axis_index("depth")
    section, me = index // owners, index % owners
    sec = section.astype(jnp.int32)[None]
    nfield, freqs, slots, points = fronts.shape
    nblk = extrap.shape[1]
    scale = 1.0 / math.sqrt(2.0 * owners * freqs)
    onward = [(i, (i + owners) % size) for i in range(size)]
    waves, images = [None] * freqs, []
    for r in range(HANDOVERS):
        parts = []
        for f in range(freqs):
            if r == 0 and f == 0:
                adv, img, code, *later = run_first(sec, offsets, assign, extrap, fronts, scale)
                token = lax.ppermute(img[:1], "depth", [(i, i ^ 1) for i in range(size)])
            elif r == 0:
                adv, img = run_step(f, code, extrap, later[f - 1], scale, token)
            else:
                adv, img = run_step(f, code, extrap, waves[f], scale)
            parts.append(img)
            waves[f] = lax.ppermute(adv, "depth", onward) if r + 1 < HANDOVERS else adv
        images.append(sum(parts[1:], parts[0]))
    early = fold_owners(jnp.stack(images[:-1], axis=1), me, owners)
    late = fold_owners(jnp.stack(images[-1:], axis=1), me, owners)
    images = jnp.concatenate([early, late], axis=1).reshape(HANDOVERS, 1, points)
    last = jnp.stack(waves).reshape(freqs, nblk, nfield, slots, BLOCK)
    last = last.transpose(2, 0, 3, 1, 4).reshape(fronts.shape)
    return images, last


def solution(mesh):
    placed = (
        P(None, ("groups", "depth"), None, None),
        P("depth", None, None, None, None, None),
        P(),
        P(),
    )
    return jax.shard_map(
        on_device,
        mesh=mesh,
        in_specs=placed,
        out_specs=(P(None, ("groups", "depth"), None), P(None, ("groups", "depth"), None, None)),
        check_vma=False,
    )
```

time: 181 us -> 107 us (0.59)
  waiting for transfers between devices: 100 us -> 66.1 us
  matrix products: 23.5 us -> 0 us
  starting transfers between devices: 35.1 us -> 14.2 us
  Pallas kernels: 0 us -> 20 us
  local copies, waits for them, and re-layouts: 11.2 us -> 4.02 us
  between operations: 8.08 us -> 1.02 us
    ppermute x31 -> x21, waiting for transfers between devices: 100 us -> 66.1 us  [the longest x14 57.8 us: on_device(): waves[f] = lax.ppermute(adv, 'depth', onward) if r + 1 < HANDOVERS else adv]
    dot_general x16 -> x0, matrix products: 23.5 us -> none  [the longest x8 21.2 us: advance(): jnp.einsum('cfskbj,fbkpjl->pcfsbl', shifted, operator, preferred_element_...]
    ppermute x31 -> x21, starting transfers between devices: 35.1 us -> 14.2 us  [the longest x14 8.3 us: on_device(): waves[f] = lax.ppermute(adv, 'depth', onward) if r + 1 < HANDOVERS else adv]
    pallas_call x0 -> x16, Pallas kernels: none -> 20 us  [the longest x15 17 us: run_step(): pl.pallas_call(functools.partial(next_kernel if streamed else step_kernel...]
    dynamic_slice x8 -> x0, local copies, waits for them, and re-layouts: 4.85 us -> none  [the longest x7 4.14 us: advance(): lax.dynamic_slice_in_dim(padded, band_offsets[band_pos] + reach, NBLK, 3)]
    unnamed x49 -> x8, local copies, waits for them, and re-layouts: 4.16 us -> 4.01 us
  transfers between devices with their start and end apart: 31 -> 21, of which waited for: 21 -> 18; matrix products, arithmetic and copies ran while one was open for 4% -> 1% of each run, Pallas kernels for 0% -> 15%
where the time goes in v1:
time: 107 us
  waiting for transfers between devices  66.1 us (62%)
  Pallas kernels  20 us (19%)
  starting transfers between devices  14.2 us (13%)
  local copies, waits for them, and re-layouts  4.02 us (4%)
  other arithmetic  1.62 us (2%)
    ppermute x14, waiting for transfers between devices, on_device(): waves[f] = lax.ppermute(adv, 'depth', onward) if r + 1 < HANDOVERS else adv  57.8 us
    pallas_call x15, Pallas kernels, run_step(): pl.pallas_call(functools.partial(next_kernel if streamed else step_kernel...  17 us
    ppermute x6, waiting for transfers between devices, fold_owners(): lax.ppermute(outgoing, 'depth', [(i, i ^ bit) for i in range(size)])  8.31 us
    ppermute x14, starting transfers between devices, on_device(): waves[f] = lax.ppermute(adv, 'depth', onward) if r + 1 < HANDOVERS else adv  8.3 us
    ppermute x6, starting transfers between devices, fold_owners(): lax.ppermute(outgoing, 'depth', [(i, i ^ bit) for i in range(size)])  5.37 us
    unnamed x8, local copies, waits for them, and re-layouts  4.01 us
    pallas_call x1, Pallas kernels, run_first(): pl.pallas_call(functools.partial(first_kernel, scale), out_shape=(wave, p...  2.99 us
  transfers between devices with their start and end apart: 21, of which 18 were waited for; matrix products, arithmetic and copies ran while one was open for 1% of the time, Pallas kernels for 15%

profile of v1, /device:TPU:0, one launch (start us, length us, event | category | flops | bytes accessed | tf_op | source)
XLA Modules:
  0.0 107.0 jit_solution(10469755685682163926)
XLA Ops:
  0.6 3.0 %first.1 = (bf16[16,32,128]{2,1,0:T(8,128)(2,1)S(1)}, f32[8,16,128]{2,1,0:T(8,128)S(1)}, s32[13,8,128]{2,1,0:T(8,128)S(1)}, bf16[16,32,128]{2,1,0:T(8,128)(2,1)S(1)}) custom-call(s32[1]{0:T(128)} %bitcast.sec_ref, s32[2,5]{1,0:T(2,128)} %offs_hbm.1, s32[2,8]{1,0:T(2,128)} %asgs_hbm.1, bf16[2,16,5,2,128,128]{5,4,3,2,1,0:T(8,128)(2,1)} %e_ref.27, ...), custom_call_target="tpu_custom_call" | custom-call | flops 167772160 | bytes 128 | tf_op jit(solution)/shard_map/first/pallas_call | solution.py:142
  4.2 3.7 %collective-permute-start.1 = (bf16[16,32,128]{2,1,0:T(8,128)(2,1)S(1)}, bf16[16,32,128]{2,1,0:T(8,128)(2,1)S(1)}, u32[]{:S(2)}, u32[]{:S(2)}) collective-permute-start(bf16[16,32,128]{2,1,0:T(8,128)(2,1)S(1)} %get-tuple-element.40), channel_id=1, source_target_pairs={{0,8},{1,9},{2,10},{3,11},{4,12},{5,13},{6,14},{7,15},{8,0},{9,1},... | collective-permute-start | bytes 393224 | tf_op jit(solution)/shard_map/ppermute | solution.py:233
  7.8 2.9 %next.1 = (bf16[16,32,128]{2,1,0:T(8,128)(2,1)S(1)}, f32[8,16,128]{2,1,0:T(8,128)S(1)}) custom-call(s32[13,8,128]{2,1,0:T(8,128)S(1)} %get-tuple-element.37.code_ref, bf16[2,16,5,2,128,128]{5,4,3,2,1,0:T(8,128)(2,1)} %e_ref.27, bf16[16,32,128]{2,1,0:T(8,128)(2,1)S(1)} %get-tuple-element.38.w_ref, f32[1,16,128]{2,1,0:T(8,128)S(1)} %collective-permute-done.tok), custom_call_target="tpu_custom_call" | custom-call | flops 167772160 | bytes 128 | tf_op jit(solution)/shard_map/next/pallas_call | solution.py:176
  10.7 1.2 %collective-permute-start.2 = (bf16[16,32,128]{2,1,0:T(8,128)(2,1)S(1)}, bf16[16,32,128]{2,1,0:T(8,128)(2,1)S(1)}, u32[]{:S(2)}, u32[]{:S(2)}) collective-permute-start(bf16[16,32,128]{2,1,0:T(8,128)(2,1)S(1)} %get-tuple-element.42), channel_id=1, source_target_pairs={{0,8},{1,9},{2,10},{3,11},{4,12},{5,13},{6,14},{7,15},{8,0},{9,1},... | collective-permute-start | bytes 393224 | tf_op jit(solution)/shard_map/ppermute | solution.py:233
  11.9 3.1 %collective-permute-done.1.w_ref = bf16[16,32,128]{2,1,0:T(8,128)(2,1)S(1)} collective-permute-done((bf16[16,32,128]{2,1,0:T(8,128)(2,1)S(1)}, bf16[16,32,128]{2,1,0:T(8,128)(2,1)S(1)}, u32[]{:S(2)}, u32[]{:S(2)}) %collective-permute-start.1) | collective-permute-done | bytes 131104 | tf_op jit(solution)/shard_map/ppermute | solution.py:233
  15.0 4.0 %copy-done = bf16[2,16,5,2,128,128]{5,4,3,2,1,0:T(8,128)(2,1)S(1)} copy-done((bf16[2,16,5,2,128,128]{5,4,3,2,1,0:T(8,128)(2,1)S(1)}, bf16[2,16,5,2,128,128]{5,4,3,2,1,0:T(8,128)(2,1)}, u32[]{:S(2)}) %copy-start) | copy-done | bytes 10485784
  21.3 2.7 %collective-permute-start.4 = (bf16[16,32,128]{2,1,0:T(8,128)(2,1)S(1)}, bf16[16,32,128]{2,1,0:T(8,128)(2,1)S(1)}, u32[]{:S(2)}, u32[]{:S(2)}) collective-permute-start(bf16[16,32,128]{2,1,0:T(8,128)(2,1)S(1)} %get-tuple-element.46), channel_id=1, source_target_pairs={{0,8},{1,9},{2,10},{3,11},{4,12},{5,13},{6,14},{7,15},{8,0},{9,1},... | collective-permute-start | bytes 393224 | tf_op jit(solution)/shard_map/ppermute | solution.py:233
  24.1 6.1 %collective-permute-done.3.w_ref = bf16[16,32,128]{2,1,0:T(8,128)(2,1)S(1)} collective-permute-done((bf16[16,32,128]{2,1,0:T(8,128)(2,1)S(1)}, bf16[16,32,128]{2,1,0:T(8,128)(2,1)S(1)}, u32[]{:S(2)}, u32[]{:S(2)}) %collective-permute-start.3) | collective-permute-done | bytes 131104 | tf_op jit(solution)/shard_map/ppermute | solution.py:233
  30.2 1.0 step.16
  31.3 4.5 %collective-permute-done.4.w_ref = bf16[16,32,128]{2,1,0:T(8,128)(2,1)S(1)} collective-permute-done((bf16[16,32,128]{2,1,0:T(8,128)(2,1)S(1)}, bf16[16,32,128]{2,1,0:T(8,128)(2,1)S(1)}, u32[]{:S(2)}, u32[]{:S(2)}) %collective-permute-start.4) | collective-permute-done | bytes 131104 | tf_op jit(solution)/shard_map/ppermute | solution.py:233
  35.8 1.0 step.17
  36.9 4.5 %collective-permute-done.5.w_ref = bf16[16,32,128]{2,1,0:T(8,128)(2,1)S(1)} collective-permute-done((bf16[16,32,128]{2,1,0:T(8,128)(2,1)S(1)}, bf16[16,32,128]{2,1,0:T(8,128)(2,1)S(1)}, u32[]{:S(2)}, u32[]{:S(2)}) %collective-permute-start.5) | collective-permute-done | bytes 131104 | tf_op jit(solution)/shard_map/ppermute | solution.py:233
  41.4 1.0 step.18
  42.5 4.5 %collective-permute-done.6.w_ref = bf16[16,32,128]{2,1,0:T(8,128)(2,1)S(1)} collective-permute-done((bf16[16,32,128]{2,1,0:T(8,128)(2,1)S(1)}, bf16[16,32,128]{2,1,0:T(8,128)(2,1)S(1)}, u32[]{:S(2)}, u32[]{:S(2)}) %collective-permute-start.6) | collective-permute-done | bytes 131104 | tf_op jit(solution)/shard_map/ppermute | solution.py:233
  48.2 4.5 %collective-permute-done.7.w_ref = bf16[16,32,128]{2,1,0:T(8,128)(2,1)S(1)} collective-permute-done((bf16[16,32,128]{2,1,0:T(8,128)(2,1)S(1)}, bf16[16,32,128]{2,1,0:T(8,128)(2,1)S(1)}, u32[]{:S(2)}, u32[]{:S(2)}) %collective-permute-start.7) | collective-permute-done | bytes 131104 | tf_op jit(solution)/shard_map/ppermute | solution.py:233
  53.8 4.5 %collective-permute-done.8.w_ref = bf16[16,32,128]{2,1,0:T(8,128)(2,1)S(1)} collective-permute-done((bf16[16,32,128]{2,1,0:T(8,128)(2,1)S(1)}, bf16[16,32,128]{2,1,0:T(8,128)(2,1)S(1)}, u32[]{:S(2)}, u32[]{:S(2)}) %collective-permute-start.8) | collective-permute-done | bytes 131104 | tf_op jit(solution)/shard_map/ppermute | solution.py:233
  59.4 4.5 %collective-permute-done.9.w_ref = bf16[16,32,128]{2,1,0:T(8,128)(2,1)S(1)} collective-permute-done((bf16[16,32,128]{2,1,0:T(8,128)(2,1)S(1)}, bf16[16,32,128]{2,1,0:T(8,128)(2,1)S(1)}, u32[]{:S(2)}, u32[]{:S(2)}) %collective-permute-start.9) | collective-permute-done | bytes 131104 | tf_op jit(solution)/shard_map/ppermute | solution.py:233
  63.9 1.0 step.22
  65.0 4.5 %collective-permute-done.10.w_ref = bf16[16,32,128]{2,1,0:T(8,128)(2,1)S(1)} collective-permute-done((bf16[16,32,128]{2,1,0:T(8,128)(2,1)S(1)}, bf16[16,32,128]{2,1,0:T(8,128)(2,1)S(1)}, u32[]{:S(2)}, u32[]{:S(2)}) %collective-permute-start.10) | collective-permute-done | bytes 131104 | tf_op jit(solution)/shard_map/ppermute | solution.py:233
  69.5 1.2 %step.23 = (bf16[16,32,128]{2,1,0:T(8,128)(2,1)S(1)}, f32[8,16,128]{2,1,0:T(8,128)S(1)}) custom-call(s32[13,8,128]{2,1,0:T(8,128)S(1)} %get-tuple-element.37.code_ref, bf16[2,16,5,2,128,128]{5,4,3,2,1,0:T(8,128)(2,1)S(1)} %bitcast.28, bf16[16,32,128]{2,1,0:T(8,128)(2,1)S(1)} %collective-permute-done.10.w_ref), custom_call_target="tpu_custom_call" | custom-call | flops 167772160 | bytes 128 | tf_op jit(solution)/shard_map/step/pallas_call | solution.py:176
  70.8 4.3 %collective-permute-done.11.w_ref = bf16[16,32,128]{2,1,0:T(8,128)(2,1)S(1)} collective-permute-done((bf16[16,32,128]{2,1,0:T(8,128)(2,1)S(1)}, bf16[16,32,128]{2,1,0:T(8,128)(2,1)S(1)}, u32[]{:S(2)}, u32[]{:S(2)}) %collective-permute-start.11) | collective-permute-done | bytes 131104 | tf_op jit(solution)/shard_map/ppermute | solution.py:233
  76.2 4.7 %collective-permute-done.12.w_ref = bf16[16,32,128]{2,1,0:T(8,128)(2,1)S(1)} collective-permute-done((bf16[16,32,128]{2,1,0:T(8,128)(2,1)S(1)}, bf16[16,32,128]{2,1,0:T(8,128)(2,1)S(1)}, u32[]{:S(2)}, u32[]{:S(2)}) %collective-permute-start.12) | collective-permute-done | bytes 131104 | tf_op jit(solution)/shard_map/ppermute | solution.py:233
  80.9 1.0 step.25
  82.0 4.3 %collective-permute-done.16.w_ref = bf16[16,32,128]{2,1,0:T(8,128)(2,1)S(1)} collective-permute-done((bf16[16,32,128]{2,1,0:T(8,128)(2,1)S(1)}, bf16[16,32,128]{2,1,0:T(8,128)(2,1)S(1)}, u32[]{:S(2)}, u32[]{:S(2)}) %collective-permute-start.16) | collective-permute-done | bytes 131104 | tf_op jit(solution)/shard_map/ppermute | solution.py:233
  87.4 3.3 %collective-permute-done.17.w_ref = bf16[16,32,128]{2,1,0:T(8,128)(2,1)S(1)} collective-permute-done((bf16[16,32,128]{2,1,0:T(8,128)(2,1)S(1)}, bf16[16,32,128]{2,1,0:T(8,128)(2,1)S(1)}, u32[]{:S(2)}, u32[]{:S(2)}) %collective-permute-start.17) | collective-permute-done | bytes 131104 | tf_op jit(solution)/shard_map/ppermute | solution.py:233
  92.0 1.9 %collective-permute-start.13 = (f32[4,7,16,128]{3,2,0,1:T(8,128)S(1)}, f32[4,7,16,128]{3,2,0,1:T(8,128)S(1)}, u32[]{:S(2)}, u32[]{:S(2)}) collective-permute-start(f32[4,7,16,128]{3,2,0,1:T(8,128)S(1)} %slice_select_fusion), channel_id=1, source_target_pairs={{0,4},{1,5},{2,6},{3,7},{4,0},{5,1},{6,2},{7,3},{8,12},{9,13},{10,... | collective-permute-start | bytes 688136 | tf_op jit(solution)/shard_map/ppermute | solution.py:205
  93.9 2.2 %collective-permute-done.18 = f32[4,1,16,128]{3,2,0,1:T(8,128)S(1)} collective-permute-done((f32[4,1,16,128]{3,2,0,1:T(8,128)S(1)}, f32[4,1,16,128]{3,2,0,1:T(8,128)S(1)}, u32[]{:S(2)}, u32[]{:S(2)}) %collective-permute-start.18) | collective-permute-done | bytes 32800 | tf_op jit(solution)/shard_map/ppermute | solution.py:205
  96.1 1.6 %collective-permute-start.19 = (f32[2,1,16,128]{3,2,0,1:T(8,128)S(1)}, f32[2,1,16,128]{3,2,0,1:T(8,128)S(1)}, u32[]{:S(2)}, u32[]{:S(2)}) collective-permute-start(f32[2,1,16,128]{3,2,0,1:T(8,128)S(1)} %slice_select_fusion.3), channel_id=1, source_target_pairs={{0,2},{1,3},{2,0},{3,1},{4,6},{5,7},{6,4},{7,5},{8,10},{9,11},{10,... | collective-permute-start | bytes 49160 | tf_op jit(solution)/shard_map/ppermute | solution.py:205
  98.4 1.6 %collective-permute-done.19 = f32[2,1,16,128]{3,2,0,1:T(8,128)S(1)} collective-permute-done((f32[2,1,16,128]{3,2,0,1:T(8,128)S(1)}, f32[2,1,16,128]{3,2,0,1:T(8,128)S(1)}, u32[]{:S(2)}, u32[]{:S(2)}) %collective-permute-start.19) | collective-permute-done | bytes 16416 | tf_op jit(solution)/shard_map/ppermute | solution.py:205
  100.1 1.6 %collective-permute-start.14 = (f32[2,7,16,128]{3,2,0,1:T(8,128)S(1)}, f32[2,7,16,128]{3,2,0,1:T(8,128)S(1)}, u32[]{:S(2)}, u32[]{:S(2)}) collective-permute-start(f32[2,7,16,128]{3,2,0,1:T(8,128)S(1)} %slice_select_fusion.1), channel_id=1, source_target_pairs={{0,2},{1,3},{2,0},{3,1},{4,6},{5,7},{6,4},{7,5},{8,10},{9,11},{10,... | collective-permute-start | bytes 344072 | tf_op jit(solution)/shard_map/ppermute | solution.py:205
  101.7 3.3 %collective-permute-done.14 = f32[2,7,16,128]{3,2,0,1:T(8,128)S(1)} collective-permute-done((f32[2,7,16,128]{3,2,0,1:T(8,128)S(1)}, f32[2,7,16,128]{3,2,0,1:T(8,128)S(1)}, u32[]{:S(2)}, u32[]{:S(2)}) %collective-permute-start.14) | collective-permute-done | bytes 114720 | tf_op jit(solution)/shard_map/ppermute | solution.py:205
  105.1 1.2 %collective-permute-done.15 = f32[1,7,16,128]{3,2,0,1:T(8,128)S(1)} collective-permute-done((f32[1,7,16,128]{3,2,0,1:T(8,128)S(1)}, f32[1,7,16,128]{3,2,0,1:T(8,128)S(1)}, u32[]{:S(2)}, u32[]{:S(2)}) %collective-permute-start.15) | collective-permute-done | bytes 57376 | tf_op jit(solution)/shard_map/ppermute | solution.py:205
  (58 shorter events, 11.5 us)
Async XLA Ops:
  3.7 4.2 %collective-permute-start = (f32[1,16,128]{2,1,0:T(8,128)S(1)}, f32[1,16,128]{2,1,0:T(8,128)S(1)}, u32[]{:S(2)}, u32[]{:S(2)}) collective-permute-start(f32[1,16,128]{2,1,0:T(8,128)S(1)} %slice.41), channel_id=1, source_target_pairs={{0,1},{1,0},{2,3},{3,2},{4,5},{5,4},{6,7},{7,6},{8,9},{9,8},{10,11... | collective-permute-start | bytes 24584 | tf_op jit(solution)/shard_map/ppermute | solution.py:227
  4.2 10.8 %collective-permute-start.1 = (bf16[16,32,128]{2,1,0:T(8,128)(2,1)S(1)}, bf16[16,32,128]{2,1,0:T(8,128)(2,1)S(1)}, u32[]{:S(2)}, u32[]{:S(2)}) collective-permute-start(bf16[16,32,128]{2,1,0:T(8,128)(2,1)S(1)} %get-tuple-element.40), channel_id=1, source_target_pairs={{0,8},{1,9},{2,10},{3,11},{4,12},{5,13},{6,14},{7,15},{8,0},{9,1},... | collective-permute-start | bytes 393224 | tf_op jit(solution)/shard_map/ppermute | solution.py:233
  10.7 9.6 %collective-permute-start.2 = (bf16[16,32,128]{2,1,0:T(8,128)(2,1)S(1)}, bf16[16,32,128]{2,1,0:T(8,128)(2,1)S(1)}, u32[]{:S(2)}, u32[]{:S(2)}) collective-permute-start(bf16[16,32,128]{2,1,0:T(8,128)(2,1)S(1)} %get-tuple-element.42), channel_id=1, source_target_pairs={{0,8},{1,9},{2,10},{3,11},{4,12},{5,13},{6,14},{7,15},{8,0},{9,1},... | collective-permute-start | bytes 393224 | tf_op jit(solution)/shard_map/ppermute | solution.py:233
  15.0 4.0 %copy-start = (bf16[2,16,5,2,128,128]{5,4,3,2,1,0:T(8,128)(2,1)S(1)}, bf16[2,16,5,2,128,128]{5,4,3,2,1,0:T(8,128)(2,1)}, u32[]{:S(2)}) copy-start(bf16[2,16,5,2,128,128]{5,4,3,2,1,0:T(8,128)(2,1)} %e_ref.27) | copy-start | bytes 31457284
  19.0 11.2 %slice-start = ((s8[10485760]{0:T(1024)(128)(4,1)}), s8[4194304]{0:T(1024)(128)(4,1)S(1)}, s32[]{:S(2)}) async-start(s8[10485760]{0:T(1024)(128)(4,1)} %bitcast.27), calls=%async_computation | async-start | bytes 8388608
  19.0 11.2 %slice-start.1 = ((s8[10485760]{0:T(1024)(128)(4,1)}), s8[4194304]{0:T(1024)(128)(4,1)S(1)}, s32[]{:S(2)}) async-start(s8[10485760]{0:T(1024)(128)(4,1)} %bitcast.27), calls=%async_computation.1 | async-start | bytes 8388608
  20.0 10.2 %slice-start.2 = ((s8[10485760]{0:T(1024)(128)(4,1)}), s8[2097152]{0:T(1024)(128)(4,1)S(1)}, s32[]{:S(2)}) async-start(s8[10485760]{0:T(1024)(128)(4,1)} %bitcast.27), calls=%async_computation.2 | async-start | bytes 4194304
  20.0 10.2 %collective-permute-start.3 = (bf16[16,32,128]{2,1,0:T(8,128)(2,1)S(1)}, bf16[16,32,128]{2,1,0:T(8,128)(2,1)S(1)}, u32[]{:S(2)}, u32[]{:S(2)}) collective-permute-start(bf16[16,32,128]{2,1,0:T(8,128)(2,1)S(1)} %get-tuple-element.44), channel_id=1, source_target_pairs={{0,8},{1,9},{2,10},{3,11},{4,12},{5,13},{6,14},{7,15},{8,0},{9,1},... | collective-permute-start | bytes 393224 | tf_op jit(solution)/shard_map/ppermute | solution.py:233
  21.3 14.5 %collective-permute-start.4 = (bf16[16,32,128]{2,1,0:T(8,128)(2,1)S(1)}, bf16[16,32,128]{2,1,0:T(8,128)(2,1)S(1)}, u32[]{:S(2)}, u32[]{:S(2)}) collective-permute-start(bf16[16,32,128]{2,1,0:T(8,128)(2,1)S(1)} %get-tuple-element.46), channel_id=1, source_target_pairs={{0,8},{1,9},{2,10},{3,11},{4,12},{5,13},{6,14},{7,15},{8,0},{9,1},... | collective-permute-start | bytes 393224 | tf_op jit(solution)/shard_map/ppermute | solution.py:233
  31.2 10.2 %collective-permute-start.5 = (bf16[16,32,128]{2,1,0:T(8,128)(2,1)S(1)}, bf16[16,32,128]{2,1,0:T(8,128)(2,1)S(1)}, u32[]{:S(2)}, u32[]{:S(2)}) collective-permute-start(bf16[16,32,128]{2,1,0:T(8,128)(2,1)S(1)} %get-tuple-element.48), channel_id=1, source_target_pairs={{0,8},{1,9},{2,10},{3,11},{4,12},{5,13},{6,14},{7,15},{8,0},{9,1},... | collective-permute-start | bytes 393224 | tf_op jit(solution)/shard_map/ppermute | solution.py:233
  36.8 10.2 %collective-permute-start.6 = (bf16[16,32,128]{2,1,0:T(8,128)(2,1)S(1)}, bf16[16,32,128]{2,1,0:T(8,128)(2,1)S(1)}, u32[]{:S(2)}, u32[]{:S(2)}) collective-permute-start(bf16[16,32,128]{2,1,0:T(8,128)(2,1)S(1)} %get-tuple-element.50), channel_id=1, source_target_pairs={{0,8},{1,9},{2,10},{3,11},{4,12},{5,13},{6,14},{7,15},{8,0},{9,1},... | collective-permute-start | bytes 393224 | tf_op jit(solution)/shard_map/ppermute | solution.py:233
  42.4 10.2 %collective-permute-start.7 = (bf16[16,32,128]{2,1,0:T(8,128)(2,1)S(1)}, bf16[16,32,128]{2,1,0:T(8,128)(2,1)S(1)}, u32[]{:S(2)}, u32[]{:S(2)}) collective-permute-start(bf16[16,32,128]{2,1,0:T(8,128)(2,1)S(1)} %get-tuple-element.52), channel_id=1, source_target_pairs={{0,8},{1,9},{2,10},{3,11},{4,12},{5,13},{6,14},{7,15},{8,0},{9,1},... | collective-permute-start | bytes 393224 | tf_op jit(solution)/shard_map/ppermute | solution.py:233
  48.1 10.2 %collective-permute-start.8 = (bf16[16,32,128]{2,1,0:T(8,128)(2,1)S(1)}, bf16[16,32,128]{2,1,0:T(8,128)(2,1)S(1)}, u32[]{:S(2)}, u32[]{:S(2)}) collective-permute-start(bf16[16,32,128]{2,1,0:T(8,128)(2,1)S(1)} %get-tuple-element.54), channel_id=1, source_target_pairs={{0,8},{1,9},{2,10},{3,11},{4,12},{5,13},{6,14},{7,15},{8,0},{9,1},... | collective-permute-start | bytes 393224 | tf_op jit(solution)/shard_map/ppermute | solution.py:233
  53.7 10.2 %collective-permute-start.9 = (bf16[16,32,128]{2,1,0:T(8,128)(2,1)S(1)}, bf16[16,32,128]{2,1,0:T(8,128)(2,1)S(1)}, u32[]{:S(2)}, u32[]{:S(2)}) collective-permute-start(bf16[16,32,128]{2,1,0:T(8,128)(2,1)S(1)} %get-tuple-element.56), channel_id=1, source_target_pairs={{0,8},{1,9},{2,10},{3,11},{4,12},{5,13},{6,14},{7,15},{8,0},{9,1},... | collective-permute-start | bytes 393224 | tf_op jit(solution)/shard_map/ppermute | solution.py:233
  59.3 10.2 %collective-permute-start.10 = (bf16[16,32,128]{2,1,0:T(8,128)(2,1)S(1)}, bf16[16,32,128]{2,1,0:T(8,128)(2,1)S(1)}, u32[]{:S(2)}, u32[]{:S(2)}) collective-permute-start(bf16[16,32,128]{2,1,0:T(8,128)(2,1)S(1)} %get-tuple-element.58), channel_id=1, source_target_pairs={{0,8},{1,9},{2,10},{3,11},{4,12},{5,13},{6,14},{7,15},{8,0},{9,1},... | collective-permute-start | bytes 393224 | tf_op jit(solution)/shard_map/ppermute | solution.py:233
  64.9 10.2 %collective-permute-start.11 = (bf16[16,32,128]{2,1,0:T(8,128)(2,1)S(1)}, bf16[16,32,128]{2,1,0:T(8,128)(2,1)S(1)}, u32[]{:S(2)}, u32[]{:S(2)}) collective-permute-start(bf16[16,32,128]{2,1,0:T(8,128)(2,1)S(1)} %get-tuple-element.60), channel_id=1, source_target_pairs={{0,8},{1,9},{2,10},{3,11},{4,12},{5,13},{6,14},{7,15},{8,0},{9,1},... | collective-permute-start | bytes 393224 | tf_op jit(solution)/shard_map/ppermute | solution.py:233
  70.7 10.2 %collective-permute-start.12 = (bf16[16,32,128]{2,1,0:T(8,128)(2,1)S(1)}, bf16[16,32,128]{2,1,0:T(8,128)(2,1)S(1)}, u32[]{:S(2)}, u32[]{:S(2)}) collective-permute-start(bf16[16,32,128]{2,1,0:T(8,128)(2,1)S(1)} %get-tuple-element.62), channel_id=1, source_target_pairs={{0,8},{1,9},{2,10},{3,11},{4,12},{5,13},{6,14},{7,15},{8,0},{9,1},... | collective-permute-start | bytes 393224 | tf_op jit(solution)/shard_map/ppermute | solution.py:233
  76.1 10.2 %collective-permute-start.16 = (bf16[16,32,128]{2,1,0:T(8,128)(2,1)S(1)}, bf16[16,32,128]{2,1,0:T(8,128)(2,1)S(1)}, u32[]{:S(2)}, u32[]{:S(2)}) collective-permute-start(bf16[16,32,128]{2,1,0:T(8,128)(2,1)S(1)} %get-tuple-element.64), channel_id=1, source_target_pairs={{0,8},{1,9},{2,10},{3,11},{4,12},{5,13},{6,14},{7,15},{8,0},{9,1},... | collective-permute-start | bytes 393224 | tf_op jit(solution)/shard_map/ppermute | solution.py:233
  81.9 8.7 %collective-permute-start.17 = (bf16[16,32,128]{2,1,0:T(8,128)(2,1)S(1)}, bf16[16,32,128]{2,1,0:T(8,128)(2,1)S(1)}, u32[]{:S(2)}, u32[]{:S(2)}) collective-permute-start(bf16[16,32,128]{2,1,0:T(8,128)(2,1)S(1)} %get-tuple-element.66), channel_id=1, source_target_pairs={{0,8},{1,9},{2,10},{3,11},{4,12},{5,13},{6,14},{7,15},{8,0},{9,1},... | collective-permute-start | bytes 393224 | tf_op jit(solution)/shard_map/ppermute | solution.py:233
  91.7 4.4 %collective-permute-start.18 = (f32[4,1,16,128]{3,2,0,1:T(8,128)S(1)}, f32[4,1,16,128]{3,2,0,1:T(8,128)S(1)}, u32[]{:S(2)}, u32[]{:S(2)}) collective-permute-start(f32[4,1,16,128]{3,2,0,1:T(8,128)S(1)} %select_bitcast_fusion), channel_id=1, source_target_pairs={{0,4},{1,5},{2,6},{3,7},{4,0},{5,1},{6,2},{7,3},{8,12},{9,13},{10,... | collective-permute-start | bytes 98312 | tf_op jit(solution)/shard_map/ppermute | solution.py:205
  92.0 8.0 %collective-permute-start.13 = (f32[4,7,16,128]{3,2,0,1:T(8,128)S(1)}, f32[4,7,16,128]{3,2,0,1:T(8,128)S(1)}, u32[]{:S(2)}, u32[]{:S(2)}) collective-permute-start(f32[4,7,16,128]{3,2,0,1:T(8,128)S(1)} %slice_select_fusion), channel_id=1, source_target_pairs={{0,4},{1,5},{2,6},{3,7},{4,0},{5,1},{6,2},{7,3},{8,12},{9,13},{10,... | collective-permute-start | bytes 688136 | tf_op jit(solution)/shard_map/ppermute | solution.py:205
  96.1 3.9 %collective-permute-start.19 = (f32[2,1,16,128]{3,2,0,1:T(8,128)S(1)}, f32[2,1,16,128]{3,2,0,1:T(8,128)S(1)}, u32[]{:S(2)}, u32[]{:S(2)}) collective-permute-start(f32[2,1,16,128]{3,2,0,1:T(8,128)S(1)} %slice_select_fusion.3), channel_id=1, source_target_pairs={{0,2},{1,3},{2,0},{3,1},{4,6},{5,7},{6,4},{7,5},{8,10},{9,11},{10,... | collective-permute-start | bytes 49160 | tf_op jit(solution)/shard_map/ppermute | solution.py:205
  100.1 4.9 %collective-permute-start.14 = (f32[2,7,16,128]{3,2,0,1:T(8,128)S(1)}, f32[2,7,16,128]{3,2,0,1:T(8,128)S(1)}, u32[]{:S(2)}, u32[]{:S(2)}) collective-permute-start(f32[2,7,16,128]{3,2,0,1:T(8,128)S(1)} %slice_select_fusion.1), channel_id=1, source_target_pairs={{0,2},{1,3},{2,0},{3,1},{4,6},{5,7},{6,4},{7,5},{8,10},{9,11},{10,... | collective-permute-start | bytes 344072 | tf_op jit(solution)/shard_map/ppermute | solution.py:205
  101.7 3.4 %collective-permute-start.20 = (f32[1,1,16,128]{3,2,0,1:T(8,128)S(1)}, f32[1,1,16,128]{3,2,0,1:T(8,128)S(1)}, u32[]{:S(2)}, u32[]{:S(2)}) collective-permute-start(f32[1,1,16,128]{3,2,0,1:T(8,128)S(1)} %slice_select_fusion.4), channel_id=1, source_target_pairs={{0,1},{1,0},{2,3},{3,2},{4,5},{5,4},{6,7},{7,6},{8,9},{9,8},{10,11... | collective-permute-start | bytes 24584 | tf_op jit(solution)/shard_map/ppermute | solution.py:205
  105.0 1.3 %collective-permute-start.15 = (f32[1,7,16,128]{3,2,0,1:T(8,128)S(1)}, f32[1,7,16,128]{3,2,0,1:T(8,128)S(1)}, u32[]{:S(2)}, u32[]{:S(2)}) collective-permute-start(f32[1,7,16,128]{3,2,0,1:T(8,128)S(1)} %slice_select_fusion.2), channel_id=1, source_target_pairs={{0,1},{1,0},{2,3},{3,2},{4,5},{5,4},{6,7},{7,6},{8,9},{9,8},{10,11... | collective-permute-start | bytes 172040 | tf_op jit(solution)/shard_map/ppermute | solution.py:205

commit v2 on v1

v2 whole, which is shorter than its diff:
```python
import functools
import math

import jax
import jax.numpy as jnp
from jax import lax
from jax.experimental import pallas as pl
from jax.experimental.pallas import tpu as pltpu
from jax.sharding import PartitionSpec as P

BLOCK = 128
HANDOVERS = 8
PARTS = 4


def advance_blocks(offs, rows, e_ref, pad_ref, adv_ref, img_ref, scale, blocks, band, slots):
    for b in blocks:
        lhs = jnp.concatenate([pad_ref[b + offs[k]] for k in range(band)], axis=1)
        er = e_ref[b, :, 0].reshape(band * BLOCK, BLOCK)
        ei = e_ref[b, :, 1].reshape(band * BLOCK, BLOCK)
        p = jnp.dot(lhs, er, preferred_element_type=jnp.float32)
        q = jnp.dot(lhs, ei, preferred_element_type=jnp.float32)
        p = [p[c * slots : (c + 1) * slots] for c in range(4)]
        q = [q[c * slots : (c + 1) * slots] for c in range(4)]
        new = jnp.concatenate([p[0] - q[1], q[0] + p[1], p[2] + q[3], p[3] - q[2]], axis=0)
        new = new.astype(jnp.bfloat16)
        adv_ref[b] = new
        f = new.astype(jnp.float32)
        f = [f[c * slots : (c + 1) * slots] for c in range(4)]
        part = scale * (f[0] * f[2] + f[1] * f[3])
        for j in range(slots):
            at = (pl.ds(rows[j], 1), b)
            img_ref[at] = part[j : j + 1]


def zero_edges(pad_ref, reach):
    nblk = pad_ref.shape[0] - 2 * reach
    edge = jnp.zeros((reach,) + pad_ref.shape[1:], pad_ref.dtype)
    pad_ref[:reach] = edge
    pad_ref[reach + nblk :] = edge


def stream(e_hbm, e_ref, sems):
    parts = sems.shape[0]
    per = e_ref.shape[0] // parts
    copies = []
    for i in range(parts):
        at = pl.ds(i * per, per)
        copies.append(pltpu.make_async_copy(e_hbm.at[at], e_ref.at[at], sems.at[i]))
        copies[-1].start()
    return [(c, range(i * per, (i + 1) * per)) for i, c in enumerate(copies)]


def fill_blocks(w_ref, pad_ref, reach):
    for b in range(pad_ref.shape[0] - 2 * reach):
        cols = slice(b * BLOCK, (b + 1) * BLOCK)
        block = [w_ref[c, :, cols].astype(jnp.float32) for c in range(4)]
        pad_ref[reach + b] = jnp.concatenate(block, axis=0).astype(jnp.bfloat16)


def read_code(code_ref, band, slots):
    code = [code_ref[k][0, 0] for k in range(band + slots)]
    return code[:band], code[band:]


def first_kernel(
    scale, place_ref, offs_hbm, asgs_hbm, e_hbm, w_hbm, adv_ref, img_ref, code_ref, e_all,
    pad_ref, off_ref, asg_ref, w_ref, e_sems, w_sems,
):
    e_ref = e_all.at[0]
    nblk, band = e_ref.shape[:2]
    slots = w_ref.shape[1]
    reach = band // 2
    loads = [
        pltpu.make_async_copy(w_hbm.at[:, 0], w_ref, w_sems.at[0]),
        pltpu.make_async_copy(offs_hbm, off_ref, w_sems.at[1]),
        pltpu.make_async_copy(asgs_hbm, asg_ref, w_sems.at[2]),
    ]
    for c in loads:
        c.start()
    copies = stream(e_hbm.at[0], e_ref, e_sems)
    zero_edges(pad_ref, reach)
    for c in loads:
        c.wait()
    fill_blocks(w_ref, pad_ref, reach)
    sec, me = place_ref[0], place_ref[1]
    offs = [off_ref[sec, k] + reach for k in range(band)]
    rows = [asg_ref[sec, j] for j in range(slots)]
    for k, value in enumerate(offs + rows + [me]):
        code_ref[k] = jnp.full(code_ref.shape[1:], value, jnp.int32)
    for c, blocks in copies:
        c.wait()
        advance_blocks(
            offs, rows, e_ref, pad_ref, adv_ref, img_ref, scale, blocks, band, slots
        )


def next_kernel(
    scale, f, code_ref, old, e_hbm, w_hbm, tok, adv_ref, img_ref, e_all,
    pad_ref, w_ref, e_sems, w_sem,
):
    e_ref = e_all.at[f]
    load = pltpu.make_async_copy(w_hbm.at[:, f], w_ref, w_sem.at[0])
    load.start()
    copies = stream(e_hbm.at[f], e_ref, e_sems)
    nblk, band = e_ref.shape[:2]
    reach = band // 2
    slots = img_ref.shape[0]
    offs, rows = read_code(code_ref, band, slots)
    zero_edges(pad_ref, reach)
    load.wait()
    fill_blocks(w_ref, pad_ref, reach)
    for c, blocks in copies:
        c.wait()
        advance_blocks(
            offs, rows, e_ref, pad_ref, adv_ref, img_ref, scale, blocks, band, slots
        )


def step_kernel(scale, f, code_ref, e_ref, w_ref, adv_ref, img_ref, pad_ref):
    nblk, band = e_ref.shape[1:3]
    reach = band // 2
    slots = img_ref.shape[0]
    offs, rows = read_code(code_ref, band, slots)
    zero_edges(pad_ref, reach)
    pad_ref[reach : reach + nblk] = w_ref[...]
    advance_blocks(
        offs, rows, e_ref.at[f], pad_ref, adv_ref, img_ref, scale, range(nblk), band, slots
    )


def split_kernel(bit, freqs, code_ref, *refs):
    ins, (keep_ref, send_ref) = refs[:-2], refs[-2:]
    side = (code_ref[code_ref.shape[0] - 1][0, 0] >> bit) & 1
    halves, rounds = keep_ref.shape[:2]
    for half in range(halves):
        for out, row in ((keep_ref, 2 * half + side), (send_ref, 2 * half + 1 - side)):
            for r in range(rounds):
                if bit == 0:
                    value = ins[r * freqs][row]
                    for f in range(1, freqs):
                        value += ins[r * freqs + f][row]
                else:
                    value = ins[0][row, r] + ins[1][row, r].astype(jnp.float32)
                out[half, r] = value.astype(out.dtype)


SMEM = pl.BlockSpec(memory_space=pltpu.SMEM)
VMEM = pl.BlockSpec(memory_space=pltpu.VMEM)
HBM = pl.BlockSpec(memory_space=pltpu.HBM)
ANY = pl.BlockSpec(memory_space=pl.ANY)


def held(x, space):
    return pltpu.with_memory_space_constraint(x, space)


def cost(e_shape, rows):
    macs = math.prod(e_shape) * rows
    return pl.CostEstimate(flops=2 * macs, bytes_accessed=BLOCK, transcendentals=0)


def run_first(place, offsets, assign, extrap, fronts, scale):
    nblk, band = extrap.shape[1:3]
    nfield, freqs, slots, points = fronts.shape
    rows = nfield * slots
    parts = math.gcd(PARTS, nblk)
    return pl.pallas_call(
        functools.partial(first_kernel, scale),
        out_shape=(
            pltpu.VMEM((nblk, rows, BLOCK), jnp.bfloat16),
            pltpu.VMEM((slots, nblk, BLOCK), jnp.float32),
            pltpu.VMEM((band + slots + 1, 8, BLOCK), jnp.int32),
            pltpu.VMEM(extrap.shape, extrap.dtype),
        ),
        in_specs=[SMEM, HBM, HBM, HBM, HBM],
        out_specs=(VMEM,) * 4,
        scratch_shapes=[
            pltpu.VMEM((nblk + 2 * (band // 2), rows, BLOCK), jnp.bfloat16),
            pltpu.SMEM(offsets.shape, jnp.int32),
            pltpu.SMEM(assign.shape, jnp.int32),
            pltpu.VMEM((nfield, slots, points), fronts.dtype),
            pltpu.SemaphoreType.DMA((parts,)),
            pltpu.SemaphoreType.DMA((3,)),
        ],
        compiler_params=pltpu.CompilerParams(vmem_limit_bytes=4 * 2**20),
        cost_estimate=cost(extrap.shape[1:], rows),
        name="first",
    )(held(place, pltpu.SMEM), *[held(x, pltpu.HBM) for x in (offsets, assign, extrap, fronts)])


def run_next(f, code, e, extrap, fronts, token, scale):
    nblk, band = e.shape[1:3]
    nfield, freqs, slots, points = fronts.shape
    rows = nfield * slots
    parts = math.gcd(PARTS, nblk)
    return pl.pallas_call(
        functools.partial(next_kernel, scale, f),
        out_shape=(
            pltpu.VMEM((nblk, rows, BLOCK), jnp.bfloat16),
            pltpu.VMEM((slots, nblk, BLOCK), jnp.float32),
            pltpu.VMEM(e.shape, e.dtype),
        ),
        in_specs=[VMEM, VMEM, HBM, HBM, ANY],
        out_specs=(VMEM,) * 3,
        scratch_shapes=[
            pltpu.VMEM((nblk + 2 * (band // 2), rows, BLOCK), jnp.bfloat16),
            pltpu.VMEM((nfield, slots, points), fronts.dtype),
            pltpu.SemaphoreType.DMA((parts,)),
            pltpu.SemaphoreType.DMA((1,)),
        ],
        input_output_aliases={1: 2},
        compiler_params=pltpu.CompilerParams(vmem_limit_bytes=4 * 2**20),
        cost_estimate=cost(e.shape[1:], rows),
        name="next",
    )(held(code, pltpu.VMEM), held(e, pltpu.VMEM), held(extrap, pltpu.HBM), held(fronts, pltpu.HBM), token)


def run_step(f, code, e, w, scale):
    nblk, band = e.shape[1:3]
    rows = w.shape[1]
    return pl.pallas_call(
        functools.partial(step_kernel, scale, f),
        out_shape=(
            pltpu.VMEM((nblk, rows, BLOCK), jnp.bfloat16),
            pltpu.VMEM((rows // 4, nblk, BLOCK), jnp.float32),
        ),
        in_specs=[VMEM, VMEM, VMEM],
        out_specs=(VMEM, VMEM),
        scratch_shapes=[pltpu.VMEM((nblk + 2 * (band // 2), rows, BLOCK), jnp.bfloat16)],
        compiler_params=pltpu.CompilerParams(vmem_limit_bytes=4 * 2**20),
        cost_estimate=cost(e.shape[1:], rows),
        name="step",
    )(*[held(x, pltpu.VMEM) for x in (code, e, w)])


def fold_owners(code, parts, rounds, owners):
    size = lax.axis_size("depth")
    rows, nblk, lanes = parts[0].shape
    freqs = len(parts) // rounds
    ins, bit = parts, 0
    while 1 << bit < owners:
        rows //= 2
        half = (rows, rounds, nblk, lanes)
        keep, send = pl.pallas_call(
            functools.partial(split_kernel, bit, freqs),
            out_shape=(pltpu.VMEM(half, jnp.float32), pltpu.VMEM(half, jnp.bfloat16)),
            in_specs=[VMEM] * (1 + len(ins)),
            out_specs=(VMEM, VMEM),
            compiler_params=pltpu.CompilerParams(vmem_limit_bytes=4 * 2**20),
            cost_estimate=pl.CostEstimate(flops=BLOCK, bytes_accessed=BLOCK, transcendentals=0),
            name="split",
        )(*[held(x, pltpu.VMEM) for x in (code, *ins)])
        came = lax.ppermute(send, "depth", [(i, i ^ (1 << bit)) for i in range(size)])
        ins = (keep, came)
        bit += 1
    return ins[0] + ins[1].astype(jnp.float32)


def on_device(fronts, extrap, offsets, assign):
    sections = offsets.shape[0]
    size = lax.axis_size("depth")
    owners = size // sections
    index = lax.axis_index("depth")
    place = jnp.stack([lax.div(index, owners), lax.rem(index, owners)]).astype(jnp.int32)
    nfield, freqs, slots, points = fronts.shape
    nblk = extrap.shape[1]
    scale = 1.0 / math.sqrt(2.0 * owners * freqs)
    onward = [(i, (i + owners) % size) for i in range(size)]
    waves, parts = [None] * freqs, []
    for r in range(HANDOVERS):
        for f in range(freqs):
            if r == 0 and f == 0:
                adv, img, code, e = run_first(place, offsets, assign, extrap, fronts, scale)
                token = lax.ppermute(img[:1], "depth", [(i, i ^ 1) for i in range(size)])
            elif r == 0:
                adv, img, e = run_next(f, code, e, extrap, fronts, token, scale)
            else:
                adv, img = run_step(f, code, e, waves[f], scale)
            parts.append(img)
            waves[f] = lax.ppermute(adv, "depth", onward) if r + 1 < HANDOVERS else adv
    images = fold_owners(code, parts, HANDOVERS, owners).reshape(HANDOVERS, 1, points)
    last = jnp.stack(waves).reshape(freqs, nblk, nfield, slots, BLOCK)
    last = last.transpose(2, 0, 3, 1, 4).reshape(fronts.shape)
    return images, last


def solution(mesh):
    placed = (
        P(None, ("groups", "depth"), None, None),
        P("depth", None, None, None, None, None),
        P(),
        P(),
    )
    return jax.shard_map(
        on_device,
        mesh=mesh,
        in_specs=placed,
        out_specs=(P(None, ("groups", "depth"), None), P(None, ("groups", "depth"), None, None)),
        check_vma=False,
    )
```

time: 107 us -> 101 us (0.944)
  local copies, waits for them, and re-layouts: 4.02 us -> 0.01 us
  waiting for transfers between devices: 66.1 us -> 63.2 us
  Pallas kernels: 20 us -> 21.3 us
    unnamed x8 -> x0, local copies, waits for them, and re-layouts: 4.01 us -> none
    ppermute x6 -> x3, waiting for transfers between devices: 8.31 us -> 5.26 us  [fold_owners(): came = lax.ppermute(send, 'depth', [(i, i ^ 1 << bit) for i in range(size)])]
    pallas_call x16 -> x19, Pallas kernels: 20 us -> 21.3 us  [the longest x14 14 us: run_step(): pl.pallas_call(functools.partial(step_kernel, scale, f), out_shape=(pltpu...]
    ppermute x6 -> x3, starting transfers between devices: 5.37 us -> 6.18 us  [fold_owners(): came = lax.ppermute(send, 'depth', [(i, i ^ 1 << bit) for i in range(size)])]
  transfers between devices with their start and end apart: 21 -> 18, of which waited for: 18 -> 17; matrix products, arithmetic and copies ran while one was open for 1% -> 1% of each run, Pallas kernels for 15% -> 16%
where the time goes in v2:
time: 101 us
  waiting for transfers between devices  63.2 us (63%)
  Pallas kernels  21.3 us (21%)
  starting transfers between devices  14.3 us (14%)
  other arithmetic  1.43 us (1%)
    ppermute x14, waiting for transfers between devices, on_device(): waves[f] = lax.ppermute(adv, 'depth', onward) if r + 1 < HANDOVERS else adv  57.9 us
    pallas_call x14, Pallas kernels, run_step(): pl.pallas_call(functools.partial(step_kernel, scale, f), out_shape=(pltpu...  14 us
    ppermute x14, starting transfers between devices, on_device(): waves[f] = lax.ppermute(adv, 'depth', onward) if r + 1 < HANDOVERS else adv  7.62 us
    ppermute x3, starting transfers between devices, fold_owners(): came = lax.ppermute(send, 'depth', [(i, i ^ 1 << bit) for i in range(size)])  6.18 us
    ppermute x3, waiting for transfers between devices, fold_owners(): came = lax.ppermute(send, 'depth', [(i, i ^ 1 << bit) for i in range(size)])  5.26 us
    pallas_call x1, Pallas kernels, run_next(): pl.pallas_call(functools.partial(next_kernel, scale, f), out_shape=(pltpu...  3.56 us
    pallas_call x1, Pallas kernels, run_first(): pl.pallas_call(functools.partial(first_kernel, scale), out_shape=(pltpu.V...  3.49 us
  transfers between devices with their start and end apart: 18, of which 17 were waited for; matrix products, arithmetic and copies ran while one was open for 1% of the time, Pallas kernels for 16%

profile of v2, /device:TPU:0, one launch (start us, length us, event | category | flops | bytes accessed | tf_op | source)
XLA Modules:
  0.0 101.1 jit_solution(8753174235288267251)
XLA Ops:
  0.7 3.5 %first.1 = (bf16[16,32,128]{2,1,0:T(8,128)(2,1)S(1)}, f32[8,16,128]{2,1,0:T(8,128)S(1)}, s32[14,8,128]{2,1,0:T(8,128)S(1)}, bf16[2,16,5,2,128,128]{5,4,3,2,1,0:T(8,128)(2,1)S(1)}) custom-call(s32[2]{0:T(128)S(1)} %pad_add_fusion.place_ref, s32[2,5]{1,0:T(2,128)} %offs_hbm.1, s32[2,8]{1,0:T(2,128)} %asgs_hbm.1, bf16[2,16,5,2,128,128]{5,4,3,2,1,0:T(8,128)(2,1)} %e_hbm.3, ...), custom_call_target="tpu_custom_call" | custom-call | flops 167772160 | bytes 128 | tf_op jit(solution)/shard_map/first/pallas_call | solution.py:168
  4.7 3.7 %collective-permute-start.1 = (bf16[16,32,128]{2,1,0:T(8,128)(2,1)S(1)}, bf16[16,32,128]{2,1,0:T(8,128)(2,1)S(1)}, u32[]{:S(2)}, u32[]{:S(2)}) collective-permute-start(bf16[16,32,128]{2,1,0:T(8,128)(2,1)S(1)} %get-tuple-element.48), channel_id=1, source_target_pairs={{0,8},{1,9},{2,10},{3,11},{4,12},{5,13},{6,14},{7,15},{8,0},{9,1},... | collective-permute-start | bytes 393224 | tf_op jit(solution)/shard_map/ppermute | solution.py:281
  8.4 3.6 %next.1 = (bf16[16,32,128]{2,1,0:T(8,128)(2,1)S(1)}, f32[8,16,128]{2,1,0:T(8,128)S(1)}, bf16[2,16,5,2,128,128]{5,4,3,2,1,0:T(8,128)(2,1)S(1)}) custom-call(s32[14,8,128]{2,1,0:T(8,128)S(1)} %get-tuple-element.43.code_ref, bf16[2,16,5,2,128,128]{5,4,3,2,1,0:T(8,128)(2,1)S(1)} %get-tuple-element.45.old, ...), custom_call_target="tpu_custom_call", output_to_operand_aliasing={{2}: (1, {})} | custom-call | flops 167772160 | bytes 128 | tf_op jit(solution)/shard_map/next/pallas_call | solution.py:197
  12.0 1.2 %collective-permute-start.2 = (bf16[16,32,128]{2,1,0:T(8,128)(2,1)S(1)}, bf16[16,32,128]{2,1,0:T(8,128)(2,1)S(1)}, u32[]{:S(2)}, u32[]{:S(2)}) collective-permute-start(bf16[16,32,128]{2,1,0:T(8,128)(2,1)S(1)} %get-tuple-element.50), channel_id=1, source_target_pairs={{0,8},{1,9},{2,10},{3,11},{4,12},{5,13},{6,14},{7,15},{8,0},{9,1},... | collective-permute-start | bytes 393224 | tf_op jit(solution)/shard_map/ppermute | solution.py:281
  13.1 2.2 %collective-permute-done.1.w_ref = bf16[16,32,128]{2,1,0:T(8,128)(2,1)S(1)} collective-permute-done((bf16[16,32,128]{2,1,0:T(8,128)(2,1)S(1)}, bf16[16,32,128]{2,1,0:T(8,128)(2,1)S(1)}, u32[]{:S(2)}, u32[]{:S(2)}) %collective-permute-start.1) | collective-permute-done | bytes 131104 | tf_op jit(solution)/shard_map/ppermute | solution.py:281
  15.3 1.0 step.14
  16.4 5.7 %collective-permute-done.2.w_ref = bf16[16,32,128]{2,1,0:T(8,128)(2,1)S(1)} collective-permute-done((bf16[16,32,128]{2,1,0:T(8,128)(2,1)S(1)}, bf16[16,32,128]{2,1,0:T(8,128)(2,1)S(1)}, u32[]{:S(2)}, u32[]{:S(2)}) %collective-permute-start.2) | collective-permute-done | bytes 131104 | tf_op jit(solution)/shard_map/ppermute | solution.py:281
  24.1 1.0 step.16
  25.1 2.0 %collective-permute-start.5 = (bf16[16,32,128]{2,1,0:T(8,128)(2,1)S(1)}, bf16[16,32,128]{2,1,0:T(8,128)(2,1)S(1)}, u32[]{:S(2)}, u32[]{:S(2)}) collective-permute-start(bf16[16,32,128]{2,1,0:T(8,128)(2,1)S(1)} %get-tuple-element.56), channel_id=1, source_target_pairs={{0,8},{1,9},{2,10},{3,11},{4,12},{5,13},{6,14},{7,15},{8,0},{9,1},... | collective-permute-start | bytes 393224 | tf_op jit(solution)/shard_map/ppermute | solution.py:281
  27.1 5.1 %collective-permute-done.4.w_ref = bf16[16,32,128]{2,1,0:T(8,128)(2,1)S(1)} collective-permute-done((bf16[16,32,128]{2,1,0:T(8,128)(2,1)S(1)}, bf16[16,32,128]{2,1,0:T(8,128)(2,1)S(1)}, u32[]{:S(2)}, u32[]{:S(2)}) %collective-permute-start.4) | collective-permute-done | bytes 131104 | tf_op jit(solution)/shard_map/ppermute | solution.py:281
  32.2 1.0 step.17
  33.3 3.1 %collective-permute-done.5.w_ref = bf16[16,32,128]{2,1,0:T(8,128)(2,1)S(1)} collective-permute-done((bf16[16,32,128]{2,1,0:T(8,128)(2,1)S(1)}, bf16[16,32,128]{2,1,0:T(8,128)(2,1)S(1)}, u32[]{:S(2)}, u32[]{:S(2)}) %collective-permute-start.5) | collective-permute-done | bytes 131104 | tf_op jit(solution)/shard_map/ppermute | solution.py:281
  37.5 5.9 %collective-permute-done.6.w_ref = bf16[16,32,128]{2,1,0:T(8,128)(2,1)S(1)} collective-permute-done((bf16[16,32,128]{2,1,0:T(8,128)(2,1)S(1)}, bf16[16,32,128]{2,1,0:T(8,128)(2,1)S(1)}, u32[]{:S(2)}, u32[]{:S(2)}) %collective-permute-start.6) | collective-permute-done | bytes 131104 | tf_op jit(solution)/shard_map/ppermute | solution.py:281
  44.5 4.5 %collective-permute-done.7.w_ref = bf16[16,32,128]{2,1,0:T(8,128)(2,1)S(1)} collective-permute-done((bf16[16,32,128]{2,1,0:T(8,128)(2,1)S(1)}, bf16[16,32,128]{2,1,0:T(8,128)(2,1)S(1)}, u32[]{:S(2)}, u32[]{:S(2)}) %collective-permute-start.7) | collective-permute-done | bytes 131104 | tf_op jit(solution)/shard_map/ppermute | solution.py:281
  50.1 4.5 %collective-permute-done.8.w_ref = bf16[16,32,128]{2,1,0:T(8,128)(2,1)S(1)} collective-permute-done((bf16[16,32,128]{2,1,0:T(8,128)(2,1)S(1)}, bf16[16,32,128]{2,1,0:T(8,128)(2,1)S(1)}, u32[]{:S(2)}, u32[]{:S(2)}) %collective-permute-start.8) | collective-permute-done | bytes 131104 | tf_op jit(solution)/shard_map/ppermute | solution.py:281
  55.7 4.5 %collective-permute-done.9.w_ref = bf16[16,32,128]{2,1,0:T(8,128)(2,1)S(1)} collective-permute-done((bf16[16,32,128]{2,1,0:T(8,128)(2,1)S(1)}, bf16[16,32,128]{2,1,0:T(8,128)(2,1)S(1)}, u32[]{:S(2)}, u32[]{:S(2)}) %collective-permute-start.9) | collective-permute-done | bytes 131104 | tf_op jit(solution)/shard_map/ppermute | solution.py:281
  60.3 1.0 step.22
  61.4 4.5 %collective-permute-done.10.w_ref = bf16[16,32,128]{2,1,0:T(8,128)(2,1)S(1)} collective-permute-done((bf16[16,32,128]{2,1,0:T(8,128)(2,1)S(1)}, bf16[16,32,128]{2,1,0:T(8,128)(2,1)S(1)}, u32[]{:S(2)}, u32[]{:S(2)}) %collective-permute-start.10) | collective-permute-done | bytes 131104 | tf_op jit(solution)/shard_map/ppermute | solution.py:281
  65.9 1.2 %step.23 = (bf16[16,32,128]{2,1,0:T(8,128)(2,1)S(1)}, f32[8,16,128]{2,1,0:T(8,128)S(1)}) custom-call(s32[14,8,128]{2,1,0:T(8,128)S(1)} %get-tuple-element.43.code_ref, bf16[2,16,5,2,128,128]{5,4,3,2,1,0:T(8,128)(2,1)S(1)} %get-tuple-element.47.e_ref, bf16[16,32,128]{2,1,0:T(8,128)(2,1)S(1)} %collective-permute-done.10.w_ref), custom_call_target="tpu_custom_call" | custom-call | flops 167772160 | bytes 128 | tf_op jit(solution)/shard_map/step/pallas_call | solution.py:222
  67.2 4.4 %collective-permute-done.11.w_ref = bf16[16,32,128]{2,1,0:T(8,128)(2,1)S(1)} collective-permute-done((bf16[16,32,128]{2,1,0:T(8,128)(2,1)S(1)}, bf16[16,32,128]{2,1,0:T(8,128)(2,1)S(1)}, u32[]{:S(2)}, u32[]{:S(2)}) %collective-permute-start.11) | collective-permute-done | bytes 131104 | tf_op jit(solution)/shard_map/ppermute | solution.py:281
  71.5 1.0 step.24
  72.6 4.7 %collective-permute-done.12.w_ref = bf16[16,32,128]{2,1,0:T(8,128)(2,1)S(1)} collective-permute-done((bf16[16,32,128]{2,1,0:T(8,128)(2,1)S(1)}, bf16[16,32,128]{2,1,0:T(8,128)(2,1)S(1)}, u32[]{:S(2)}, u32[]{:S(2)}) %collective-permute-start.12) | collective-permute-done | bytes 131104 | tf_op jit(solution)/shard_map/ppermute | solution.py:281
  77.3 1.0 step.25
  78.4 4.4 %collective-permute-done.13.w_ref = bf16[16,32,128]{2,1,0:T(8,128)(2,1)S(1)} collective-permute-done((bf16[16,32,128]{2,1,0:T(8,128)(2,1)S(1)}, bf16[16,32,128]{2,1,0:T(8,128)(2,1)S(1)}, u32[]{:S(2)}, u32[]{:S(2)}) %collective-permute-start.13) | collective-permute-done | bytes 131104 | tf_op jit(solution)/shard_map/ppermute | solution.py:281
  82.8 1.0 step.26
  83.8 3.2 %collective-permute-done.14.w_ref = bf16[16,32,128]{2,1,0:T(8,128)(2,1)S(1)} collective-permute-done((bf16[16,32,128]{2,1,0:T(8,128)(2,1)S(1)}, bf16[16,32,128]{2,1,0:T(8,128)(2,1)S(1)}, u32[]{:S(2)}, u32[]{:S(2)}) %collective-permute-start.14) | collective-permute-done | bytes 131104 | tf_op jit(solution)/shard_map/ppermute | solution.py:281
  87.0 1.0 step.27
  88.2 1.3 %collective-permute-done.15.refs_1_ = bf16[4,8,16,128]{3,2,1,0:T(8,128)(2,1)S(1)} collective-permute-done((bf16[4,8,16,128]{3,2,1,0:T(8,128)(2,1)S(1)}, bf16[4,8,16,128]{3,2,1,0:T(8,128)(2,1)S(1)}, u32[]{:S(2)}, u32[]{:S(2)}) %collective-permute-start.15) | collective-permute-done | bytes 131104 | tf_op jit(solution)/shard_map/ppermute | solution.py:254
  89.6 1.6 %collective-permute-start.16 = (bf16[2,8,16,128]{3,2,1,0:T(8,128)(2,1)S(1)}, bf16[2,8,16,128]{3,2,1,0:T(8,128)(2,1)S(1)}, u32[]{:S(2)}, u32[]{:S(2)}) collective-permute-start(bf16[2,8,16,128]{3,2,1,0:T(8,128)(2,1)S(1)} %get-tuple-element.79), channel_id=1, source_target_pairs={{0,2},{1,3},{2,0},{3,1},{4,6},{5,7},{6,4},{7,5},{8,10},{9,11},{10,... | collective-permute-start | bytes 196616 | tf_op jit(solution)/shard_map/ppermute | solution.py:254
  91.2 2.7 %collective-permute-done.16.refs_1_ = bf16[2,8,16,128]{3,2,1,0:T(8,128)(2,1)S(1)} collective-permute-done((bf16[2,8,16,128]{3,2,1,0:T(8,128)(2,1)S(1)}, bf16[2,8,16,128]{3,2,1,0:T(8,128)(2,1)S(1)}, u32[]{:S(2)}, u32[]{:S(2)}) %collective-permute-start.16) | collective-permute-done | bytes 65568 | tf_op jit(solution)/shard_map/ppermute | solution.py:254
  94.0 4.5 %collective-permute-start.17 = (bf16[1,8,16,128]{3,2,1,0:T(8,128)(2,1)S(1)}, bf16[1,8,16,128]{3,2,1,0:T(8,128)(2,1)S(1)}, u32[]{:S(2)}, u32[]{:S(2)}) collective-permute-start(bf16[1,8,16,128]{3,2,1,0:T(8,128)(2,1)S(1)} %get-tuple-element.81), channel_id=1, source_target_pairs={{0,4},{1,5},{2,6},{3,7},{4,0},{5,1},{6,2},{7,3},{8,12},{9,13},{10,... | collective-permute-start | bytes 98312 | tf_op jit(solution)/shard_map/ppermute | solution.py:254
  99.3 1.2 %collective-permute-done.17 = bf16[1,8,16,128]{3,2,1,0:T(8,128)(2,1)S(1)} collective-permute-done((bf16[1,8,16,128]{3,2,1,0:T(8,128)(2,1)S(1)}, bf16[1,8,16,128]{3,2,1,0:T(8,128)(2,1)S(1)}, u32[]{:S(2)}, u32[]{:S(2)}) %collective-permute-start.17) | collective-permute-done | bytes 32800 | tf_op jit(solution)/shard_map/ppermute | solution.py:254
  (27 shorter events, 8.9 us)
Async XLA Ops:
  4.2 4.2 %collective-permute-start = (f32[1,16,128]{2,1,0:T(8,128)S(1)}, f32[1,16,128]{2,1,0:T(8,128)S(1)}, u32[]{:S(2)}, u32[]{:S(2)}) collective-permute-start(f32[1,16,128]{2,1,0:T(8,128)S(1)} %slice.3), channel_id=1, source_target_pairs={{0,1},{1,0},{2,3},{3,2},{4,5},{5,4},{6,7},{7,6},{8,9},{9,8},{10,11... | collective-permute-start | bytes 24584 | tf_op jit(solution)/shard_map/ppermute | solution.py:275
  4.7 10.6 %collective-permute-start.1 = (bf16[16,32,128]{2,1,0:T(8,128)(2,1)S(1)}, bf16[16,32,128]{2,1,0:T(8,128)(2,1)S(1)}, u32[]{:S(2)}, u32[]{:S(2)}) collective-permute-start(bf16[16,32,128]{2,1,0:T(8,128)(2,1)S(1)} %get-tuple-element.48), channel_id=1, source_target_pairs={{0,8},{1,9},{2,10},{3,11},{4,12},{5,13},{6,14},{7,15},{8,0},{9,1},... | collective-permute-start | bytes 393224 | tf_op jit(solution)/shard_map/ppermute | solution.py:281
  12.0 10.1 %collective-permute-start.2 = (bf16[16,32,128]{2,1,0:T(8,128)(2,1)S(1)}, bf16[16,32,128]{2,1,0:T(8,128)(2,1)S(1)}, u32[]{:S(2)}, u32[]{:S(2)}) collective-permute-start(bf16[16,32,128]{2,1,0:T(8,128)(2,1)S(1)} %get-tuple-element.50), channel_id=1, source_target_pairs={{0,8},{1,9},{2,10},{3,11},{4,12},{5,13},{6,14},{7,15},{8,0},{9,1},... | collective-permute-start | bytes 393224 | tf_op jit(solution)/shard_map/ppermute | solution.py:281
  16.3 7.8 %collective-permute-start.3 = (bf16[16,32,128]{2,1,0:T(8,128)(2,1)S(1)}, bf16[16,32,128]{2,1,0:T(8,128)(2,1)S(1)}, u32[]{:S(2)}, u32[]{:S(2)}) collective-permute-start(bf16[16,32,128]{2,1,0:T(8,128)(2,1)S(1)} %get-tuple-element.52), channel_id=1, source_target_pairs={{0,8},{1,9},{2,10},{3,11},{4,12},{5,13},{6,14},{7,15},{8,0},{9,1},... | collective-permute-start | bytes 393224 | tf_op jit(solution)/shard_map/ppermute | solution.py:281
  23.1 9.1 %collective-permute-start.4 = (bf16[16,32,128]{2,1,0:T(8,128)(2,1)S(1)}, bf16[16,32,128]{2,1,0:T(8,128)(2,1)S(1)}, u32[]{:S(2)}, u32[]{:S(2)}) collective-permute-start(bf16[16,32,128]{2,1,0:T(8,128)(2,1)S(1)} %get-tuple-element.54), channel_id=1, source_target_pairs={{0,8},{1,9},{2,10},{3,11},{4,12},{5,13},{6,14},{7,15},{8,0},{9,1},... | collective-permute-start | bytes 393224 | tf_op jit(solution)/shard_map/ppermute | solution.py:281
  25.1 11.3 %collective-permute-start.5 = (bf16[16,32,128]{2,1,0:T(8,128)(2,1)S(1)}, bf16[16,32,128]{2,1,0:T(8,128)(2,1)S(1)}, u32[]{:S(2)}, u32[]{:S(2)}) collective-permute-start(bf16[16,32,128]{2,1,0:T(8,128)(2,1)S(1)} %get-tuple-element.56), channel_id=1, source_target_pairs={{0,8},{1,9},{2,10},{3,11},{4,12},{5,13},{6,14},{7,15},{8,0},{9,1},... | collective-permute-start | bytes 393224 | tf_op jit(solution)/shard_map/ppermute | solution.py:281
  33.2 10.2 %collective-permute-start.6 = (bf16[16,32,128]{2,1,0:T(8,128)(2,1)S(1)}, bf16[16,32,128]{2,1,0:T(8,128)(2,1)S(1)}, u32[]{:S(2)}, u32[]{:S(2)}) collective-permute-start(bf16[16,32,128]{2,1,0:T(8,128)(2,1)S(1)} %get-tuple-element.58), channel_id=1, source_target_pairs={{0,8},{1,9},{2,10},{3,11},{4,12},{5,13},{6,14},{7,15},{8,0},{9,1},... | collective-permute-start | bytes 393224 | tf_op jit(solution)/shard_map/ppermute | solution.py:281
  37.4 11.6 %collective-permute-start.7 = (bf16[16,32,128]{2,1,0:T(8,128)(2,1)S(1)}, bf16[16,32,128]{2,1,0:T(8,128)(2,1)S(1)}, u32[]{:S(2)}, u32[]{:S(2)}) collective-permute-start(bf16[16,32,128]{2,1,0:T(8,128)(2,1)S(1)} %get-tuple-element.60), channel_id=1, source_target_pairs={{0,8},{1,9},{2,10},{3,11},{4,12},{5,13},{6,14},{7,15},{8,0},{9,1},... | collective-permute-start | bytes 393224 | tf_op jit(solution)/shard_map/ppermute | solution.py:281
  44.4 10.2 %collective-permute-start.8 = (bf16[16,32,128]{2,1,0:T(8,128)(2,1)S(1)}, bf16[16,32,128]{2,1,0:T(8,128)(2,1)S(1)}, u32[]{:S(2)}, u32[]{:S(2)}) collective-permute-start(bf16[16,32,128]{2,1,0:T(8,128)(2,1)S(1)} %get-tuple-element.62), channel_id=1, source_target_pairs={{0,8},{1,9},{2,10},{3,11},{4,12},{5,13},{6,14},{7,15},{8,0},{9,1},... | collective-permute-start | bytes 393224 | tf_op jit(solution)/shard_map/ppermute | solution.py:281
  50.0 10.2 %collective-permute-start.9 = (bf16[16,32,128]{2,1,0:T(8,128)(2,1)S(1)}, bf16[16,32,128]{2,1,0:T(8,128)(2,1)S(1)}, u32[]{:S(2)}, u32[]{:S(2)}) collective-permute-start(bf16[16,32,128]{2,1,0:T(8,128)(2,1)S(1)} %get-tuple-element.64), channel_id=1, source_target_pairs={{0,8},{1,9},{2,10},{3,11},{4,12},{5,13},{6,14},{7,15},{8,0},{9,1},... | collective-permute-start | bytes 393224 | tf_op jit(solution)/shard_map/ppermute | solution.py:281
  55.7 10.2 %collective-permute-start.10 = (bf16[16,32,128]{2,1,0:T(8,128)(2,1)S(1)}, bf16[16,32,128]{2,1,0:T(8,128)(2,1)S(1)}, u32[]{:S(2)}, u32[]{:S(2)}) collective-permute-start(bf16[16,32,128]{2,1,0:T(8,128)(2,1)S(1)} %get-tuple-element.66), channel_id=1, source_target_pairs={{0,8},{1,9},{2,10},{3,11},{4,12},{5,13},{6,14},{7,15},{8,0},{9,1},... | collective-permute-start | bytes 393224 | tf_op jit(solution)/shard_map/ppermute | solution.py:281
  61.3 10.2 %collective-permute-start.11 = (bf16[16,32,128]{2,1,0:T(8,128)(2,1)S(1)}, bf16[16,32,128]{2,1,0:T(8,128)(2,1)S(1)}, u32[]{:S(2)}, u32[]{:S(2)}) collective-permute-start(bf16[16,32,128]{2,1,0:T(8,128)(2,1)S(1)} %get-tuple-element.68), channel_id=1, source_target_pairs={{0,8},{1,9},{2,10},{3,11},{4,12},{5,13},{6,14},{7,15},{8,0},{9,1},... | collective-permute-start | bytes 393224 | tf_op jit(solution)/shard_map/ppermute | solution.py:281
  67.1 10.2 %collective-permute-start.12 = (bf16[16,32,128]{2,1,0:T(8,128)(2,1)S(1)}, bf16[16,32,128]{2,1,0:T(8,128)(2,1)S(1)}, u32[]{:S(2)}, u32[]{:S(2)}) collective-permute-start(bf16[16,32,128]{2,1,0:T(8,128)(2,1)S(1)} %get-tuple-element.70), channel_id=1, source_target_pairs={{0,8},{1,9},{2,10},{3,11},{4,12},{5,13},{6,14},{7,15},{8,0},{9,1},... | collective-permute-start | bytes 393224 | tf_op jit(solution)/shard_map/ppermute | solution.py:281
  72.5 10.3 %collective-permute-start.13 = (bf16[16,32,128]{2,1,0:T(8,128)(2,1)S(1)}, bf16[16,32,128]{2,1,0:T(8,128)(2,1)S(1)}, u32[]{:S(2)}, u32[]{:S(2)}) collective-permute-start(bf16[16,32,128]{2,1,0:T(8,128)(2,1)S(1)} %get-tuple-element.72), channel_id=1, source_target_pairs={{0,8},{1,9},{2,10},{3,11},{4,12},{5,13},{6,14},{7,15},{8,0},{9,1},... | collective-permute-start | bytes 393224 | tf_op jit(solution)/shard_map/ppermute | solution.py:281
  78.3 8.7 %collective-permute-start.14 = (bf16[16,32,128]{2,1,0:T(8,128)(2,1)S(1)}, bf16[16,32,128]{2,1,0:T(8,128)(2,1)S(1)}, u32[]{:S(2)}, u32[]{:S(2)}) collective-permute-start(bf16[16,32,128]{2,1,0:T(8,128)(2,1)S(1)} %get-tuple-element.74), channel_id=1, source_target_pairs={{0,8},{1,9},{2,10},{3,11},{4,12},{5,13},{6,14},{7,15},{8,0},{9,1},... | collective-permute-start | bytes 393224 | tf_op jit(solution)/shard_map/ppermute | solution.py:281
  88.1 1.4 %collective-permute-start.15 = (bf16[4,8,16,128]{3,2,1,0:T(8,128)(2,1)S(1)}, bf16[4,8,16,128]{3,2,1,0:T(8,128)(2,1)S(1)}, u32[]{:S(2)}, u32[]{:S(2)}) collective-permute-start(bf16[4,8,16,128]{3,2,1,0:T(8,128)(2,1)S(1)} %get-tuple-element.77), channel_id=1, source_target_pairs={{0,1},{1,0},{2,3},{3,2},{4,5},{5,4},{6,7},{7,6},{8,9},{9,8},{10,11... | collective-permute-start | bytes 393224 | tf_op jit(solution)/shard_map/ppermute | solution.py:254
  89.6 4.3 %collective-permute-start.16 = (bf16[2,8,16,128]{3,2,1,0:T(8,128)(2,1)S(1)}, bf16[2,8,16,128]{3,2,1,0:T(8,128)(2,1)S(1)}, u32[]{:S(2)}, u32[]{:S(2)}) collective-permute-start(bf16[2,8,16,128]{3,2,1,0:T(8,128)(2,1)S(1)} %get-tuple-element.79), channel_id=1, source_target_pairs={{0,2},{1,3},{2,0},{3,1},{4,6},{5,7},{6,4},{7,5},{8,10},{9,11},{10,... | collective-permute-start | bytes 196616 | tf_op jit(solution)/shard_map/ppermute | solution.py:254
  94.0 6.4 %collective-permute-start.17 = (bf16[1,8,16,128]{3,2,1,0:T(8,128)(2,1)S(1)}, bf16[1,8,16,128]{3,2,1,0:T(8,128)(2,1)S(1)}, u32[]{:S(2)}, u32[]{:S(2)}) collective-permute-start(bf16[1,8,16,128]{3,2,1,0:T(8,128)(2,1)S(1)} %get-tuple-element.81), channel_id=1, source_target_pairs={{0,4},{1,5},{2,6},{3,7},{4,0},{5,1},{6,2},{7,3},{8,12},{9,13},{10,... | collective-permute-start | bytes 98312 | tf_op jit(solution)/shard_map/ppermute | solution.py:254

commit v3 on v2

--- a/solution.py
+++ b/solution.py
@@ -83,7 +83,7 @@
     for c in loads:
         c.wait()
     fill_blocks(w_ref, pad_ref, reach)
-    sec, me = place_ref[0], place_ref[1]
+    sec, me = place_ref[0][0, 0], place_ref[1][0, 0]
     offs = [off_ref[sec, k] + reach for k in range(band)]
     rows = [asg_ref[sec, j] for j in range(slots)]
     for k, value in enumerate(offs + rows + [me]):
@@ -129,23 +129,26 @@
     )
 
 
-def split_kernel(bit, freqs, code_ref, *refs):
+def pair_kernel(freqs, code_ref, *refs):
     ins, (keep_ref, send_ref) = refs[:-2], refs[-2:]
-    side = (code_ref[code_ref.shape[0] - 1][0, 0] >> bit) & 1
+    side = code_ref[code_ref.shape[0] - 1][0, 0] & 1
     halves, rounds = keep_ref.shape[:2]
     for half in range(halves):
         for out, row in ((keep_ref, 2 * half + side), (send_ref, 2 * half + 1 - side)):
             for r in range(rounds):
-                if bit == 0:
-                    value = ins[r * freqs][row]
-                    for f in range(1, freqs):
-                        value += ins[r * freqs + f][row]
-                else:
-                    value = ins[0][row, r] + ins[1][row, r].astype(jnp.float32)
+                value = ins[r * freqs][row]
+                for f in range(1, freqs):
+                    value += ins[r * freqs + f][row]
                 out[half, r] = value.astype(out.dtype)
 
 
-SMEM = pl.BlockSpec(memory_space=pltpu.SMEM)
+def spread_kernel(code_ref, kept_ref, came_ref, *outs):
+    mine = code_ref[code_ref.shape[0] - 1][0, 0] >> 1
+    for mask, out in enumerate(outs):
+        row = mine ^ mask
+        out[...] = (kept_ref[row] + came_ref[row].astype(jnp.float32)).astype(out.dtype)
+
+
 VMEM = pl.BlockSpec(memory_space=pltpu.VMEM)
 HBM = pl.BlockSpec(memory_space=pltpu.HBM)
 ANY = pl.BlockSpec(memory_space=pl.ANY)
@@ -173,7 +176,7 @@
             pltpu.VMEM((band + slots + 1, 8, BLOCK), jnp.int32),
             pltpu.VMEM(extrap.shape, extrap.dtype),
         ),
-        in_specs=[SMEM, HBM, HBM, HBM, HBM],
+        in_specs=[VMEM, HBM, HBM, HBM, HBM],
         out_specs=(VMEM,) * 4,
         scratch_shapes=[
             pltpu.VMEM((nblk + 2 * (band // 2), rows, BLOCK), jnp.bfloat16),
@@ -186,7 +189,7 @@
         compiler_params=pltpu.CompilerParams(vmem_limit_bytes=4 * 2**20),
         cost_estimate=cost(extrap.shape[1:], rows),
         name="first",
-    )(held(place, pltpu.SMEM), *[held(x, pltpu.HBM) for x in (offsets, assign, extrap, fronts)])
+    )(held(place, pltpu.VMEM), *[held(x, pltpu.HBM) for x in (offsets, assign, extrap, fronts)])
 
 
 def run_next(f, code, e, extrap, fronts, token, scale):
@@ -237,24 +240,34 @@
 def fold_owners(code, parts, rounds, owners):
     size = lax.axis_size("depth")
     rows, nblk, lanes = parts[0].shape
-    freqs = len(parts) // rounds
-    ins, bit = parts, 0
-    while 1 << bit < owners:
-        rows //= 2
-        half = (rows, rounds, nblk, lanes)
-        keep, send = pl.pallas_call(
-            functools.partial(split_kernel, bit, freqs),
-            out_shape=(pltpu.VMEM(half, jnp.float32), pltpu.VMEM(half, jnp.bfloat16)),
-            in_specs=[VMEM] * (1 + len(ins)),
-            out_specs=(VMEM, VMEM),
-            compiler_params=pltpu.CompilerParams(vmem_limit_bytes=4 * 2**20),
-            cost_estimate=pl.CostEstimate(flops=BLOCK, bytes_accessed=BLOCK, transcendentals=0),
-            name="split",
-        )(*[held(x, pltpu.VMEM) for x in (code, *ins)])
-        came = lax.ppermute(send, "depth", [(i, i ^ (1 << bit)) for i in range(size)])
-        ins = (keep, came)
-        bit += 1
-    return ins[0] + ins[1].astype(jnp.float32)
+    left = owners // 2
+    half = (left, rounds, nblk, lanes)
+    small = pl.CostEstimate(flops=BLOCK, bytes_accessed=BLOCK, transcendentals=0)
+    keep, send = pl.pallas_call(
+        functools.partial(pair_kernel, len(parts) // rounds),
+        out_shape=(pltpu.VMEM(half, jnp.float32), pltpu.VMEM(half, jnp.bfloat16)),
+        in_specs=[VMEM] * (1 + len(parts)),
+        out_specs=(VMEM, VMEM),
+        compiler_params=pltpu.CompilerParams(vmem_limit_bytes=4 * 2**20),
+        cost_estimate=small,
+        name="pair",
+    )(*[held(x, pltpu.VMEM) for x in (code, *parts)])
+    came = lax.ppermute(send, "depth", [(i, i ^ 1) for i in range(size)])
+    own, *others = pl.pallas_call(
+        spread_kernel,
+        out_shape=tuple(
+            pltpu.VMEM(half[1:], jnp.bfloat16 if mask else jnp.float32) for mask in range(left)
+        ),
+        in_specs=[VMEM] * 3,
+        out_specs=(VMEM,) * left,
+        compiler_params=pltpu.CompilerParams(vmem_limit_bytes=4 * 2**20),
+        cost_estimate=small,
+        name="spread",
+    )(*[held(x, pltpu.VMEM) for x in (code, keep, came)])
+    for mask, other in enumerate(others, 1):
+        other = lax.ppermute(other, "depth", [(i, i ^ (2 * mask)) for i in range(size)])
+        own = own + other.astype(jnp.float32)
+    return own
 
 
 def on_device(fronts, extrap, offsets, assign):
@@ -263,6 +276,7 @@
     owners = size // sections
     index = lax.axis_index("depth")
     place = jnp.stack([lax.div(index, owners), lax.rem(index, owners)]).astype(jnp.int32)
+    place = jnp.broadcast_to(place[:, None, None], (2, 8, BLOCK))
     nfield, freqs, slots, points = fronts.shape
     nblk = extrap.shape[1]
     scale = 1.0 / math.sqrt(2.0 * owners * freqs)

time: 101 us -> 101 us (level)
    ppermute x3 -> x4, waiting for transfers between devices: 5.26 us -> 5.42 us  [the longest x3 4.09 us: fold_owners(): lax.ppermute(other, 'depth', [(i, i ^ 2 * mask) for i in range(size)])]
    ppermute x3 -> x4, starting transfers between devices: 6.18 us -> 6.11 us  [the longest x3 6.04 us: fold_owners(): lax.ppermute(other, 'depth', [(i, i ^ 2 * mask) for i in range(size)])]
  transfers between devices with their start and end apart: 18 -> 19, of which waited for: 17 -> 17; matrix products, arithmetic and copies ran while one was open for 1% -> 1% of each run, Pallas kernels for 16% -> 16%
where the time goes in v3:
time: 101 us
  waiting for transfers between devices  63.3 us (63%)
  Pallas kernels  20.7 us (20%)
  starting transfers between devices  14.2 us (14%)
  other arithmetic  1.44 us (1%)
    ppermute x14, waiting for transfers between devices, on_device(): waves[f] = lax.ppermute(adv, 'depth', onward) if r + 1 < HANDOVERS else adv  57.9 us
    pallas_call x14, Pallas kernels, run_step(): pl.pallas_call(functools.partial(step_kernel, scale, f), out_shape=(pltpu...  14 us
    ppermute x14, starting transfers between devices, on_device(): waves[f] = lax.ppermute(adv, 'depth', onward) if r + 1 < HANDOVERS else adv  7.62 us
    ppermute x3, starting transfers between devices, fold_owners(): lax.ppermute(other, 'depth', [(i, i ^ 2 * mask) for i in range(size)])  6.04 us
    ppermute x3, waiting for transfers between devices, fold_owners(): lax.ppermute(other, 'depth', [(i, i ^ 2 * mask) for i in range(size)])  4.09 us
    pallas_call x1, Pallas kernels, run_next(): pl.pallas_call(functools.partial(next_kernel, scale, f), out_shape=(pltpu...  3.57 us
    pallas_call x1, Pallas kernels, run_first(): pl.pallas_call(functools.partial(first_kernel, scale), out_shape=(pltpu.V...  2.95 us
  transfers between devices with their start and end apart: 19, of which 17 were waited for; matrix products, arithmetic and copies ran while one was open for 1% of the time, Pallas kernels for 16%

profile of v3, /device:TPU:0, one launch (start us, length us, event | category | flops | bytes accessed | tf_op | source)
XLA Modules:
  0.0 100.7 jit_solution(14768162253897883682)
XLA Ops:
  0.8 3.0 %first.1 = (bf16[16,32,128]{2,1,0:T(8,128)(2,1)S(1)}, f32[8,16,128]{2,1,0:T(8,128)S(1)}, s32[14,8,128]{2,1,0:T(8,128)S(1)}, bf16[2,16,5,2,128,128]{5,4,3,2,1,0:T(8,128)(2,1)S(1)}) custom-call(s32[2,8,128]{2,1,0:T(8,128)S(1)} %broadcast_in_dim.2.place_ref, s32[2,5]{1,0:T(2,128)} %offs_hbm.1, s32[2,8]{1,0:T(2,128)} %asgs_hbm.1, ...), custom_call_target="tpu_custom_call" | custom-call | flops 167772160 | bytes 128 | tf_op jit(solution)/shard_map/first/pallas_call | solution.py:171
  4.3 3.7 %collective-permute-start.1 = (bf16[16,32,128]{2,1,0:T(8,128)(2,1)S(1)}, bf16[16,32,128]{2,1,0:T(8,128)(2,1)S(1)}, u32[]{:S(2)}, u32[]{:S(2)}) collective-permute-start(bf16[16,32,128]{2,1,0:T(8,128)(2,1)S(1)} %get-tuple-element.48), channel_id=1, source_target_pairs={{0,8},{1,9},{2,10},{3,11},{4,12},{5,13},{6,14},{7,15},{8,0},{9,1},... | collective-permute-start | bytes 393224 | tf_op jit(solution)/shard_map/ppermute | solution.py:295
  7.9 3.6 %next.1 = (bf16[16,32,128]{2,1,0:T(8,128)(2,1)S(1)}, f32[8,16,128]{2,1,0:T(8,128)S(1)}, bf16[2,16,5,2,128,128]{5,4,3,2,1,0:T(8,128)(2,1)S(1)}) custom-call(s32[14,8,128]{2,1,0:T(8,128)S(1)} %get-tuple-element.43.code_ref, bf16[2,16,5,2,128,128]{5,4,3,2,1,0:T(8,128)(2,1)S(1)} %get-tuple-element.45.old, ...), custom_call_target="tpu_custom_call", output_to_operand_aliasing={{2}: (1, {})} | custom-call | flops 167772160 | bytes 128 | tf_op jit(solution)/shard_map/next/pallas_call | solution.py:200
  11.5 1.2 %collective-permute-start.2 = (bf16[16,32,128]{2,1,0:T(8,128)(2,1)S(1)}, bf16[16,32,128]{2,1,0:T(8,128)(2,1)S(1)}, u32[]{:S(2)}, u32[]{:S(2)}) collective-permute-start(bf16[16,32,128]{2,1,0:T(8,128)(2,1)S(1)} %get-tuple-element.50), channel_id=1, source_target_pairs={{0,8},{1,9},{2,10},{3,11},{4,12},{5,13},{6,14},{7,15},{8,0},{9,1},... | collective-permute-start | bytes 393224 | tf_op jit(solution)/shard_map/ppermute | solution.py:295
  12.7 2.2 %collective-permute-done.1.w_ref = bf16[16,32,128]{2,1,0:T(8,128)(2,1)S(1)} collective-permute-done((bf16[16,32,128]{2,1,0:T(8,128)(2,1)S(1)}, bf16[16,32,128]{2,1,0:T(8,128)(2,1)S(1)}, u32[]{:S(2)}, u32[]{:S(2)}) %collective-permute-start.1) | collective-permute-done | bytes 131104 | tf_op jit(solution)/shard_map/ppermute | solution.py:295
  14.8 1.0 step.14
  15.9 5.7 %collective-permute-done.2.w_ref = bf16[16,32,128]{2,1,0:T(8,128)(2,1)S(1)} collective-permute-done((bf16[16,32,128]{2,1,0:T(8,128)(2,1)S(1)}, bf16[16,32,128]{2,1,0:T(8,128)(2,1)S(1)}, u32[]{:S(2)}, u32[]{:S(2)}) %collective-permute-start.2) | collective-permute-done | bytes 131104 | tf_op jit(solution)/shard_map/ppermute | solution.py:295
  23.7 1.0 step.16
  24.7 2.0 %collective-permute-start.5 = (bf16[16,32,128]{2,1,0:T(8,128)(2,1)S(1)}, bf16[16,32,128]{2,1,0:T(8,128)(2,1)S(1)}, u32[]{:S(2)}, u32[]{:S(2)}) collective-permute-start(bf16[16,32,128]{2,1,0:T(8,128)(2,1)S(1)} %get-tuple-element.56), channel_id=1, source_target_pairs={{0,8},{1,9},{2,10},{3,11},{4,12},{5,13},{6,14},{7,15},{8,0},{9,1},... | collective-permute-start | bytes 393224 | tf_op jit(solution)/shard_map/ppermute | solution.py:295
  26.7 5.1 %collective-permute-done.4.w_ref = bf16[16,32,128]{2,1,0:T(8,128)(2,1)S(1)} collective-permute-done((bf16[16,32,128]{2,1,0:T(8,128)(2,1)S(1)}, bf16[16,32,128]{2,1,0:T(8,128)(2,1)S(1)}, u32[]{:S(2)}, u32[]{:S(2)}) %collective-permute-start.4) | collective-permute-done | bytes 131104 | tf_op jit(solution)/shard_map/ppermute | solution.py:295
  31.8 1.0 step.17
  32.8 3.1 %collective-permute-done.5.w_ref = bf16[16,32,128]{2,1,0:T(8,128)(2,1)S(1)} collective-permute-done((bf16[16,32,128]{2,1,0:T(8,128)(2,1)S(1)}, bf16[16,32,128]{2,1,0:T(8,128)(2,1)S(1)}, u32[]{:S(2)}, u32[]{:S(2)}) %collective-permute-start.5) | collective-permute-done | bytes 131104 | tf_op jit(solution)/shard_map/ppermute | solution.py:295
  36.0 1.0 step.18
  37.0 5.9 %collective-permute-done.6.w_ref = bf16[16,32,128]{2,1,0:T(8,128)(2,1)S(1)} collective-permute-done((bf16[16,32,128]{2,1,0:T(8,128)(2,1)S(1)}, bf16[16,32,128]{2,1,0:T(8,128)(2,1)S(1)}, u32[]{:S(2)}, u32[]{:S(2)}) %collective-permute-start.6) | collective-permute-done | bytes 131104 | tf_op jit(solution)/shard_map/ppermute | solution.py:295
  43.0 1.0 step.19
  44.0 4.5 %collective-permute-done.7.w_ref = bf16[16,32,128]{2,1,0:T(8,128)(2,1)S(1)} collective-permute-done((bf16[16,32,128]{2,1,0:T(8,128)(2,1)S(1)}, bf16[16,32,128]{2,1,0:T(8,128)(2,1)S(1)}, u32[]{:S(2)}, u32[]{:S(2)}) %collective-permute-start.7) | collective-permute-done | bytes 131104 | tf_op jit(solution)/shard_map/ppermute | solution.py:295
  49.7 4.5 %collective-permute-done.8.w_ref = bf16[16,32,128]{2,1,0:T(8,128)(2,1)S(1)} collective-permute-done((bf16[16,32,128]{2,1,0:T(8,128)(2,1)S(1)}, bf16[16,32,128]{2,1,0:T(8,128)(2,1)S(1)}, u32[]{:S(2)}, u32[]{:S(2)}) %collective-permute-start.8) | collective-permute-done | bytes 131104 | tf_op jit(solution)/shard_map/ppermute | solution.py:295
  55.3 4.5 %collective-permute-done.9.w_ref = bf16[16,32,128]{2,1,0:T(8,128)(2,1)S(1)} collective-permute-done((bf16[16,32,128]{2,1,0:T(8,128)(2,1)S(1)}, bf16[16,32,128]{2,1,0:T(8,128)(2,1)S(1)}, u32[]{:S(2)}, u32[]{:S(2)}) %collective-permute-start.9) | collective-permute-done | bytes 131104 | tf_op jit(solution)/shard_map/ppermute | solution.py:295
  59.8 1.0 step.22
  60.9 4.5 %collective-permute-done.10.w_ref = bf16[16,32,128]{2,1,0:T(8,128)(2,1)S(1)} collective-permute-done((bf16[16,32,128]{2,1,0:T(8,128)(2,1)S(1)}, bf16[16,32,128]{2,1,0:T(8,128)(2,1)S(1)}, u32[]{:S(2)}, u32[]{:S(2)}) %collective-permute-start.10) | collective-permute-done | bytes 131104 | tf_op jit(solution)/shard_map/ppermute | solution.py:295
  65.4 1.2 %step.23 = (bf16[16,32,128]{2,1,0:T(8,128)(2,1)S(1)}, f32[8,16,128]{2,1,0:T(8,128)S(1)}) custom-call(s32[14,8,128]{2,1,0:T(8,128)S(1)} %get-tuple-element.43.code_ref, bf16[2,16,5,2,128,128]{5,4,3,2,1,0:T(8,128)(2,1)S(1)} %get-tuple-element.47.e_ref, bf16[16,32,128]{2,1,0:T(8,128)(2,1)S(1)} %collective-permute-done.10.w_ref), custom_call_target="tpu_custom_call" | custom-call | flops 167772160 | bytes 128 | tf_op jit(solution)/shard_map/step/pallas_call | solution.py:225
  66.7 4.4 %collective-permute-done.11.w_ref = bf16[16,32,128]{2,1,0:T(8,128)(2,1)S(1)} collective-permute-done((bf16[16,32,128]{2,1,0:T(8,128)(2,1)S(1)}, bf16[16,32,128]{2,1,0:T(8,128)(2,1)S(1)}, u32[]{:S(2)}, u32[]{:S(2)}) %collective-permute-start.11) | collective-permute-done | bytes 131104 | tf_op jit(solution)/shard_map/ppermute | solution.py:295
  71.1 1.0 step.24
  72.1 4.7 %collective-permute-done.12.w_ref = bf16[16,32,128]{2,1,0:T(8,128)(2,1)S(1)} collective-permute-done((bf16[16,32,128]{2,1,0:T(8,128)(2,1)S(1)}, bf16[16,32,128]{2,1,0:T(8,128)(2,1)S(1)}, u32[]{:S(2)}, u32[]{:S(2)}) %collective-permute-start.12) | collective-permute-done | bytes 131104 | tf_op jit(solution)/shard_map/ppermute | solution.py:295
  77.9 4.4 %collective-permute-done.13.w_ref = bf16[16,32,128]{2,1,0:T(8,128)(2,1)S(1)} collective-permute-done((bf16[16,32,128]{2,1,0:T(8,128)(2,1)S(1)}, bf16[16,32,128]{2,1,0:T(8,128)(2,1)S(1)}, u32[]{:S(2)}, u32[]{:S(2)}) %collective-permute-start.13) | collective-permute-done | bytes 131104 | tf_op jit(solution)/shard_map/ppermute | solution.py:295
  82.3 1.0 step.26
  83.3 3.2 %collective-permute-done.14.w_ref = bf16[16,32,128]{2,1,0:T(8,128)(2,1)S(1)} collective-permute-done((bf16[16,32,128]{2,1,0:T(8,128)(2,1)S(1)}, bf16[16,32,128]{2,1,0:T(8,128)(2,1)S(1)}, u32[]{:S(2)}, u32[]{:S(2)}) %collective-permute-start.14) | collective-permute-done | bytes 131104 | tf_op jit(solution)/shard_map/ppermute | solution.py:295
  87.8 1.3 %collective-permute-done.15.came_ref = bf16[4,8,16,128]{3,2,1,0:T(8,128)(2,1)S(1)} collective-permute-done((bf16[4,8,16,128]{3,2,1,0:T(8,128)(2,1)S(1)}, bf16[4,8,16,128]{3,2,1,0:T(8,128)(2,1)S(1)}, u32[]{:S(2)}, u32[]{:S(2)}) %collective-permute-start.15) | collective-permute-done | bytes 131104 | tf_op jit(solution)/shard_map/ppermute | solution.py:255
  89.2 1.6 %collective-permute-start.16 = (bf16[8,16,128]{2,1,0:T(8,128)(2,1)S(1)}, bf16[8,16,128]{2,1,0:T(8,128)(2,1)S(1)}, u32[]{:S(2)}, u32[]{:S(2)}) collective-permute-start(bf16[8,16,128]{2,1,0:T(8,128)(2,1)S(1)} %get-tuple-element.79), channel_id=1, source_target_pairs={{0,2},{1,3},{2,0},{3,1},{4,6},{5,7},{6,4},{7,5},{8,10},{9,11},{10,... | collective-permute-start | bytes 98312 | tf_op jit(solution)/shard_map/ppermute | solution.py:268
  90.7 4.5 %collective-permute-start.17 = (bf16[8,16,128]{2,1,0:T(8,128)(2,1)S(1)}, bf16[8,16,128]{2,1,0:T(8,128)(2,1)S(1)}, u32[]{:S(2)}, u32[]{:S(2)}) collective-permute-start(bf16[8,16,128]{2,1,0:T(8,128)(2,1)S(1)} %get-tuple-element.80), channel_id=1, source_target_pairs={{0,4},{1,5},{2,6},{3,7},{4,0},{5,1},{6,2},{7,3},{8,12},{9,13},{10,... | collective-permute-start | bytes 98312 | tf_op jit(solution)/shard_map/ppermute | solution.py:268
  95.9 1.2 %collective-permute-done.17 = bf16[8,16,128]{2,1,0:T(8,128)(2,1)S(1)} collective-permute-done((bf16[8,16,128]{2,1,0:T(8,128)(2,1)S(1)}, bf16[8,16,128]{2,1,0:T(8,128)(2,1)S(1)}, u32[]{:S(2)}, u32[]{:S(2)}) %collective-permute-start.17) | collective-permute-done | bytes 32800 | tf_op jit(solution)/shard_map/ppermute | solution.py:268
  97.1 2.9 %collective-permute-done.18 = bf16[8,16,128]{2,1,0:T(8,128)(2,1)S(1)} collective-permute-done((bf16[8,16,128]{2,1,0:T(8,128)(2,1)S(1)}, bf16[8,16,128]{2,1,0:T(8,128)(2,1)S(1)}, u32[]{:S(2)}, u32[]{:S(2)}) %collective-permute-start.18) | collective-permute-done | bytes 32800 | tf_op jit(solution)/shard_map/ppermute | solution.py:268
  (29 shorter events, 9.0 us)
Async XLA Ops:
  3.8 4.2 %collective-permute-start = (f32[1,16,128]{2,1,0:T(8,128)S(1)}, f32[1,16,128]{2,1,0:T(8,128)S(1)}, u32[]{:S(2)}, u32[]{:S(2)}) collective-permute-start(f32[1,16,128]{2,1,0:T(8,128)S(1)} %slice.3), channel_id=1, source_target_pairs={{0,1},{1,0},{2,3},{3,2},{4,5},{5,4},{6,7},{7,6},{8,9},{9,8},{10,11... | collective-permute-start | bytes 24584 | tf_op jit(solution)/shard_map/ppermute | solution.py:289
  4.3 10.6 %collective-permute-start.1 = (bf16[16,32,128]{2,1,0:T(8,128)(2,1)S(1)}, bf16[16,32,128]{2,1,0:T(8,128)(2,1)S(1)}, u32[]{:S(2)}, u32[]{:S(2)}) collective-permute-start(bf16[16,32,128]{2,1,0:T(8,128)(2,1)S(1)} %get-tuple-element.48), channel_id=1, source_target_pairs={{0,8},{1,9},{2,10},{3,11},{4,12},{5,13},{6,14},{7,15},{8,0},{9,1},... | collective-permute-start | bytes 393224 | tf_op jit(solution)/shard_map/ppermute | solution.py:295
  11.5 10.1 %collective-permute-start.2 = (bf16[16,32,128]{2,1,0:T(8,128)(2,1)S(1)}, bf16[16,32,128]{2,1,0:T(8,128)(2,1)S(1)}, u32[]{:S(2)}, u32[]{:S(2)}) collective-permute-start(bf16[16,32,128]{2,1,0:T(8,128)(2,1)S(1)} %get-tuple-element.50), channel_id=1, source_target_pairs={{0,8},{1,9},{2,10},{3,11},{4,12},{5,13},{6,14},{7,15},{8,0},{9,1},... | collective-permute-start | bytes 393224 | tf_op jit(solution)/shard_map/ppermute | solution.py:295
  15.8 7.8 %collective-permute-start.3 = (bf16[16,32,128]{2,1,0:T(8,128)(2,1)S(1)}, bf16[16,32,128]{2,1,0:T(8,128)(2,1)S(1)}, u32[]{:S(2)}, u32[]{:S(2)}) collective-permute-start(bf16[16,32,128]{2,1,0:T(8,128)(2,1)S(1)} %get-tuple-element.52), channel_id=1, source_target_pairs={{0,8},{1,9},{2,10},{3,11},{4,12},{5,13},{6,14},{7,15},{8,0},{9,1},... | collective-permute-start | bytes 393224 | tf_op jit(solution)/shard_map/ppermute | solution.py:295
  22.6 9.1 %collective-permute-start.4 = (bf16[16,32,128]{2,1,0:T(8,128)(2,1)S(1)}, bf16[16,32,128]{2,1,0:T(8,128)(2,1)S(1)}, u32[]{:S(2)}, u32[]{:S(2)}) collective-permute-start(bf16[16,32,128]{2,1,0:T(8,128)(2,1)S(1)} %get-tuple-element.54), channel_id=1, source_target_pairs={{0,8},{1,9},{2,10},{3,11},{4,12},{5,13},{6,14},{7,15},{8,0},{9,1},... | collective-permute-start | bytes 393224 | tf_op jit(solution)/shard_map/ppermute | solution.py:295
  24.7 11.3 %collective-permute-start.5 = (bf16[16,32,128]{2,1,0:T(8,128)(2,1)S(1)}, bf16[16,32,128]{2,1,0:T(8,128)(2,1)S(1)}, u32[]{:S(2)}, u32[]{:S(2)}) collective-permute-start(bf16[16,32,128]{2,1,0:T(8,128)(2,1)S(1)} %get-tuple-element.56), channel_id=1, source_target_pairs={{0,8},{1,9},{2,10},{3,11},{4,12},{5,13},{6,14},{7,15},{8,0},{9,1},... | collective-permute-start | bytes 393224 | tf_op jit(solution)/shard_map/ppermute | solution.py:295
  32.8 10.2 %collective-permute-start.6 = (bf16[16,32,128]{2,1,0:T(8,128)(2,1)S(1)}, bf16[16,32,128]{2,1,0:T(8,128)(2,1)S(1)}, u32[]{:S(2)}, u32[]{:S(2)}) collective-permute-start(bf16[16,32,128]{2,1,0:T(8,128)(2,1)S(1)} %get-tuple-element.58), channel_id=1, source_target_pairs={{0,8},{1,9},{2,10},{3,11},{4,12},{5,13},{6,14},{7,15},{8,0},{9,1},... | collective-permute-start | bytes 393224 | tf_op jit(solution)/shard_map/ppermute | solution.py:295
  37.0 11.6 %collective-permute-start.7 = (bf16[16,32,128]{2,1,0:T(8,128)(2,1)S(1)}, bf16[16,32,128]{2,1,0:T(8,128)(2,1)S(1)}, u32[]{:S(2)}, u32[]{:S(2)}) collective-permute-start(bf16[16,32,128]{2,1,0:T(8,128)(2,1)S(1)} %get-tuple-element.60), channel_id=1, source_target_pairs={{0,8},{1,9},{2,10},{3,11},{4,12},{5,13},{6,14},{7,15},{8,0},{9,1},... | collective-permute-start | bytes 393224 | tf_op jit(solution)/shard_map/ppermute | solution.py:295
  44.0 10.2 %collective-permute-start.8 = (bf16[16,32,128]{2,1,0:T(8,128)(2,1)S(1)}, bf16[16,32,128]{2,1,0:T(8,128)(2,1)S(1)}, u32[]{:S(2)}, u32[]{:S(2)}) collective-permute-start(bf16[16,32,128]{2,1,0:T(8,128)(2,1)S(1)} %get-tuple-element.62), channel_id=1, source_target_pairs={{0,8},{1,9},{2,10},{3,11},{4,12},{5,13},{6,14},{7,15},{8,0},{9,1},... | collective-permute-start | bytes 393224 | tf_op jit(solution)/shard_map/ppermute | solution.py:295
  49.6 10.2 %collective-permute-start.9 = (bf16[16,32,128]{2,1,0:T(8,128)(2,1)S(1)}, bf16[16,32,128]{2,1,0:T(8,128)(2,1)S(1)}, u32[]{:S(2)}, u32[]{:S(2)}) collective-permute-start(bf16[16,32,128]{2,1,0:T(8,128)(2,1)S(1)} %get-tuple-element.64), channel_id=1, source_target_pairs={{0,8},{1,9},{2,10},{3,11},{4,12},{5,13},{6,14},{7,15},{8,0},{9,1},... | collective-permute-start | bytes 393224 | tf_op jit(solution)/shard_map/ppermute | solution.py:295
  55.2 10.2 %collective-permute-start.10 = (bf16[16,32,128]{2,1,0:T(8,128)(2,1)S(1)}, bf16[16,32,128]{2,1,0:T(8,128)(2,1)S(1)}, u32[]{:S(2)}, u32[]{:S(2)}) collective-permute-start(bf16[16,32,128]{2,1,0:T(8,128)(2,1)S(1)} %get-tuple-element.66), channel_id=1, source_target_pairs={{0,8},{1,9},{2,10},{3,11},{4,12},{5,13},{6,14},{7,15},{8,0},{9,1},... | collective-permute-start | bytes 393224 | tf_op jit(solution)/shard_map/ppermute | solution.py:295
  60.8 10.2 %collective-permute-start.11 = (bf16[16,32,128]{2,1,0:T(8,128)(2,1)S(1)}, bf16[16,32,128]{2,1,0:T(8,128)(2,1)S(1)}, u32[]{:S(2)}, u32[]{:S(2)}) collective-permute-start(bf16[16,32,128]{2,1,0:T(8,128)(2,1)S(1)} %get-tuple-element.68), channel_id=1, source_target_pairs={{0,8},{1,9},{2,10},{3,11},{4,12},{5,13},{6,14},{7,15},{8,0},{9,1},... | collective-permute-start | bytes 393224 | tf_op jit(solution)/shard_map/ppermute | solution.py:295
  66.6 10.2 %collective-permute-start.12 = (bf16[16,32,128]{2,1,0:T(8,128)(2,1)S(1)}, bf16[16,32,128]{2,1,0:T(8,128)(2,1)S(1)}, u32[]{:S(2)}, u32[]{:S(2)}) collective-permute-start(bf16[16,32,128]{2,1,0:T(8,128)(2,1)S(1)} %get-tuple-element.70), channel_id=1, source_target_pairs={{0,8},{1,9},{2,10},{3,11},{4,12},{5,13},{6,14},{7,15},{8,0},{9,1},... | collective-permute-start | bytes 393224 | tf_op jit(solution)/shard_map/ppermute | solution.py:295
  72.0 10.3 %collective-permute-start.13 = (bf16[16,32,128]{2,1,0:T(8,128)(2,1)S(1)}, bf16[16,32,128]{2,1,0:T(8,128)(2,1)S(1)}, u32[]{:S(2)}, u32[]{:S(2)}) collective-permute-start(bf16[16,32,128]{2,1,0:T(8,128)(2,1)S(1)} %get-tuple-element.72), channel_id=1, source_target_pairs={{0,8},{1,9},{2,10},{3,11},{4,12},{5,13},{6,14},{7,15},{8,0},{9,1},... | collective-permute-start | bytes 393224 | tf_op jit(solution)/shard_map/ppermute | solution.py:295
  77.8 8.7 %collective-permute-start.14 = (bf16[16,32,128]{2,1,0:T(8,128)(2,1)S(1)}, bf16[16,32,128]{2,1,0:T(8,128)(2,1)S(1)}, u32[]{:S(2)}, u32[]{:S(2)}) collective-permute-start(bf16[16,32,128]{2,1,0:T(8,128)(2,1)S(1)} %get-tuple-element.74), channel_id=1, source_target_pairs={{0,8},{1,9},{2,10},{3,11},{4,12},{5,13},{6,14},{7,15},{8,0},{9,1},... | collective-permute-start | bytes 393224 | tf_op jit(solution)/shard_map/ppermute | solution.py:295
  87.7 1.4 %collective-permute-start.15 = (bf16[4,8,16,128]{3,2,1,0:T(8,128)(2,1)S(1)}, bf16[4,8,16,128]{3,2,1,0:T(8,128)(2,1)S(1)}, u32[]{:S(2)}, u32[]{:S(2)}) collective-permute-start(bf16[4,8,16,128]{3,2,1,0:T(8,128)(2,1)S(1)} %get-tuple-element.77), channel_id=1, source_target_pairs={{0,1},{1,0},{2,3},{3,2},{4,5},{5,4},{6,7},{7,6},{8,9},{9,8},{10,11... | collective-permute-start | bytes 393224 | tf_op jit(solution)/shard_map/ppermute | solution.py:255
  89.2 6.8 %collective-permute-start.16 = (bf16[8,16,128]{2,1,0:T(8,128)(2,1)S(1)}, bf16[8,16,128]{2,1,0:T(8,128)(2,1)S(1)}, u32[]{:S(2)}, u32[]{:S(2)}) collective-permute-start(bf16[8,16,128]{2,1,0:T(8,128)(2,1)S(1)} %get-tuple-element.79), channel_id=1, source_target_pairs={{0,2},{1,3},{2,0},{3,1},{4,6},{5,7},{6,4},{7,5},{8,10},{9,11},{10,... | collective-permute-start | bytes 98312 | tf_op jit(solution)/shard_map/ppermute | solution.py:268
  90.7 6.3 %collective-permute-start.17 = (bf16[8,16,128]{2,1,0:T(8,128)(2,1)S(1)}, bf16[8,16,128]{2,1,0:T(8,128)(2,1)S(1)}, u32[]{:S(2)}, u32[]{:S(2)}) collective-permute-start(bf16[8,16,128]{2,1,0:T(8,128)(2,1)S(1)} %get-tuple-element.80), channel_id=1, source_target_pairs={{0,4},{1,5},{2,6},{3,7},{4,0},{5,1},{6,2},{7,3},{8,12},{9,13},{10,... | collective-permute-start | bytes 98312 | tf_op jit(solution)/shard_map/ppermute | solution.py:268
  95.2 4.8 %collective-permute-start.18 = (bf16[8,16,128]{2,1,0:T(8,128)(2,1)S(1)}, bf16[8,16,128]{2,1,0:T(8,128)(2,1)S(1)}, u32[]{:S(2)}, u32[]{:S(2)}) collective-permute-start(bf16[8,16,128]{2,1,0:T(8,128)(2,1)S(1)} %get-tuple-element.81), channel_id=1, source_target_pairs={{0,6},{1,7},{2,4},{3,5},{4,2},{5,3},{6,0},{7,1},{8,14},{9,15},{10,... | collective-permute-start | bytes 98312 | tf_op jit(solution)/shard_map/ppermute | solution.py:268

commit v4 on v3

--- a/solution.py
+++ b/solution.py
@@ -10,6 +10,7 @@
 
 BLOCK = 128
 HANDOVERS = 8
+ORDER = (3, 2, 1)
 PARTS = 4
 
 
@@ -264,8 +265,8 @@
         cost_estimate=small,
         name="spread",
     )(*[held(x, pltpu.VMEM) for x in (code, keep, came)])
-    for mask, other in enumerate(others, 1):
-        other = lax.ppermute(other, "depth", [(i, i ^ (2 * mask)) for i in range(size)])
+    for mask in ORDER:
+        other = lax.ppermute(others[mask - 1], "depth", [(i, i ^ (2 * mask)) for i in range(size)])
         own = own + other.astype(jnp.float32)
     return own
 

time: 101 us -> 99.3 us (0.983)
  waiting for transfers between devices: 63.3 us -> 61.8 us
    ppermute x3, waiting for transfers between devices: 4.09 us -> 2.55 us  [fold_owners(): lax.ppermute(others[mask - 1], 'depth', [(i, i ^ 2 * mask) for i in range...]
  transfers between devices with their start and end apart: 19 -> 19, of which waited for: 17 -> 17; matrix products, arithmetic and copies ran while one was open for 1% -> 1% of each run, Pallas kernels for 16% -> 17%
where the time goes in v4:
time: 99.3 us; the launch traced here: 99.2 us
  waiting for transfers between devices  61.8 us (62%)
  Pallas kernels  20.7 us (21%)
  starting transfers between devices  14.3 us (14%)
  other arithmetic  1.44 us (1%)
    ppermute x14, waiting for transfers between devices, on_device(): waves[f] = lax.ppermute(adv, 'depth', onward) if r + 1 < HANDOVERS else adv  57.9 us
    pallas_call x14, Pallas kernels, run_step(): pl.pallas_call(functools.partial(step_kernel, scale, f), out_shape=(pltpu...  14 us
    ppermute x14, starting transfers between devices, on_device(): waves[f] = lax.ppermute(adv, 'depth', onward) if r + 1 < HANDOVERS else adv  7.61 us
    ppermute x3, starting transfers between devices, fold_owners(): lax.ppermute(others[mask - 1], 'depth', [(i, i ^ 2 * mask) for i in range...  6.12 us
    pallas_call x1, Pallas kernels, run_next(): pl.pallas_call(functools.partial(next_kernel, scale, f), out_shape=(pltpu...  3.57 us
    pallas_call x1, Pallas kernels, run_first(): pl.pallas_call(functools.partial(first_kernel, scale), out_shape=(pltpu.V...  2.95 us
    ppermute x3, waiting for transfers between devices, fold_owners(): lax.ppermute(others[mask - 1], 'depth', [(i, i ^ 2 * mask) for i in range...  2.55 us
  transfers between devices with their start and end apart: 19, of which 17 were waited for; matrix products, arithmetic and copies ran while one was open for 1% of the time, Pallas kernels for 17%

profile of v4, /device:TPU:0, one launch (start us, length us, event | category | flops | bytes accessed | tf_op | source)
XLA Modules:
  0.0 99.2 jit_solution(4952544104805972028)
XLA Ops:
  0.8 3.0 %first.1 = (bf16[16,32,128]{2,1,0:T(8,128)(2,1)S(1)}, f32[8,16,128]{2,1,0:T(8,128)S(1)}, s32[14,8,128]{2,1,0:T(8,128)S(1)}, bf16[2,16,5,2,128,128]{5,4,3,2,1,0:T(8,128)(2,1)S(1)}) custom-call(s32[2,8,128]{2,1,0:T(8,128)S(1)} %broadcast_in_dim.2.place_ref, s32[2,5]{1,0:T(2,128)} %offs_hbm.1, s32[2,8]{1,0:T(2,128)} %asgs_hbm.1, ...), custom_call_target="tpu_custom_call" | custom-call | flops 167772160 | bytes 128 | tf_op jit(solution)/shard_map/first/pallas_call | solution.py:172
  4.3 3.7 %collective-permute-start.1 = (bf16[16,32,128]{2,1,0:T(8,128)(2,1)S(1)}, bf16[16,32,128]{2,1,0:T(8,128)(2,1)S(1)}, u32[]{:S(2)}, u32[]{:S(2)}) collective-permute-start(bf16[16,32,128]{2,1,0:T(8,128)(2,1)S(1)} %get-tuple-element.48), channel_id=1, source_target_pairs={{0,8},{1,9},{2,10},{3,11},{4,12},{5,13},{6,14},{7,15},{8,0},{9,1},... | collective-permute-start | bytes 393224 | tf_op jit(solution)/shard_map/ppermute | solution.py:296
  7.9 3.6 %next.1 = (bf16[16,32,128]{2,1,0:T(8,128)(2,1)S(1)}, f32[8,16,128]{2,1,0:T(8,128)S(1)}, bf16[2,16,5,2,128,128]{5,4,3,2,1,0:T(8,128)(2,1)S(1)}) custom-call(s32[14,8,128]{2,1,0:T(8,128)S(1)} %get-tuple-element.43.code_ref, bf16[2,16,5,2,128,128]{5,4,3,2,1,0:T(8,128)(2,1)S(1)} %get-tuple-element.45.old, ...), custom_call_target="tpu_custom_call", output_to_operand_aliasing={{2}: (1, {})} | custom-call | flops 167772160 | bytes 128 | tf_op jit(solution)/shard_map/next/pallas_call | solution.py:201
  11.5 1.2 %collective-permute-start.2 = (bf16[16,32,128]{2,1,0:T(8,128)(2,1)S(1)}, bf16[16,32,128]{2,1,0:T(8,128)(2,1)S(1)}, u32[]{:S(2)}, u32[]{:S(2)}) collective-permute-start(bf16[16,32,128]{2,1,0:T(8,128)(2,1)S(1)} %get-tuple-element.50), channel_id=1, source_target_pairs={{0,8},{1,9},{2,10},{3,11},{4,12},{5,13},{6,14},{7,15},{8,0},{9,1},... | collective-permute-start | bytes 393224 | tf_op jit(solution)/shard_map/ppermute | solution.py:296
  12.7 2.2 %collective-permute-done.1.w_ref = bf16[16,32,128]{2,1,0:T(8,128)(2,1)S(1)} collective-permute-done((bf16[16,32,128]{2,1,0:T(8,128)(2,1)S(1)}, bf16[16,32,128]{2,1,0:T(8,128)(2,1)S(1)}, u32[]{:S(2)}, u32[]{:S(2)}) %collective-permute-start.1) | collective-permute-done | bytes 131104 | tf_op jit(solution)/shard_map/ppermute | solution.py:296
  14.8 1.0 step.14
  15.9 5.7 %collective-permute-done.2.w_ref = bf16[16,32,128]{2,1,0:T(8,128)(2,1)S(1)} collective-permute-done((bf16[16,32,128]{2,1,0:T(8,128)(2,1)S(1)}, bf16[16,32,128]{2,1,0:T(8,128)(2,1)S(1)}, u32[]{:S(2)}, u32[]{:S(2)}) %collective-permute-start.2) | collective-permute-done | bytes 131104 | tf_op jit(solution)/shard_map/ppermute | solution.py:296
  21.6 1.0 step.15
  23.7 1.0 step.16
  24.7 2.0 %collective-permute-start.5 = (bf16[16,32,128]{2,1,0:T(8,128)(2,1)S(1)}, bf16[16,32,128]{2,1,0:T(8,128)(2,1)S(1)}, u32[]{:S(2)}, u32[]{:S(2)}) collective-permute-start(bf16[16,32,128]{2,1,0:T(8,128)(2,1)S(1)} %get-tuple-element.56), channel_id=1, source_target_pairs={{0,8},{1,9},{2,10},{3,11},{4,12},{5,13},{6,14},{7,15},{8,0},{9,1},... | collective-permute-start | bytes 393224 | tf_op jit(solution)/shard_map/ppermute | solution.py:296
  26.7 5.1 %collective-permute-done.4.w_ref = bf16[16,32,128]{2,1,0:T(8,128)(2,1)S(1)} collective-permute-done((bf16[16,32,128]{2,1,0:T(8,128)(2,1)S(1)}, bf16[16,32,128]{2,1,0:T(8,128)(2,1)S(1)}, u32[]{:S(2)}, u32[]{:S(2)}) %collective-permute-start.4) | collective-permute-done | bytes 131104 | tf_op jit(solution)/shard_map/ppermute | solution.py:296
  31.8 1.0 step.17
  32.8 3.1 %collective-permute-done.5.w_ref = bf16[16,32,128]{2,1,0:T(8,128)(2,1)S(1)} collective-permute-done((bf16[16,32,128]{2,1,0:T(8,128)(2,1)S(1)}, bf16[16,32,128]{2,1,0:T(8,128)(2,1)S(1)}, u32[]{:S(2)}, u32[]{:S(2)}) %collective-permute-start.5) | collective-permute-done | bytes 131104 | tf_op jit(solution)/shard_map/ppermute | solution.py:296
  36.0 1.0 step.18
  37.0 5.9 %collective-permute-done.6.w_ref = bf16[16,32,128]{2,1,0:T(8,128)(2,1)S(1)} collective-permute-done((bf16[16,32,128]{2,1,0:T(8,128)(2,1)S(1)}, bf16[16,32,128]{2,1,0:T(8,128)(2,1)S(1)}, u32[]{:S(2)}, u32[]{:S(2)}) %collective-permute-start.6) | collective-permute-done | bytes 131104 | tf_op jit(solution)/shard_map/ppermute | solution.py:296
  43.0 1.0 step.19
  44.0 4.5 %collective-permute-done.7.w_ref = bf16[16,32,128]{2,1,0:T(8,128)(2,1)S(1)} collective-permute-done((bf16[16,32,128]{2,1,0:T(8,128)(2,1)S(1)}, bf16[16,32,128]{2,1,0:T(8,128)(2,1)S(1)}, u32[]{:S(2)}, u32[]{:S(2)}) %collective-permute-start.7) | collective-permute-done | bytes 131104 | tf_op jit(solution)/shard_map/ppermute | solution.py:296
  49.7 4.5 %collective-permute-done.8.w_ref = bf16[16,32,128]{2,1,0:T(8,128)(2,1)S(1)} collective-permute-done((bf16[16,32,128]{2,1,0:T(8,128)(2,1)S(1)}, bf16[16,32,128]{2,1,0:T(8,128)(2,1)S(1)}, u32[]{:S(2)}, u32[]{:S(2)}) %collective-permute-start.8) | collective-permute-done | bytes 131104 | tf_op jit(solution)/shard_map/ppermute | solution.py:296
  54.2 1.0 step.21
  55.3 4.5 %collective-permute-done.9.w_ref = bf16[16,32,128]{2,1,0:T(8,128)(2,1)S(1)} collective-permute-done((bf16[16,32,128]{2,1,0:T(8,128)(2,1)S(1)}, bf16[16,32,128]{2,1,0:T(8,128)(2,1)S(1)}, u32[]{:S(2)}, u32[]{:S(2)}) %collective-permute-start.9) | collective-permute-done | bytes 131104 | tf_op jit(solution)/shard_map/ppermute | solution.py:296
  59.8 1.0 step.22
  60.9 4.5 %collective-permute-done.10.w_ref = bf16[16,32,128]{2,1,0:T(8,128)(2,1)S(1)} collective-permute-done((bf16[16,32,128]{2,1,0:T(8,128)(2,1)S(1)}, bf16[16,32,128]{2,1,0:T(8,128)(2,1)S(1)}, u32[]{:S(2)}, u32[]{:S(2)}) %collective-permute-start.10) | collective-permute-done | bytes 131104 | tf_op jit(solution)/shard_map/ppermute | solution.py:296
  65.4 1.2 %step.23 = (bf16[16,32,128]{2,1,0:T(8,128)(2,1)S(1)}, f32[8,16,128]{2,1,0:T(8,128)S(1)}) custom-call(s32[14,8,128]{2,1,0:T(8,128)S(1)} %get-tuple-element.43.code_ref, bf16[2,16,5,2,128,128]{5,4,3,2,1,0:T(8,128)(2,1)S(1)} %get-tuple-element.47.e_ref, bf16[16,32,128]{2,1,0:T(8,128)(2,1)S(1)} %collective-permute-done.10.w_ref), custom_call_target="tpu_custom_call" | custom-call | flops 167772160 | bytes 128 | tf_op jit(solution)/shard_map/step/pallas_call | solution.py:226
  66.7 4.4 %collective-permute-done.11.w_ref = bf16[16,32,128]{2,1,0:T(8,128)(2,1)S(1)} collective-permute-done((bf16[16,32,128]{2,1,0:T(8,128)(2,1)S(1)}, bf16[16,32,128]{2,1,0:T(8,128)(2,1)S(1)}, u32[]{:S(2)}, u32[]{:S(2)}) %collective-permute-start.11) | collective-permute-done | bytes 131104 | tf_op jit(solution)/shard_map/ppermute | solution.py:296
  71.1 1.0 step.24
  72.1 4.7 %collective-permute-done.12.w_ref = bf16[16,32,128]{2,1,0:T(8,128)(2,1)S(1)} collective-permute-done((bf16[16,32,128]{2,1,0:T(8,128)(2,1)S(1)}, bf16[16,32,128]{2,1,0:T(8,128)(2,1)S(1)}, u32[]{:S(2)}, u32[]{:S(2)}) %collective-permute-start.12) | collective-permute-done | bytes 131104 | tf_op jit(solution)/shard_map/ppermute | solution.py:296
  77.9 4.4 %collective-permute-done.13.w_ref = bf16[16,32,128]{2,1,0:T(8,128)(2,1)S(1)} collective-permute-done((bf16[16,32,128]{2,1,0:T(8,128)(2,1)S(1)}, bf16[16,32,128]{2,1,0:T(8,128)(2,1)S(1)}, u32[]{:S(2)}, u32[]{:S(2)}) %collective-permute-start.13) | collective-permute-done | bytes 131104 | tf_op jit(solution)/shard_map/ppermute | solution.py:296
  82.3 1.0 step.26
  83.3 3.2 %collective-permute-done.14.w_ref = bf16[16,32,128]{2,1,0:T(8,128)(2,1)S(1)} collective-permute-done((bf16[16,32,128]{2,1,0:T(8,128)(2,1)S(1)}, bf16[16,32,128]{2,1,0:T(8,128)(2,1)S(1)}, u32[]{:S(2)}, u32[]{:S(2)}) %collective-permute-start.14) | collective-permute-done | bytes 131104 | tf_op jit(solution)/shard_map/ppermute | solution.py:296
  87.8 1.3 %collective-permute-done.15.came_ref = bf16[4,8,16,128]{3,2,1,0:T(8,128)(2,1)S(1)} collective-permute-done((bf16[4,8,16,128]{3,2,1,0:T(8,128)(2,1)S(1)}, bf16[4,8,16,128]{3,2,1,0:T(8,128)(2,1)S(1)}, u32[]{:S(2)}, u32[]{:S(2)}) %collective-permute-start.15) | collective-permute-done | bytes 131104 | tf_op jit(solution)/shard_map/ppermute | solution.py:256
  89.2 5.5 %collective-permute-start.16 = (bf16[8,16,128]{2,1,0:T(8,128)(2,1)S(1)}, bf16[8,16,128]{2,1,0:T(8,128)(2,1)S(1)}, u32[]{:S(2)}, u32[]{:S(2)}) collective-permute-start(bf16[8,16,128]{2,1,0:T(8,128)(2,1)S(1)} %get-tuple-element.79), channel_id=1, source_target_pairs={{0,6},{1,7},{2,4},{3,5},{4,2},{5,3},{6,0},{7,1},{8,14},{9,15},{10,... | collective-permute-start | bytes 98312 | tf_op jit(solution)/shard_map/ppermute | solution.py:269
  96.5 2.0 %collective-permute-done.17 = bf16[8,16,128]{2,1,0:T(8,128)(2,1)S(1)} collective-permute-done((bf16[8,16,128]{2,1,0:T(8,128)(2,1)S(1)}, bf16[8,16,128]{2,1,0:T(8,128)(2,1)S(1)}, u32[]{:S(2)}, u32[]{:S(2)}) %collective-permute-start.17) | collective-permute-done | bytes 32800 | tf_op jit(solution)/shard_map/ppermute | solution.py:269
  (29 shorter events, 8.2 us)
Async XLA Ops:
  3.8 4.2 %collective-permute-start = (f32[1,16,128]{2,1,0:T(8,128)S(1)}, f32[1,16,128]{2,1,0:T(8,128)S(1)}, u32[]{:S(2)}, u32[]{:S(2)}) collective-permute-start(f32[1,16,128]{2,1,0:T(8,128)S(1)} %slice.3), channel_id=1, source_target_pairs={{0,1},{1,0},{2,3},{3,2},{4,5},{5,4},{6,7},{7,6},{8,9},{9,8},{10,11... | collective-permute-start | bytes 24584 | tf_op jit(solution)/shard_map/ppermute | solution.py:290
  4.3 10.6 %collective-permute-start.1 = (bf16[16,32,128]{2,1,0:T(8,128)(2,1)S(1)}, bf16[16,32,128]{2,1,0:T(8,128)(2,1)S(1)}, u32[]{:S(2)}, u32[]{:S(2)}) collective-permute-start(bf16[16,32,128]{2,1,0:T(8,128)(2,1)S(1)} %get-tuple-element.48), channel_id=1, source_target_pairs={{0,8},{1,9},{2,10},{3,11},{4,12},{5,13},{6,14},{7,15},{8,0},{9,1},... | collective-permute-start | bytes 393224 | tf_op jit(solution)/shard_map/ppermute | solution.py:296
  11.5 10.1 %collective-permute-start.2 = (bf16[16,32,128]{2,1,0:T(8,128)(2,1)S(1)}, bf16[16,32,128]{2,1,0:T(8,128)(2,1)S(1)}, u32[]{:S(2)}, u32[]{:S(2)}) collective-permute-start(bf16[16,32,128]{2,1,0:T(8,128)(2,1)S(1)} %get-tuple-element.50), channel_id=1, source_target_pairs={{0,8},{1,9},{2,10},{3,11},{4,12},{5,13},{6,14},{7,15},{8,0},{9,1},... | collective-permute-start | bytes 393224 | tf_op jit(solution)/shard_map/ppermute | solution.py:296
  15.8 7.8 %collective-permute-start.3 = (bf16[16,32,128]{2,1,0:T(8,128)(2,1)S(1)}, bf16[16,32,128]{2,1,0:T(8,128)(2,1)S(1)}, u32[]{:S(2)}, u32[]{:S(2)}) collective-permute-start(bf16[16,32,128]{2,1,0:T(8,128)(2,1)S(1)} %get-tuple-element.52), channel_id=1, source_target_pairs={{0,8},{1,9},{2,10},{3,11},{4,12},{5,13},{6,14},{7,15},{8,0},{9,1},... | collective-permute-start | bytes 393224 | tf_op jit(solution)/shard_map/ppermute | solution.py:296
  22.6 9.1 %collective-permute-start.4 = (bf16[16,32,128]{2,1,0:T(8,128)(2,1)S(1)}, bf16[16,32,128]{2,1,0:T(8,128)(2,1)S(1)}, u32[]{:S(2)}, u32[]{:S(2)}) collective-permute-start(bf16[16,32,128]{2,1,0:T(8,128)(2,1)S(1)} %get-tuple-element.54), channel_id=1, source_target_pairs={{0,8},{1,9},{2,10},{3,11},{4,12},{5,13},{6,14},{7,15},{8,0},{9,1},... | collective-permute-start | bytes 393224 | tf_op jit(solution)/shard_map/ppermute | solution.py:296
  24.7 11.3 %collective-permute-start.5 = (bf16[16,32,128]{2,1,0:T(8,128)(2,1)S(1)}, bf16[16,32,128]{2,1,0:T(8,128)(2,1)S(1)}, u32[]{:S(2)}, u32[]{:S(2)}) collective-permute-start(bf16[16,32,128]{2,1,0:T(8,128)(2,1)S(1)} %get-tuple-element.56), channel_id=1, source_target_pairs={{0,8},{1,9},{2,10},{3,11},{4,12},{5,13},{6,14},{7,15},{8,0},{9,1},... | collective-permute-start | bytes 393224 | tf_op jit(solution)/shard_map/ppermute | solution.py:296
  32.8 10.2 %collective-permute-start.6 = (bf16[16,32,128]{2,1,0:T(8,128)(2,1)S(1)}, bf16[16,32,128]{2,1,0:T(8,128)(2,1)S(1)}, u32[]{:S(2)}, u32[]{:S(2)}) collective-permute-start(bf16[16,32,128]{2,1,0:T(8,128)(2,1)S(1)} %get-tuple-element.58), channel_id=1, source_target_pairs={{0,8},{1,9},{2,10},{3,11},{4,12},{5,13},{6,14},{7,15},{8,0},{9,1},... | collective-permute-start | bytes 393224 | tf_op jit(solution)/shard_map/ppermute | solution.py:296
  37.0 11.6 %collective-permute-start.7 = (bf16[16,32,128]{2,1,0:T(8,128)(2,1)S(1)}, bf16[16,32,128]{2,1,0:T(8,128)(2,1)S(1)}, u32[]{:S(2)}, u32[]{:S(2)}) collective-permute-start(bf16[16,32,128]{2,1,0:T(8,128)(2,1)S(1)} %get-tuple-element.60), channel_id=1, source_target_pairs={{0,8},{1,9},{2,10},{3,11},{4,12},{5,13},{6,14},{7,15},{8,0},{9,1},... | collective-permute-start | bytes 393224 | tf_op jit(solution)/shard_map/ppermute | solution.py:296
  44.0 10.2 %collective-permute-start.8 = (bf16[16,32,128]{2,1,0:T(8,128)(2,1)S(1)}, bf16[16,32,128]{2,1,0:T(8,128)(2,1)S(1)}, u32[]{:S(2)}, u32[]{:S(2)}) collective-permute-start(bf16[16,32,128]{2,1,0:T(8,128)(2,1)S(1)} %get-tuple-element.62), channel_id=1, source_target_pairs={{0,8},{1,9},{2,10},{3,11},{4,12},{5,13},{6,14},{7,15},{8,0},{9,1},... | collective-permute-start | bytes 393224 | tf_op jit(solution)/shard_map/ppermute | solution.py:296
  49.6 10.2 %collective-permute-start.9 = (bf16[16,32,128]{2,1,0:T(8,128)(2,1)S(1)}, bf16[16,32,128]{2,1,0:T(8,128)(2,1)S(1)}, u32[]{:S(2)}, u32[]{:S(2)}) collective-permute-start(bf16[16,32,128]{2,1,0:T(8,128)(2,1)S(1)} %get-tuple-element.64), channel_id=1, source_target_pairs={{0,8},{1,9},{2,10},{3,11},{4,12},{5,13},{6,14},{7,15},{8,0},{9,1},... | collective-permute-start | bytes 393224 | tf_op jit(solution)/shard_map/ppermute | solution.py:296
  55.2 10.2 %collective-permute-start.10 = (bf16[16,32,128]{2,1,0:T(8,128)(2,1)S(1)}, bf16[16,32,128]{2,1,0:T(8,128)(2,1)S(1)}, u32[]{:S(2)}, u32[]{:S(2)}) collective-permute-start(bf16[16,32,128]{2,1,0:T(8,128)(2,1)S(1)} %get-tuple-element.66), channel_id=1, source_target_pairs={{0,8},{1,9},{2,10},{3,11},{4,12},{5,13},{6,14},{7,15},{8,0},{9,1},... | collective-permute-start | bytes 393224 | tf_op jit(solution)/shard_map/ppermute | solution.py:296
  60.8 10.2 %collective-permute-start.11 = (bf16[16,32,128]{2,1,0:T(8,128)(2,1)S(1)}, bf16[16,32,128]{2,1,0:T(8,128)(2,1)S(1)}, u32[]{:S(2)}, u32[]{:S(2)}) collective-permute-start(bf16[16,32,128]{2,1,0:T(8,128)(2,1)S(1)} %get-tuple-element.68), channel_id=1, source_target_pairs={{0,8},{1,9},{2,10},{3,11},{4,12},{5,13},{6,14},{7,15},{8,0},{9,1},... | collective-permute-start | bytes 393224 | tf_op jit(solution)/shard_map/ppermute | solution.py:296
  66.6 10.2 %collective-permute-start.12 = (bf16[16,32,128]{2,1,0:T(8,128)(2,1)S(1)}, bf16[16,32,128]{2,1,0:T(8,128)(2,1)S(1)}, u32[]{:S(2)}, u32[]{:S(2)}) collective-permute-start(bf16[16,32,128]{2,1,0:T(8,128)(2,1)S(1)} %get-tuple-element.70), channel_id=1, source_target_pairs={{0,8},{1,9},{2,10},{3,11},{4,12},{5,13},{6,14},{7,15},{8,0},{9,1},... | collective-permute-start | bytes 393224 | tf_op jit(solution)/shard_map/ppermute | solution.py:296
  72.0 10.3 %collective-permute-start.13 = (bf16[16,32,128]{2,1,0:T(8,128)(2,1)S(1)}, bf16[16,32,128]{2,1,0:T(8,128)(2,1)S(1)}, u32[]{:S(2)}, u32[]{:S(2)}) collective-permute-start(bf16[16,32,128]{2,1,0:T(8,128)(2,1)S(1)} %get-tuple-element.72), channel_id=1, source_target_pairs={{0,8},{1,9},{2,10},{3,11},{4,12},{5,13},{6,14},{7,15},{8,0},{9,1},... | collective-permute-start | bytes 393224 | tf_op jit(solution)/shard_map/ppermute | solution.py:296
  77.8 8.7 %collective-permute-start.14 = (bf16[16,32,128]{2,1,0:T(8,128)(2,1)S(1)}, bf16[16,32,128]{2,1,0:T(8,128)(2,1)S(1)}, u32[]{:S(2)}, u32[]{:S(2)}) collective-permute-start(bf16[16,32,128]{2,1,0:T(8,128)(2,1)S(1)} %get-tuple-element.74), channel_id=1, source_target_pairs={{0,8},{1,9},{2,10},{3,11},{4,12},{5,13},{6,14},{7,15},{8,0},{9,1},... | collective-permute-start | bytes 393224 | tf_op jit(solution)/shard_map/ppermute | solution.py:296
  87.7 1.4 %collective-permute-start.15 = (bf16[4,8,16,128]{3,2,1,0:T(8,128)(2,1)S(1)}, bf16[4,8,16,128]{3,2,1,0:T(8,128)(2,1)S(1)}, u32[]{:S(2)}, u32[]{:S(2)}) collective-permute-start(bf16[4,8,16,128]{3,2,1,0:T(8,128)(2,1)S(1)} %get-tuple-element.77), channel_id=1, source_target_pairs={{0,1},{1,0},{2,3},{3,2},{4,5},{5,4},{6,7},{7,6},{8,9},{9,8},{10,11... | collective-permute-start | bytes 393224 | tf_op jit(solution)/shard_map/ppermute | solution.py:256
  89.2 7.4 %collective-permute-start.16 = (bf16[8,16,128]{2,1,0:T(8,128)(2,1)S(1)}, bf16[8,16,128]{2,1,0:T(8,128)(2,1)S(1)}, u32[]{:S(2)}, u32[]{:S(2)}) collective-permute-start(bf16[8,16,128]{2,1,0:T(8,128)(2,1)S(1)} %get-tuple-element.79), channel_id=1, source_target_pairs={{0,6},{1,7},{2,4},{3,5},{4,2},{5,3},{6,0},{7,1},{8,14},{9,15},{10,... | collective-permute-start | bytes 98312 | tf_op jit(solution)/shard_map/ppermute | solution.py:269
  94.6 3.9 %collective-permute-start.17 = (bf16[8,16,128]{2,1,0:T(8,128)(2,1)S(1)}, bf16[8,16,128]{2,1,0:T(8,128)(2,1)S(1)}, u32[]{:S(2)}, u32[]{:S(2)}) collective-permute-start(bf16[8,16,128]{2,1,0:T(8,128)(2,1)S(1)} %get-tuple-element.80), channel_id=1, source_target_pairs={{0,4},{1,5},{2,6},{3,7},{4,0},{5,1},{6,2},{7,3},{8,12},{9,13},{10,... | collective-permute-start | bytes 98312 | tf_op jit(solution)/shard_map/ppermute | solution.py:269
  94.6 3.9 %collective-permute-start.18 = (bf16[8,16,128]{2,1,0:T(8,128)(2,1)S(1)}, bf16[8,16,128]{2,1,0:T(8,128)(2,1)S(1)}, u32[]{:S(2)}, u32[]{:S(2)}) collective-permute-start(bf16[8,16,128]{2,1,0:T(8,128)(2,1)S(1)} %get-tuple-element.81), channel_id=1, source_target_pairs={{0,2},{1,3},{2,0},{3,1},{4,6},{5,7},{6,4},{7,5},{8,10},{9,11},{10,... | collective-permute-start | bytes 98312 | tf_op jit(solution)/shard_map/ppermute | solution.py:269

commit v5 on v4

--- a/solution.py
+++ b/solution.py
@@ -16,11 +16,11 @@
 
 def advance_blocks(offs, rows, e_ref, pad_ref, adv_ref, img_ref, scale, blocks, band, slots):
     for b in blocks:
-        lhs = jnp.concatenate([pad_ref[b + offs[k]] for k in range(band)], axis=1)
-        er = e_ref[b, :, 0].reshape(band * BLOCK, BLOCK)
-        ei = e_ref[b, :, 1].reshape(band * BLOCK, BLOCK)
-        p = jnp.dot(lhs, er, preferred_element_type=jnp.float32)
-        q = jnp.dot(lhs, ei, preferred_element_type=jnp.float32)
+        both = 0.0
+        for k in range(band):
+            planes = jnp.concatenate([e_ref[b, k, 0], e_ref[b, k, 1]], axis=1)
+            both += jnp.dot(pad_ref[b + offs[k]], planes, preferred_element_type=jnp.float32)
+        p, q = both[:, :BLOCK], both[:, BLOCK:]
         p = [p[c * slots : (c + 1) * slots] for c in range(4)]
         q = [q[c * slots : (c + 1) * slots] for c in range(4)]
         new = jnp.concatenate([p[0] - q[1], q[0] + p[1], p[2] + q[3], p[3] - q[2]], axis=0)

time: 99.3 us -> 99.3 us (level)
  starting transfers between devices: 14.3 us -> 17.3 us
  Pallas kernels: 20.7 us -> 19.1 us
  waiting for transfers between devices: 61.8 us -> 60.3 us
    ppermute x3, starting transfers between devices: 6.12 us -> 9.19 us  [fold_owners(): lax.ppermute(others[mask - 1], 'depth', [(i, i ^ 2 * mask) for i in range...]
    ppermute x14, waiting for transfers between devices: 57.9 us -> 56.4 us  [on_device(): waves[f] = lax.ppermute(adv, 'depth', onward) if r + 1 < HANDOVERS else adv]
    pallas_call x14, Pallas kernels: 14 us -> 12.6 us  [run_step(): pl.pallas_call(functools.partial(step_kernel, scale, f), out_shape=(pltpu...]
  transfers between devices with their start and end apart: 19 -> 19, of which waited for: 17 -> 17; matrix products, arithmetic and copies ran while one was open for 1% -> 1% of each run, Pallas kernels for 17% -> 15%
where the time goes in v5:
time: 99.3 us; the launch traced here: 99.1 us
  waiting for transfers between devices  60.3 us (61%)
  Pallas kernels  19.1 us (19%)
  starting transfers between devices  17.3 us (17%)
  other arithmetic  1.44 us (1%)
    ppermute x14, waiting for transfers between devices, on_device(): waves[f] = lax.ppermute(adv, 'depth', onward) if r + 1 < HANDOVERS else adv  56.4 us
    pallas_call x14, Pallas kernels, run_step(): pl.pallas_call(functools.partial(step_kernel, scale, f), out_shape=(pltpu...  12.6 us
    ppermute x3, starting transfers between devices, fold_owners(): lax.ppermute(others[mask - 1], 'depth', [(i, i ^ 2 * mask) for i in range...  9.19 us
    ppermute x14, starting transfers between devices, on_device(): waves[f] = lax.ppermute(adv, 'depth', onward) if r + 1 < HANDOVERS else adv  7.51 us
    pallas_call x1, Pallas kernels, run_next(): pl.pallas_call(functools.partial(next_kernel, scale, f), out_shape=(pltpu...  3.45 us
    pallas_call x1, Pallas kernels, run_first(): pl.pallas_call(functools.partial(first_kernel, scale), out_shape=(pltpu.V...  2.92 us
    ppermute x3, waiting for transfers between devices, fold_owners(): lax.ppermute(others[mask - 1], 'depth', [(i, i ^ 2 * mask) for i in range...  2.55 us
  transfers between devices with their start and end apart: 19, of which 17 were waited for; matrix products, arithmetic and copies ran while one was open for 1% of the time, Pallas kernels for 15%

profile of v5, /device:TPU:0, one launch (start us, length us, event | category | flops | bytes accessed | tf_op | source)
XLA Modules:
  0.0 99.1 jit_solution(12177308981692860292)
XLA Ops:
  0.8 2.9 %first.1 = (bf16[16,32,128]{2,1,0:T(8,128)(2,1)S(1)}, f32[8,16,128]{2,1,0:T(8,128)S(1)}, s32[14,8,128]{2,1,0:T(8,128)S(1)}, bf16[2,16,5,2,128,128]{5,4,3,2,1,0:T(8,128)(2,1)S(1)}) custom-call(s32[2,8,128]{2,1,0:T(8,128)S(1)} %broadcast_in_dim.2.place_ref, s32[2,5]{1,0:T(2,128)} %offs_hbm.1, s32[2,8]{1,0:T(2,128)} %asgs_hbm.1, ...), custom_call_target="tpu_custom_call" | custom-call | flops 167772160 | bytes 128 | tf_op jit(solution)/shard_map/first/pallas_call | solution.py:172
  4.2 3.7 %collective-permute-start.1 = (bf16[16,32,128]{2,1,0:T(8,128)(2,1)S(1)}, bf16[16,32,128]{2,1,0:T(8,128)(2,1)S(1)}, u32[]{:S(2)}, u32[]{:S(2)}) collective-permute-start(bf16[16,32,128]{2,1,0:T(8,128)(2,1)S(1)} %get-tuple-element.48), channel_id=1, source_target_pairs={{0,8},{1,9},{2,10},{3,11},{4,12},{5,13},{6,14},{7,15},{8,0},{9,1},... | collective-permute-start | bytes 393224 | tf_op jit(solution)/shard_map/ppermute | solution.py:296
  7.9 3.4 %next.1 = (bf16[16,32,128]{2,1,0:T(8,128)(2,1)S(1)}, f32[8,16,128]{2,1,0:T(8,128)S(1)}, bf16[2,16,5,2,128,128]{5,4,3,2,1,0:T(8,128)(2,1)S(1)}) custom-call(s32[14,8,128]{2,1,0:T(8,128)S(1)} %get-tuple-element.43.code_ref, bf16[2,16,5,2,128,128]{5,4,3,2,1,0:T(8,128)(2,1)S(1)} %get-tuple-element.45.old, ...), custom_call_target="tpu_custom_call", output_to_operand_aliasing={{2}: (1, {})} | custom-call | flops 167772160 | bytes 128 | tf_op jit(solution)/shard_map/next/pallas_call | solution.py:201
  11.4 1.1 %collective-permute-start.2 = (bf16[16,32,128]{2,1,0:T(8,128)(2,1)S(1)}, bf16[16,32,128]{2,1,0:T(8,128)(2,1)S(1)}, u32[]{:S(2)}, u32[]{:S(2)}) collective-permute-start(bf16[16,32,128]{2,1,0:T(8,128)(2,1)S(1)} %get-tuple-element.50), channel_id=1, source_target_pairs={{0,8},{1,9},{2,10},{3,11},{4,12},{5,13},{6,14},{7,15},{8,0},{9,1},... | collective-permute-start | bytes 393224 | tf_op jit(solution)/shard_map/ppermute | solution.py:296
  12.5 2.3 %collective-permute-done.1.w_ref = bf16[16,32,128]{2,1,0:T(8,128)(2,1)S(1)} collective-permute-done((bf16[16,32,128]{2,1,0:T(8,128)(2,1)S(1)}, bf16[16,32,128]{2,1,0:T(8,128)(2,1)S(1)}, u32[]{:S(2)}, u32[]{:S(2)}) %collective-permute-start.1) | collective-permute-done | bytes 131104 | tf_op jit(solution)/shard_map/ppermute | solution.py:296
  14.8 0.9 step.14
  15.8 5.7 %collective-permute-done.2.w_ref = bf16[16,32,128]{2,1,0:T(8,128)(2,1)S(1)} collective-permute-done((bf16[16,32,128]{2,1,0:T(8,128)(2,1)S(1)}, bf16[16,32,128]{2,1,0:T(8,128)(2,1)S(1)}, u32[]{:S(2)}, u32[]{:S(2)}) %collective-permute-start.2) | collective-permute-done | bytes 131104 | tf_op jit(solution)/shard_map/ppermute | solution.py:296
  21.5 0.9 step.15
  22.5 1.1 %collective-permute-done.3.w_ref = bf16[16,32,128]{2,1,0:T(8,128)(2,1)S(1)} collective-permute-done((bf16[16,32,128]{2,1,0:T(8,128)(2,1)S(1)}, bf16[16,32,128]{2,1,0:T(8,128)(2,1)S(1)}, u32[]{:S(2)}, u32[]{:S(2)}) %collective-permute-start.3) | collective-permute-done | bytes 131104 | tf_op jit(solution)/shard_map/ppermute | solution.py:296
  23.5 0.9 step.16
  24.4 1.9 %collective-permute-start.5 = (bf16[16,32,128]{2,1,0:T(8,128)(2,1)S(1)}, bf16[16,32,128]{2,1,0:T(8,128)(2,1)S(1)}, u32[]{:S(2)}, u32[]{:S(2)}) collective-permute-start(bf16[16,32,128]{2,1,0:T(8,128)(2,1)S(1)} %get-tuple-element.56), channel_id=1, source_target_pairs={{0,8},{1,9},{2,10},{3,11},{4,12},{5,13},{6,14},{7,15},{8,0},{9,1},... | collective-permute-start | bytes 393224 | tf_op jit(solution)/shard_map/ppermute | solution.py:296
  26.3 5.1 %collective-permute-done.4.w_ref = bf16[16,32,128]{2,1,0:T(8,128)(2,1)S(1)} collective-permute-done((bf16[16,32,128]{2,1,0:T(8,128)(2,1)S(1)}, bf16[16,32,128]{2,1,0:T(8,128)(2,1)S(1)}, u32[]{:S(2)}, u32[]{:S(2)}) %collective-permute-start.4) | collective-permute-done | bytes 131104 | tf_op jit(solution)/shard_map/ppermute | solution.py:296
  31.5 0.9 step.17
  32.5 4.6 %collective-permute-done.5.w_ref = bf16[16,32,128]{2,1,0:T(8,128)(2,1)S(1)} collective-permute-done((bf16[16,32,128]{2,1,0:T(8,128)(2,1)S(1)}, bf16[16,32,128]{2,1,0:T(8,128)(2,1)S(1)}, u32[]{:S(2)}, u32[]{:S(2)}) %collective-permute-start.5) | collective-permute-done | bytes 131104 | tf_op jit(solution)/shard_map/ppermute | solution.py:296
  37.1 0.9 step.18
  38.1 4.6 %collective-permute-done.6.w_ref = bf16[16,32,128]{2,1,0:T(8,128)(2,1)S(1)} collective-permute-done((bf16[16,32,128]{2,1,0:T(8,128)(2,1)S(1)}, bf16[16,32,128]{2,1,0:T(8,128)(2,1)S(1)}, u32[]{:S(2)}, u32[]{:S(2)}) %collective-permute-start.6) | collective-permute-done | bytes 131104 | tf_op jit(solution)/shard_map/ppermute | solution.py:296
  42.7 0.9 step.19
  43.7 4.6 %collective-permute-done.7.w_ref = bf16[16,32,128]{2,1,0:T(8,128)(2,1)S(1)} collective-permute-done((bf16[16,32,128]{2,1,0:T(8,128)(2,1)S(1)}, bf16[16,32,128]{2,1,0:T(8,128)(2,1)S(1)}, u32[]{:S(2)}, u32[]{:S(2)}) %collective-permute-start.7) | collective-permute-done | bytes 131104 | tf_op jit(solution)/shard_map/ppermute | solution.py:296
  48.3 0.9 step.20
  49.3 4.6 %collective-permute-done.8.w_ref = bf16[16,32,128]{2,1,0:T(8,128)(2,1)S(1)} collective-permute-done((bf16[16,32,128]{2,1,0:T(8,128)(2,1)S(1)}, bf16[16,32,128]{2,1,0:T(8,128)(2,1)S(1)}, u32[]{:S(2)}, u32[]{:S(2)}) %collective-permute-start.8) | collective-permute-done | bytes 131104 | tf_op jit(solution)/shard_map/ppermute | solution.py:296
  54.0 0.9 step.21
  54.9 4.6 %collective-permute-done.9.w_ref = bf16[16,32,128]{2,1,0:T(8,128)(2,1)S(1)} collective-permute-done((bf16[16,32,128]{2,1,0:T(8,128)(2,1)S(1)}, bf16[16,32,128]{2,1,0:T(8,128)(2,1)S(1)}, u32[]{:S(2)}, u32[]{:S(2)}) %collective-permute-start.9) | collective-permute-done | bytes 131104 | tf_op jit(solution)/shard_map/ppermute | solution.py:296
  59.6 0.9 step.22
  60.6 4.6 %collective-permute-done.10.w_ref = bf16[16,32,128]{2,1,0:T(8,128)(2,1)S(1)} collective-permute-done((bf16[16,32,128]{2,1,0:T(8,128)(2,1)S(1)}, bf16[16,32,128]{2,1,0:T(8,128)(2,1)S(1)}, u32[]{:S(2)}, u32[]{:S(2)}) %collective-permute-start.10) | collective-permute-done | bytes 131104 | tf_op jit(solution)/shard_map/ppermute | solution.py:296
  66.2 4.6 %collective-permute-done.11.w_ref = bf16[16,32,128]{2,1,0:T(8,128)(2,1)S(1)} collective-permute-done((bf16[16,32,128]{2,1,0:T(8,128)(2,1)S(1)}, bf16[16,32,128]{2,1,0:T(8,128)(2,1)S(1)}, u32[]{:S(2)}, u32[]{:S(2)}) %collective-permute-start.11) | collective-permute-done | bytes 131104 | tf_op jit(solution)/shard_map/ppermute | solution.py:296
  70.8 0.9 step.24
  71.8 4.6 %collective-permute-done.12.w_ref = bf16[16,32,128]{2,1,0:T(8,128)(2,1)S(1)} collective-permute-done((bf16[16,32,128]{2,1,0:T(8,128)(2,1)S(1)}, bf16[16,32,128]{2,1,0:T(8,128)(2,1)S(1)}, u32[]{:S(2)}, u32[]{:S(2)}) %collective-permute-start.12) | collective-permute-done | bytes 131104 | tf_op jit(solution)/shard_map/ppermute | solution.py:296
  77.4 4.6 %collective-permute-done.13.w_ref = bf16[16,32,128]{2,1,0:T(8,128)(2,1)S(1)} collective-permute-done((bf16[16,32,128]{2,1,0:T(8,128)(2,1)S(1)}, bf16[16,32,128]{2,1,0:T(8,128)(2,1)S(1)}, u32[]{:S(2)}, u32[]{:S(2)}) %collective-permute-start.13) | collective-permute-done | bytes 131104 | tf_op jit(solution)/shard_map/ppermute | solution.py:296
  83.5 0.9 step.27
  84.6 1.3 %collective-permute-done.15.came_ref = bf16[4,8,16,128]{3,2,1,0:T(8,128)(2,1)S(1)} collective-permute-done((bf16[4,8,16,128]{3,2,1,0:T(8,128)(2,1)S(1)}, bf16[4,8,16,128]{3,2,1,0:T(8,128)(2,1)S(1)}, u32[]{:S(2)}, u32[]{:S(2)}) %collective-permute-start.15) | collective-permute-done | bytes 131104 | tf_op jit(solution)/shard_map/ppermute | solution.py:256
  86.0 8.5 %collective-permute-start.16 = (bf16[8,16,128]{2,1,0:T(8,128)(2,1)S(1)}, bf16[8,16,128]{2,1,0:T(8,128)(2,1)S(1)}, u32[]{:S(2)}, u32[]{:S(2)}) collective-permute-start(bf16[8,16,128]{2,1,0:T(8,128)(2,1)S(1)} %get-tuple-element.79), channel_id=1, source_target_pairs={{0,6},{1,7},{2,4},{3,5},{4,2},{5,3},{6,0},{7,1},{8,14},{9,15},{10,... | collective-permute-start | bytes 98312 | tf_op jit(solution)/shard_map/ppermute | solution.py:269
  96.5 2.0 %collective-permute-done.17 = bf16[8,16,128]{2,1,0:T(8,128)(2,1)S(1)} collective-permute-done((bf16[8,16,128]{2,1,0:T(8,128)(2,1)S(1)}, bf16[8,16,128]{2,1,0:T(8,128)(2,1)S(1)}, u32[]{:S(2)}, u32[]{:S(2)}) %collective-permute-start.17) | collective-permute-done | bytes 32800 | tf_op jit(solution)/shard_map/ppermute | solution.py:269
  (29 shorter events, 7.5 us)
Async XLA Ops:
  3.7 4.2 %collective-permute-start = (f32[1,16,128]{2,1,0:T(8,128)S(1)}, f32[1,16,128]{2,1,0:T(8,128)S(1)}, u32[]{:S(2)}, u32[]{:S(2)}) collective-permute-start(f32[1,16,128]{2,1,0:T(8,128)S(1)} %slice.3), channel_id=1, source_target_pairs={{0,1},{1,0},{2,3},{3,2},{4,5},{5,4},{6,7},{7,6},{8,9},{9,8},{10,11... | collective-permute-start | bytes 24584 | tf_op jit(solution)/shard_map/ppermute | solution.py:290
  4.2 10.6 %collective-permute-start.1 = (bf16[16,32,128]{2,1,0:T(8,128)(2,1)S(1)}, bf16[16,32,128]{2,1,0:T(8,128)(2,1)S(1)}, u32[]{:S(2)}, u32[]{:S(2)}) collective-permute-start(bf16[16,32,128]{2,1,0:T(8,128)(2,1)S(1)} %get-tuple-element.48), channel_id=1, source_target_pairs={{0,8},{1,9},{2,10},{3,11},{4,12},{5,13},{6,14},{7,15},{8,0},{9,1},... | collective-permute-start | bytes 393224 | tf_op jit(solution)/shard_map/ppermute | solution.py:296
  11.4 10.1 %collective-permute-start.2 = (bf16[16,32,128]{2,1,0:T(8,128)(2,1)S(1)}, bf16[16,32,128]{2,1,0:T(8,128)(2,1)S(1)}, u32[]{:S(2)}, u32[]{:S(2)}) collective-permute-start(bf16[16,32,128]{2,1,0:T(8,128)(2,1)S(1)} %get-tuple-element.50), channel_id=1, source_target_pairs={{0,8},{1,9},{2,10},{3,11},{4,12},{5,13},{6,14},{7,15},{8,0},{9,1},... | collective-permute-start | bytes 393224 | tf_op jit(solution)/shard_map/ppermute | solution.py:296
  15.7 7.8 %collective-permute-start.3 = (bf16[16,32,128]{2,1,0:T(8,128)(2,1)S(1)}, bf16[16,32,128]{2,1,0:T(8,128)(2,1)S(1)}, u32[]{:S(2)}, u32[]{:S(2)}) collective-permute-start(bf16[16,32,128]{2,1,0:T(8,128)(2,1)S(1)} %get-tuple-element.52), channel_id=1, source_target_pairs={{0,8},{1,9},{2,10},{3,11},{4,12},{5,13},{6,14},{7,15},{8,0},{9,1},... | collective-permute-start | bytes 393224 | tf_op jit(solution)/shard_map/ppermute | solution.py:296
  22.4 9.1 %collective-permute-start.4 = (bf16[16,32,128]{2,1,0:T(8,128)(2,1)S(1)}, bf16[16,32,128]{2,1,0:T(8,128)(2,1)S(1)}, u32[]{:S(2)}, u32[]{:S(2)}) collective-permute-start(bf16[16,32,128]{2,1,0:T(8,128)(2,1)S(1)} %get-tuple-element.54), channel_id=1, source_target_pairs={{0,8},{1,9},{2,10},{3,11},{4,12},{5,13},{6,14},{7,15},{8,0},{9,1},... | collective-permute-start | bytes 393224 | tf_op jit(solution)/shard_map/ppermute | solution.py:296
  24.4 12.7 %collective-permute-start.5 = (bf16[16,32,128]{2,1,0:T(8,128)(2,1)S(1)}, bf16[16,32,128]{2,1,0:T(8,128)(2,1)S(1)}, u32[]{:S(2)}, u32[]{:S(2)}) collective-permute-start(bf16[16,32,128]{2,1,0:T(8,128)(2,1)S(1)} %get-tuple-element.56), channel_id=1, source_target_pairs={{0,8},{1,9},{2,10},{3,11},{4,12},{5,13},{6,14},{7,15},{8,0},{9,1},... | collective-permute-start | bytes 393224 | tf_op jit(solution)/shard_map/ppermute | solution.py:296
  32.4 10.3 %collective-permute-start.6 = (bf16[16,32,128]{2,1,0:T(8,128)(2,1)S(1)}, bf16[16,32,128]{2,1,0:T(8,128)(2,1)S(1)}, u32[]{:S(2)}, u32[]{:S(2)}) collective-permute-start(bf16[16,32,128]{2,1,0:T(8,128)(2,1)S(1)} %get-tuple-element.58), channel_id=1, source_target_pairs={{0,8},{1,9},{2,10},{3,11},{4,12},{5,13},{6,14},{7,15},{8,0},{9,1},... | collective-permute-start | bytes 393224 | tf_op jit(solution)/shard_map/ppermute | solution.py:296
  38.0 10.3 %collective-permute-start.7 = (bf16[16,32,128]{2,1,0:T(8,128)(2,1)S(1)}, bf16[16,32,128]{2,1,0:T(8,128)(2,1)S(1)}, u32[]{:S(2)}, u32[]{:S(2)}) collective-permute-start(bf16[16,32,128]{2,1,0:T(8,128)(2,1)S(1)} %get-tuple-element.60), channel_id=1, source_target_pairs={{0,8},{1,9},{2,10},{3,11},{4,12},{5,13},{6,14},{7,15},{8,0},{9,1},... | collective-permute-start | bytes 393224 | tf_op jit(solution)/shard_map/ppermute | solution.py:296
  43.6 10.3 %collective-permute-start.8 = (bf16[16,32,128]{2,1,0:T(8,128)(2,1)S(1)}, bf16[16,32,128]{2,1,0:T(8,128)(2,1)S(1)}, u32[]{:S(2)}, u32[]{:S(2)}) collective-permute-start(bf16[16,32,128]{2,1,0:T(8,128)(2,1)S(1)} %get-tuple-element.62), channel_id=1, source_target_pairs={{0,8},{1,9},{2,10},{3,11},{4,12},{5,13},{6,14},{7,15},{8,0},{9,1},... | collective-permute-start | bytes 393224 | tf_op jit(solution)/shard_map/ppermute | solution.py:296
  49.2 10.3 %collective-permute-start.9 = (bf16[16,32,128]{2,1,0:T(8,128)(2,1)S(1)}, bf16[16,32,128]{2,1,0:T(8,128)(2,1)S(1)}, u32[]{:S(2)}, u32[]{:S(2)}) collective-permute-start(bf16[16,32,128]{2,1,0:T(8,128)(2,1)S(1)} %get-tuple-element.64), channel_id=1, source_target_pairs={{0,8},{1,9},{2,10},{3,11},{4,12},{5,13},{6,14},{7,15},{8,0},{9,1},... | collective-permute-start | bytes 393224 | tf_op jit(solution)/shard_map/ppermute | solution.py:296
  54.9 10.3 %collective-permute-start.10 = (bf16[16,32,128]{2,1,0:T(8,128)(2,1)S(1)}, bf16[16,32,128]{2,1,0:T(8,128)(2,1)S(1)}, u32[]{:S(2)}, u32[]{:S(2)}) collective-permute-start(bf16[16,32,128]{2,1,0:T(8,128)(2,1)S(1)} %get-tuple-element.66), channel_id=1, source_target_pairs={{0,8},{1,9},{2,10},{3,11},{4,12},{5,13},{6,14},{7,15},{8,0},{9,1},... | collective-permute-start | bytes 393224 | tf_op jit(solution)/shard_map/ppermute | solution.py:296
  60.5 10.3 %collective-permute-start.11 = (bf16[16,32,128]{2,1,0:T(8,128)(2,1)S(1)}, bf16[16,32,128]{2,1,0:T(8,128)(2,1)S(1)}, u32[]{:S(2)}, u32[]{:S(2)}) collective-permute-start(bf16[16,32,128]{2,1,0:T(8,128)(2,1)S(1)} %get-tuple-element.68), channel_id=1, source_target_pairs={{0,8},{1,9},{2,10},{3,11},{4,12},{5,13},{6,14},{7,15},{8,0},{9,1},... | collective-permute-start | bytes 393224 | tf_op jit(solution)/shard_map/ppermute | solution.py:296
  66.1 10.3 %collective-permute-start.12 = (bf16[16,32,128]{2,1,0:T(8,128)(2,1)S(1)}, bf16[16,32,128]{2,1,0:T(8,128)(2,1)S(1)}, u32[]{:S(2)}, u32[]{:S(2)}) collective-permute-start(bf16[16,32,128]{2,1,0:T(8,128)(2,1)S(1)} %get-tuple-element.70), channel_id=1, source_target_pairs={{0,8},{1,9},{2,10},{3,11},{4,12},{5,13},{6,14},{7,15},{8,0},{9,1},... | collective-permute-start | bytes 393224 | tf_op jit(solution)/shard_map/ppermute | solution.py:296
  71.7 10.3 %collective-permute-start.13 = (bf16[16,32,128]{2,1,0:T(8,128)(2,1)S(1)}, bf16[16,32,128]{2,1,0:T(8,128)(2,1)S(1)}, u32[]{:S(2)}, u32[]{:S(2)}) collective-permute-start(bf16[16,32,128]{2,1,0:T(8,128)(2,1)S(1)} %get-tuple-element.72), channel_id=1, source_target_pairs={{0,8},{1,9},{2,10},{3,11},{4,12},{5,13},{6,14},{7,15},{8,0},{9,1},... | collective-permute-start | bytes 393224 | tf_op jit(solution)/shard_map/ppermute | solution.py:296
  77.3 6.2 %collective-permute-start.14 = (bf16[16,32,128]{2,1,0:T(8,128)(2,1)S(1)}, bf16[16,32,128]{2,1,0:T(8,128)(2,1)S(1)}, u32[]{:S(2)}, u32[]{:S(2)}) collective-permute-start(bf16[16,32,128]{2,1,0:T(8,128)(2,1)S(1)} %get-tuple-element.74), channel_id=1, source_target_pairs={{0,8},{1,9},{2,10},{3,11},{4,12},{5,13},{6,14},{7,15},{8,0},{9,1},... | collective-permute-start | bytes 393224 | tf_op jit(solution)/shard_map/ppermute | solution.py:296
  84.5 1.4 %collective-permute-start.15 = (bf16[4,8,16,128]{3,2,1,0:T(8,128)(2,1)S(1)}, bf16[4,8,16,128]{3,2,1,0:T(8,128)(2,1)S(1)}, u32[]{:S(2)}, u32[]{:S(2)}) collective-permute-start(bf16[4,8,16,128]{3,2,1,0:T(8,128)(2,1)S(1)} %get-tuple-element.77), channel_id=1, source_target_pairs={{0,1},{1,0},{2,3},{3,2},{4,5},{5,4},{6,7},{7,6},{8,9},{9,8},{10,11... | collective-permute-start | bytes 393224 | tf_op jit(solution)/shard_map/ppermute | solution.py:256
  86.0 10.4 %collective-permute-start.16 = (bf16[8,16,128]{2,1,0:T(8,128)(2,1)S(1)}, bf16[8,16,128]{2,1,0:T(8,128)(2,1)S(1)}, u32[]{:S(2)}, u32[]{:S(2)}) collective-permute-start(bf16[8,16,128]{2,1,0:T(8,128)(2,1)S(1)} %get-tuple-element.79), channel_id=1, source_target_pairs={{0,6},{1,7},{2,4},{3,5},{4,2},{5,3},{6,0},{7,1},{8,14},{9,15},{10,... | collective-permute-start | bytes 98312 | tf_op jit(solution)/shard_map/ppermute | solution.py:269
  94.6 3.9 %collective-permute-start.17 = (bf16[8,16,128]{2,1,0:T(8,128)(2,1)S(1)}, bf16[8,16,128]{2,1,0:T(8,128)(2,1)S(1)}, u32[]{:S(2)}, u32[]{:S(2)}) collective-permute-start(bf16[8,16,128]{2,1,0:T(8,128)(2,1)S(1)} %get-tuple-element.80), channel_id=1, source_target_pairs={{0,4},{1,5},{2,6},{3,7},{4,0},{5,1},{6,2},{7,3},{8,12},{9,13},{10,... | collective-permute-start | bytes 98312 | tf_op jit(solution)/shard_map/ppermute | solution.py:269
  94.6 3.9 %collective-permute-start.18 = (bf16[8,16,128]{2,1,0:T(8,128)(2,1)S(1)}, bf16[8,16,128]{2,1,0:T(8,128)(2,1)S(1)}, u32[]{:S(2)}, u32[]{:S(2)}) collective-permute-start(bf16[8,16,128]{2,1,0:T(8,128)(2,1)S(1)} %get-tuple-element.81), channel_id=1, source_target_pairs={{0,2},{1,3},{2,0},{3,1},{4,6},{5,7},{6,4},{7,5},{8,10},{9,11},{10,... | collective-permute-start | bytes 98312 | tf_op jit(solution)/shard_map/ppermute | solution.py:269

commit v6 on v5

--- a/solution.py
+++ b/solution.py
@@ -16,10 +16,11 @@
 
 def advance_blocks(offs, rows, e_ref, pad_ref, adv_ref, img_ref, scale, blocks, band, slots):
     for b in blocks:
-        both = 0.0
+        both = None
         for k in range(band):
             planes = jnp.concatenate([e_ref[b, k, 0], e_ref[b, k, 1]], axis=1)
-            both += jnp.dot(pad_ref[b + offs[k]], planes, preferred_element_type=jnp.float32)
+            part = jnp.dot(pad_ref[b + offs[k]], planes, preferred_element_type=jnp.float32)
+            both = part if both is None else both + part
         p, q = both[:, :BLOCK], both[:, BLOCK:]
         p = [p[c * slots : (c + 1) * slots] for c in range(4)]
         q = [q[c * slots : (c + 1) * slots] for c in range(4)]
@@ -276,8 +277,8 @@
     size = lax.axis_size("depth")
     owners = size // sections
     index = lax.axis_index("depth")
-    place = jnp.stack([lax.div(index, owners), lax.rem(index, owners)]).astype(jnp.int32)
-    place = jnp.broadcast_to(place[:, None, None], (2, 8, BLOCK))
+    which = lax.broadcasted_iota(jnp.int32, (2, 8, BLOCK), 0)
+    place = jnp.where(which == 0, lax.div(index, owners), lax.rem(index, owners)).astype(jnp.int32)
     nfield, freqs, slots, points = fronts.shape
     nblk = extrap.shape[1]
     scale = 1.0 / math.sqrt(2.0 * owners * freqs)

time: 99.3 us -> 99.2 us (level)
  no operation moved by 1% of the time
where the time goes in v6:
time: 99.2 us; the launch traced here: 99.1 us
  waiting for transfers between devices  60.4 us (61%)
  Pallas kernels  19.1 us (19%)
  starting transfers between devices  17.3 us (17%)
  other arithmetic  1.37 us (1%)
    ppermute x14, waiting for transfers between devices, on_device(): waves[f] = lax.ppermute(adv, 'depth', onward) if r + 1 < HANDOVERS else adv  56.5 us
    pallas_call x14, Pallas kernels, run_step(): pl.pallas_call(functools.partial(step_kernel, scale, f), out_shape=(pltpu...  12.5 us
    ppermute x3, starting transfers between devices, fold_owners(): lax.ppermute(others[mask - 1], 'depth', [(i, i ^ 2 * mask) for i in range...  9.16 us
    ppermute x14, starting transfers between devices, on_device(): waves[f] = lax.ppermute(adv, 'depth', onward) if r + 1 < HANDOVERS else adv  7.51 us
    pallas_call x1, Pallas kernels, run_next(): pl.pallas_call(functools.partial(next_kernel, scale, f), out_shape=(pltpu...  3.46 us
    pallas_call x1, Pallas kernels, run_first(): pl.pallas_call(functools.partial(first_kernel, scale), out_shape=(pltpu.V...  2.93 us
    ppermute x3, waiting for transfers between devices, fold_owners(): lax.ppermute(others[mask - 1], 'depth', [(i, i ^ 2 * mask) for i in range...  2.55 us
  transfers between devices with their start and end apart: 19, of which 17 were waited for; matrix products, arithmetic and copies ran while one was open for 1% of the time, Pallas kernels for 15%

profile of v6, /device:TPU:0, one launch (start us, length us, event | category | flops | bytes accessed | tf_op | source)
XLA Modules:
  0.0 99.1 jit_solution(16722476743302421063)
XLA Ops:
  0.7 2.9 %first.1 = (bf16[16,32,128]{2,1,0:T(8,128)(2,1)S(1)}, f32[8,16,128]{2,1,0:T(8,128)S(1)}, s32[14,8,128]{2,1,0:T(8,128)S(1)}, bf16[2,16,5,2,128,128]{5,4,3,2,1,0:T(8,128)(2,1)S(1)}) custom-call(s32[2,8,128]{2,1,0:T(8,128)S(1)} %iota.7.place_ref, s32[2,5]{1,0:T(2,128)} %offs_hbm.1, s32[2,8]{1,0:T(2,128)} %asgs_hbm.1, bf16[2,16,5,2,128,128]{5,4,3,2,1,0:T(8,128)(2,1)} %e_hbm.3, ...), custom_call_target="tpu_custom_call" | custom-call | flops 167772160 | bytes 128 | tf_op jit(solution)/shard_map/first/pallas_call | solution.py:173
  4.2 3.7 %collective-permute-start.1 = (bf16[16,32,128]{2,1,0:T(8,128)(2,1)S(1)}, bf16[16,32,128]{2,1,0:T(8,128)(2,1)S(1)}, u32[]{:S(2)}, u32[]{:S(2)}) collective-permute-start(bf16[16,32,128]{2,1,0:T(8,128)(2,1)S(1)} %get-tuple-element.48), channel_id=1, source_target_pairs={{0,8},{1,9},{2,10},{3,11},{4,12},{5,13},{6,14},{7,15},{8,0},{9,1},... | collective-permute-start | bytes 393224 | tf_op jit(solution)/shard_map/ppermute | solution.py:297
  7.8 3.5 %next.1 = (bf16[16,32,128]{2,1,0:T(8,128)(2,1)S(1)}, f32[8,16,128]{2,1,0:T(8,128)S(1)}, bf16[2,16,5,2,128,128]{5,4,3,2,1,0:T(8,128)(2,1)S(1)}) custom-call(s32[14,8,128]{2,1,0:T(8,128)S(1)} %get-tuple-element.43.code_ref, bf16[2,16,5,2,128,128]{5,4,3,2,1,0:T(8,128)(2,1)S(1)} %get-tuple-element.45.old, ...), custom_call_target="tpu_custom_call", output_to_operand_aliasing={{2}: (1, {})} | custom-call | flops 167772160 | bytes 128 | tf_op jit(solution)/shard_map/next/pallas_call | solution.py:202
  11.3 1.2 %collective-permute-start.2 = (bf16[16,32,128]{2,1,0:T(8,128)(2,1)S(1)}, bf16[16,32,128]{2,1,0:T(8,128)(2,1)S(1)}, u32[]{:S(2)}, u32[]{:S(2)}) collective-permute-start(bf16[16,32,128]{2,1,0:T(8,128)(2,1)S(1)} %get-tuple-element.50), channel_id=1, source_target_pairs={{0,8},{1,9},{2,10},{3,11},{4,12},{5,13},{6,14},{7,15},{8,0},{9,1},... | collective-permute-start | bytes 393224 | tf_op jit(solution)/shard_map/ppermute | solution.py:297
  12.5 2.3 %collective-permute-done.1.w_ref = bf16[16,32,128]{2,1,0:T(8,128)(2,1)S(1)} collective-permute-done((bf16[16,32,128]{2,1,0:T(8,128)(2,1)S(1)}, bf16[16,32,128]{2,1,0:T(8,128)(2,1)S(1)}, u32[]{:S(2)}, u32[]{:S(2)}) %collective-permute-start.1) | collective-permute-done | bytes 131104 | tf_op jit(solution)/shard_map/ppermute | solution.py:297
  14.7 0.9 step.14
  15.7 5.7 %collective-permute-done.2.w_ref = bf16[16,32,128]{2,1,0:T(8,128)(2,1)S(1)} collective-permute-done((bf16[16,32,128]{2,1,0:T(8,128)(2,1)S(1)}, bf16[16,32,128]{2,1,0:T(8,128)(2,1)S(1)}, u32[]{:S(2)}, u32[]{:S(2)}) %collective-permute-start.2) | collective-permute-done | bytes 131104 | tf_op jit(solution)/shard_map/ppermute | solution.py:297
  21.4 0.9 step.15
  22.4 1.1 %collective-permute-done.3.w_ref = bf16[16,32,128]{2,1,0:T(8,128)(2,1)S(1)} collective-permute-done((bf16[16,32,128]{2,1,0:T(8,128)(2,1)S(1)}, bf16[16,32,128]{2,1,0:T(8,128)(2,1)S(1)}, u32[]{:S(2)}, u32[]{:S(2)}) %collective-permute-start.3) | collective-permute-done | bytes 131104 | tf_op jit(solution)/shard_map/ppermute | solution.py:297
  23.5 0.9 step.16
  24.4 1.9 %collective-permute-start.5 = (bf16[16,32,128]{2,1,0:T(8,128)(2,1)S(1)}, bf16[16,32,128]{2,1,0:T(8,128)(2,1)S(1)}, u32[]{:S(2)}, u32[]{:S(2)}) collective-permute-start(bf16[16,32,128]{2,1,0:T(8,128)(2,1)S(1)} %get-tuple-element.56), channel_id=1, source_target_pairs={{0,8},{1,9},{2,10},{3,11},{4,12},{5,13},{6,14},{7,15},{8,0},{9,1},... | collective-permute-start | bytes 393224 | tf_op jit(solution)/shard_map/ppermute | solution.py:297
  26.3 5.2 %collective-permute-done.4.w_ref = bf16[16,32,128]{2,1,0:T(8,128)(2,1)S(1)} collective-permute-done((bf16[16,32,128]{2,1,0:T(8,128)(2,1)S(1)}, bf16[16,32,128]{2,1,0:T(8,128)(2,1)S(1)}, u32[]{:S(2)}, u32[]{:S(2)}) %collective-permute-start.4) | collective-permute-done | bytes 131104 | tf_op jit(solution)/shard_map/ppermute | solution.py:297
  31.5 0.9 step.17
  32.4 4.6 %collective-permute-done.5.w_ref = bf16[16,32,128]{2,1,0:T(8,128)(2,1)S(1)} collective-permute-done((bf16[16,32,128]{2,1,0:T(8,128)(2,1)S(1)}, bf16[16,32,128]{2,1,0:T(8,128)(2,1)S(1)}, u32[]{:S(2)}, u32[]{:S(2)}) %collective-permute-start.5) | collective-permute-done | bytes 131104 | tf_op jit(solution)/shard_map/ppermute | solution.py:297
  38.1 4.6 %collective-permute-done.6.w_ref = bf16[16,32,128]{2,1,0:T(8,128)(2,1)S(1)} collective-permute-done((bf16[16,32,128]{2,1,0:T(8,128)(2,1)S(1)}, bf16[16,32,128]{2,1,0:T(8,128)(2,1)S(1)}, u32[]{:S(2)}, u32[]{:S(2)}) %collective-permute-start.6) | collective-permute-done | bytes 131104 | tf_op jit(solution)/shard_map/ppermute | solution.py:297
  42.7 0.9 step.19
  43.7 4.6 %collective-permute-done.7.w_ref = bf16[16,32,128]{2,1,0:T(8,128)(2,1)S(1)} collective-permute-done((bf16[16,32,128]{2,1,0:T(8,128)(2,1)S(1)}, bf16[16,32,128]{2,1,0:T(8,128)(2,1)S(1)}, u32[]{:S(2)}, u32[]{:S(2)}) %collective-permute-start.7) | collective-permute-done | bytes 131104 | tf_op jit(solution)/shard_map/ppermute | solution.py:297
  49.3 4.6 %collective-permute-done.8.w_ref = bf16[16,32,128]{2,1,0:T(8,128)(2,1)S(1)} collective-permute-done((bf16[16,32,128]{2,1,0:T(8,128)(2,1)S(1)}, bf16[16,32,128]{2,1,0:T(8,128)(2,1)S(1)}, u32[]{:S(2)}, u32[]{:S(2)}) %collective-permute-start.8) | collective-permute-done | bytes 131104 | tf_op jit(solution)/shard_map/ppermute | solution.py:297
  53.9 0.9 step.21
  54.9 4.6 %collective-permute-done.9.w_ref = bf16[16,32,128]{2,1,0:T(8,128)(2,1)S(1)} collective-permute-done((bf16[16,32,128]{2,1,0:T(8,128)(2,1)S(1)}, bf16[16,32,128]{2,1,0:T(8,128)(2,1)S(1)}, u32[]{:S(2)}, u32[]{:S(2)}) %collective-permute-start.9) | collective-permute-done | bytes 131104 | tf_op jit(solution)/shard_map/ppermute | solution.py:297
  60.5 4.6 %collective-permute-done.10.w_ref = bf16[16,32,128]{2,1,0:T(8,128)(2,1)S(1)} collective-permute-done((bf16[16,32,128]{2,1,0:T(8,128)(2,1)S(1)}, bf16[16,32,128]{2,1,0:T(8,128)(2,1)S(1)}, u32[]{:S(2)}, u32[]{:S(2)}) %collective-permute-start.10) | collective-permute-done | bytes 131104 | tf_op jit(solution)/shard_map/ppermute | solution.py:297
  65.2 0.9 step.23
  66.2 4.6 %collective-permute-done.11.w_ref = bf16[16,32,128]{2,1,0:T(8,128)(2,1)S(1)} collective-permute-done((bf16[16,32,128]{2,1,0:T(8,128)(2,1)S(1)}, bf16[16,32,128]{2,1,0:T(8,128)(2,1)S(1)}, u32[]{:S(2)}, u32[]{:S(2)}) %collective-permute-start.11) | collective-permute-done | bytes 131104 | tf_op jit(solution)/shard_map/ppermute | solution.py:297
  70.8 0.9 step.24
  71.8 4.6 %collective-permute-done.12.w_ref = bf16[16,32,128]{2,1,0:T(8,128)(2,1)S(1)} collective-permute-done((bf16[16,32,128]{2,1,0:T(8,128)(2,1)S(1)}, bf16[16,32,128]{2,1,0:T(8,128)(2,1)S(1)}, u32[]{:S(2)}, u32[]{:S(2)}) %collective-permute-start.12) | collective-permute-done | bytes 131104 | tf_op jit(solution)/shard_map/ppermute | solution.py:297
  76.4 0.9 step.25
  77.4 4.6 %collective-permute-done.13.w_ref = bf16[16,32,128]{2,1,0:T(8,128)(2,1)S(1)} collective-permute-done((bf16[16,32,128]{2,1,0:T(8,128)(2,1)S(1)}, bf16[16,32,128]{2,1,0:T(8,128)(2,1)S(1)}, u32[]{:S(2)}, u32[]{:S(2)}) %collective-permute-start.13) | collective-permute-done | bytes 131104 | tf_op jit(solution)/shard_map/ppermute | solution.py:297
  82.0 0.9 step.26
  83.5 0.9 step.27
  84.6 1.3 %collective-permute-done.15.came_ref = bf16[4,8,16,128]{3,2,1,0:T(8,128)(2,1)S(1)} collective-permute-done((bf16[4,8,16,128]{3,2,1,0:T(8,128)(2,1)S(1)}, bf16[4,8,16,128]{3,2,1,0:T(8,128)(2,1)S(1)}, u32[]{:S(2)}, u32[]{:S(2)}) %collective-permute-start.15) | collective-permute-done | bytes 131104 | tf_op jit(solution)/shard_map/ppermute | solution.py:257
  86.0 8.5 %collective-permute-start.16 = (bf16[8,16,128]{2,1,0:T(8,128)(2,1)S(1)}, bf16[8,16,128]{2,1,0:T(8,128)(2,1)S(1)}, u32[]{:S(2)}, u32[]{:S(2)}) collective-permute-start(bf16[8,16,128]{2,1,0:T(8,128)(2,1)S(1)} %get-tuple-element.79), channel_id=1, source_target_pairs={{0,6},{1,7},{2,4},{3,5},{4,2},{5,3},{6,0},{7,1},{8,14},{9,15},{10,... | collective-permute-start | bytes 98312 | tf_op jit(solution)/shard_map/ppermute | solution.py:270
  96.4 2.0 %collective-permute-done.17 = bf16[8,16,128]{2,1,0:T(8,128)(2,1)S(1)} collective-permute-done((bf16[8,16,128]{2,1,0:T(8,128)(2,1)S(1)}, bf16[8,16,128]{2,1,0:T(8,128)(2,1)S(1)}, u32[]{:S(2)}, u32[]{:S(2)}) %collective-permute-start.17) | collective-permute-done | bytes 32800 | tf_op jit(solution)/shard_map/ppermute | solution.py:270
  (29 shorter events, 7.4 us)
Async XLA Ops:
  3.7 4.2 %collective-permute-start = (f32[1,16,128]{2,1,0:T(8,128)S(1)}, f32[1,16,128]{2,1,0:T(8,128)S(1)}, u32[]{:S(2)}, u32[]{:S(2)}) collective-permute-start(f32[1,16,128]{2,1,0:T(8,128)S(1)} %slice.3), channel_id=1, source_target_pairs={{0,1},{1,0},{2,3},{3,2},{4,5},{5,4},{6,7},{7,6},{8,9},{9,8},{10,11... | collective-permute-start | bytes 24584 | tf_op jit(solution)/shard_map/ppermute | solution.py:291
  4.2 10.6 %collective-permute-start.1 = (bf16[16,32,128]{2,1,0:T(8,128)(2,1)S(1)}, bf16[16,32,128]{2,1,0:T(8,128)(2,1)S(1)}, u32[]{:S(2)}, u32[]{:S(2)}) collective-permute-start(bf16[16,32,128]{2,1,0:T(8,128)(2,1)S(1)} %get-tuple-element.48), channel_id=1, source_target_pairs={{0,8},{1,9},{2,10},{3,11},{4,12},{5,13},{6,14},{7,15},{8,0},{9,1},... | collective-permute-start | bytes 393224 | tf_op jit(solution)/shard_map/ppermute | solution.py:297
  11.3 10.1 %collective-permute-start.2 = (bf16[16,32,128]{2,1,0:T(8,128)(2,1)S(1)}, bf16[16,32,128]{2,1,0:T(8,128)(2,1)S(1)}, u32[]{:S(2)}, u32[]{:S(2)}) collective-permute-start(bf16[16,32,128]{2,1,0:T(8,128)(2,1)S(1)} %get-tuple-element.50), channel_id=1, source_target_pairs={{0,8},{1,9},{2,10},{3,11},{4,12},{5,13},{6,14},{7,15},{8,0},{9,1},... | collective-permute-start | bytes 393224 | tf_op jit(solution)/shard_map/ppermute | solution.py:297
  15.6 7.8 %collective-permute-start.3 = (bf16[16,32,128]{2,1,0:T(8,128)(2,1)S(1)}, bf16[16,32,128]{2,1,0:T(8,128)(2,1)S(1)}, u32[]{:S(2)}, u32[]{:S(2)}) collective-permute-start(bf16[16,32,128]{2,1,0:T(8,128)(2,1)S(1)} %get-tuple-element.52), channel_id=1, source_target_pairs={{0,8},{1,9},{2,10},{3,11},{4,12},{5,13},{6,14},{7,15},{8,0},{9,1},... | collective-permute-start | bytes 393224 | tf_op jit(solution)/shard_map/ppermute | solution.py:297
  22.3 9.1 %collective-permute-start.4 = (bf16[16,32,128]{2,1,0:T(8,128)(2,1)S(1)}, bf16[16,32,128]{2,1,0:T(8,128)(2,1)S(1)}, u32[]{:S(2)}, u32[]{:S(2)}) collective-permute-start(bf16[16,32,128]{2,1,0:T(8,128)(2,1)S(1)} %get-tuple-element.54), channel_id=1, source_target_pairs={{0,8},{1,9},{2,10},{3,11},{4,12},{5,13},{6,14},{7,15},{8,0},{9,1},... | collective-permute-start | bytes 393224 | tf_op jit(solution)/shard_map/ppermute | solution.py:297
  24.4 12.7 %collective-permute-start.5 = (bf16[16,32,128]{2,1,0:T(8,128)(2,1)S(1)}, bf16[16,32,128]{2,1,0:T(8,128)(2,1)S(1)}, u32[]{:S(2)}, u32[]{:S(2)}) collective-permute-start(bf16[16,32,128]{2,1,0:T(8,128)(2,1)S(1)} %get-tuple-element.56), channel_id=1, source_target_pairs={{0,8},{1,9},{2,10},{3,11},{4,12},{5,13},{6,14},{7,15},{8,0},{9,1},... | collective-permute-start | bytes 393224 | tf_op jit(solution)/shard_map/ppermute | solution.py:297
  32.4 10.3 %collective-permute-start.6 = (bf16[16,32,128]{2,1,0:T(8,128)(2,1)S(1)}, bf16[16,32,128]{2,1,0:T(8,128)(2,1)S(1)}, u32[]{:S(2)}, u32[]{:S(2)}) collective-permute-start(bf16[16,32,128]{2,1,0:T(8,128)(2,1)S(1)} %get-tuple-element.58), channel_id=1, source_target_pairs={{0,8},{1,9},{2,10},{3,11},{4,12},{5,13},{6,14},{7,15},{8,0},{9,1},... | collective-permute-start | bytes 393224 | tf_op jit(solution)/shard_map/ppermute | solution.py:297
  38.0 10.3 %collective-permute-start.7 = (bf16[16,32,128]{2,1,0:T(8,128)(2,1)S(1)}, bf16[16,32,128]{2,1,0:T(8,128)(2,1)S(1)}, u32[]{:S(2)}, u32[]{:S(2)}) collective-permute-start(bf16[16,32,128]{2,1,0:T(8,128)(2,1)S(1)} %get-tuple-element.60), channel_id=1, source_target_pairs={{0,8},{1,9},{2,10},{3,11},{4,12},{5,13},{6,14},{7,15},{8,0},{9,1},... | collective-permute-start | bytes 393224 | tf_op jit(solution)/shard_map/ppermute | solution.py:297
  43.6 10.3 %collective-permute-start.8 = (bf16[16,32,128]{2,1,0:T(8,128)(2,1)S(1)}, bf16[16,32,128]{2,1,0:T(8,128)(2,1)S(1)}, u32[]{:S(2)}, u32[]{:S(2)}) collective-permute-start(bf16[16,32,128]{2,1,0:T(8,128)(2,1)S(1)} %get-tuple-element.62), channel_id=1, source_target_pairs={{0,8},{1,9},{2,10},{3,11},{4,12},{5,13},{6,14},{7,15},{8,0},{9,1},... | collective-permute-start | bytes 393224 | tf_op jit(solution)/shard_map/ppermute | solution.py:297
  49.2 10.3 %collective-permute-start.9 = (bf16[16,32,128]{2,1,0:T(8,128)(2,1)S(1)}, bf16[16,32,128]{2,1,0:T(8,128)(2,1)S(1)}, u32[]{:S(2)}, u32[]{:S(2)}) collective-permute-start(bf16[16,32,128]{2,1,0:T(8,128)(2,1)S(1)} %get-tuple-element.64), channel_id=1, source_target_pairs={{0,8},{1,9},{2,10},{3,11},{4,12},{5,13},{6,14},{7,15},{8,0},{9,1},... | collective-permute-start | bytes 393224 | tf_op jit(solution)/shard_map/ppermute | solution.py:297
  54.8 10.3 %collective-permute-start.10 = (bf16[16,32,128]{2,1,0:T(8,128)(2,1)S(1)}, bf16[16,32,128]{2,1,0:T(8,128)(2,1)S(1)}, u32[]{:S(2)}, u32[]{:S(2)}) collective-permute-start(bf16[16,32,128]{2,1,0:T(8,128)(2,1)S(1)} %get-tuple-element.66), channel_id=1, source_target_pairs={{0,8},{1,9},{2,10},{3,11},{4,12},{5,13},{6,14},{7,15},{8,0},{9,1},... | collective-permute-start | bytes 393224 | tf_op jit(solution)/shard_map/ppermute | solution.py:297
  60.5 10.3 %collective-permute-start.11 = (bf16[16,32,128]{2,1,0:T(8,128)(2,1)S(1)}, bf16[16,32,128]{2,1,0:T(8,128)(2,1)S(1)}, u32[]{:S(2)}, u32[]{:S(2)}) collective-permute-start(bf16[16,32,128]{2,1,0:T(8,128)(2,1)S(1)} %get-tuple-element.68), channel_id=1, source_target_pairs={{0,8},{1,9},{2,10},{3,11},{4,12},{5,13},{6,14},{7,15},{8,0},{9,1},... | collective-permute-start | bytes 393224 | tf_op jit(solution)/shard_map/ppermute | solution.py:297
  66.1 10.3 %collective-permute-start.12 = (bf16[16,32,128]{2,1,0:T(8,128)(2,1)S(1)}, bf16[16,32,128]{2,1,0:T(8,128)(2,1)S(1)}, u32[]{:S(2)}, u32[]{:S(2)}) collective-permute-start(bf16[16,32,128]{2,1,0:T(8,128)(2,1)S(1)} %get-tuple-element.70), channel_id=1, source_target_pairs={{0,8},{1,9},{2,10},{3,11},{4,12},{5,13},{6,14},{7,15},{8,0},{9,1},... | collective-permute-start | bytes 393224 | tf_op jit(solution)/shard_map/ppermute | solution.py:297
  71.7 10.3 %collective-permute-start.13 = (bf16[16,32,128]{2,1,0:T(8,128)(2,1)S(1)}, bf16[16,32,128]{2,1,0:T(8,128)(2,1)S(1)}, u32[]{:S(2)}, u32[]{:S(2)}) collective-permute-start(bf16[16,32,128]{2,1,0:T(8,128)(2,1)S(1)} %get-tuple-element.72), channel_id=1, source_target_pairs={{0,8},{1,9},{2,10},{3,11},{4,12},{5,13},{6,14},{7,15},{8,0},{9,1},... | collective-permute-start | bytes 393224 | tf_op jit(solution)/shard_map/ppermute | solution.py:297
  77.3 6.2 %collective-permute-start.14 = (bf16[16,32,128]{2,1,0:T(8,128)(2,1)S(1)}, bf16[16,32,128]{2,1,0:T(8,128)(2,1)S(1)}, u32[]{:S(2)}, u32[]{:S(2)}) collective-permute-start(bf16[16,32,128]{2,1,0:T(8,128)(2,1)S(1)} %get-tuple-element.74), channel_id=1, source_target_pairs={{0,8},{1,9},{2,10},{3,11},{4,12},{5,13},{6,14},{7,15},{8,0},{9,1},... | collective-permute-start | bytes 393224 | tf_op jit(solution)/shard_map/ppermute | solution.py:297
  84.5 1.4 %collective-permute-start.15 = (bf16[4,8,16,128]{3,2,1,0:T(8,128)(2,1)S(1)}, bf16[4,8,16,128]{3,2,1,0:T(8,128)(2,1)S(1)}, u32[]{:S(2)}, u32[]{:S(2)}) collective-permute-start(bf16[4,8,16,128]{3,2,1,0:T(8,128)(2,1)S(1)} %get-tuple-element.77), channel_id=1, source_target_pairs={{0,1},{1,0},{2,3},{3,2},{4,5},{5,4},{6,7},{7,6},{8,9},{9,8},{10,11... | collective-permute-start | bytes 393224 | tf_op jit(solution)/shard_map/ppermute | solution.py:257
  86.0 10.4 %collective-permute-start.16 = (bf16[8,16,128]{2,1,0:T(8,128)(2,1)S(1)}, bf16[8,16,128]{2,1,0:T(8,128)(2,1)S(1)}, u32[]{:S(2)}, u32[]{:S(2)}) collective-permute-start(bf16[8,16,128]{2,1,0:T(8,128)(2,1)S(1)} %get-tuple-element.79), channel_id=1, source_target_pairs={{0,6},{1,7},{2,4},{3,5},{4,2},{5,3},{6,0},{7,1},{8,14},{9,15},{10,... | collective-permute-start | bytes 98312 | tf_op jit(solution)/shard_map/ppermute | solution.py:270
  94.5 3.9 %collective-permute-start.17 = (bf16[8,16,128]{2,1,0:T(8,128)(2,1)S(1)}, bf16[8,16,128]{2,1,0:T(8,128)(2,1)S(1)}, u32[]{:S(2)}, u32[]{:S(2)}) collective-permute-start(bf16[8,16,128]{2,1,0:T(8,128)(2,1)S(1)} %get-tuple-element.80), channel_id=1, source_target_pairs={{0,4},{1,5},{2,6},{3,7},{4,0},{5,1},{6,2},{7,3},{8,12},{9,13},{10,... | collective-permute-start | bytes 98312 | tf_op jit(solution)/shard_map/ppermute | solution.py:270
  94.5 3.9 %collective-permute-start.18 = (bf16[8,16,128]{2,1,0:T(8,128)(2,1)S(1)}, bf16[8,16,128]{2,1,0:T(8,128)(2,1)S(1)}, u32[]{:S(2)}, u32[]{:S(2)}) collective-permute-start(bf16[8,16,128]{2,1,0:T(8,128)(2,1)S(1)} %get-tuple-element.81), channel_id=1, source_target_pairs={{0,2},{1,3},{2,0},{3,1},{4,6},{5,7},{6,4},{7,5},{8,10},{9,11},{10,... | collective-permute-start | bytes 98312 | tf_op jit(solution)/shard_map/ppermute | solution.py:270
